TPU v7x, 32 devices: a whole 2x2x4 slice. The times are simulated.
32 devices in a mesh: wide: 8 (over z, y), narrow: 4 (over x, core).
Axes of the slice: x: 2, y: 2, z: 4, core: 2. Of those that a mesh axis runs over, the one named last changes fastest.
Arguments:
- hidden: bfloat16 [32768, 768], P(('wide', 'narrow')), may hold values from -6 to 6
- segment: int32 [64, 512], P(('wide', 'narrow')), may hold values from 0 to 3, never falling along the last dimension, each value on 1 to 256 neighbouring positions
- w_qkv: bfloat16 [768, 2304], P('wide', 'narrow'), may hold values from -0.21875 to 0.21875
- w_out: bfloat16 [768, 768], P('wide', 'narrow'), may hold values from -0.875 to 0.875
- w_in: bfloat16 [768, 3072], P('wide', 'narrow'), may hold values from -0.21875 to 0.21875
- w_back: bfloat16 [3072, 768], P('wide', 'narrow'), may hold values from -0.109375 to 0.109375
- vectors: float32 [9216], P(('wide', 'narrow')), may hold values from -0.5 to 1.4, as said below
- cotangent: bfloat16 [32768, 768], P(('wide', 'narrow')), may hold values from -6 to 6
Outputs:
- output: bfloat16 [32768, 768], P(('wide', 'narrow'))
- grad_hidden: float32 [32768, 768], P(('wide', 'narrow'))
- grad_w_qkv: float32 [768, 2304], P('wide', 'narrow')
- grad_w_out: float32 [768, 768], P('wide', 'narrow')
- grad_w_in: float32 [768, 3072], P('wide', 'narrow')
- grad_w_back: float32 [3072, 768], P('wide', 'narrow')
- grad_vectors: float32 [9216], P(('wide', 'narrow'))
Inputs may be any that keep to these rules, and one draw needn't show every extreme that they name: segment numbers never fall along a packed row; each document covers 1 to 256 tokens. `vectors`: the gains lie from 0.6 to 1.4, the biases and shifts from -0.5 to 0.5.
All inputs are finite; a program needn't handle non-finite values.
Results may differ from a plain program's by a relative error of at most 0.015.
Values may be sent and summed in bfloat16 or wider, within the bound.
No kernel may reach another device: no remote copies, remote signals or barrier semaphores. Data moves between devices by JAX's collectives and lax.ppermute only.
A program may use at most 192 MiB of HBM per device.

v0:
```python
import functools

import jax
import jax.numpy as jnp
from jax import lax
from jax.experimental import pallas as pl
from jax.experimental.pallas import tpu as pltpu
from jax.sharding import PartitionSpec as P

D = 768
HEADS = 12
FF = 3072
TILE = 256
ALL = ("wide", "narrow")
CHIP_STEPS = ((0, 0), (1, 0), (0, 1), (1, 1))
VMEM_LIMIT = 60 * 2**20
bf16, f32 = jnp.bfloat16, jnp.float32
Shape = jax.ShapeDtypeStruct

epsilon = 1e-06


def cost(us):
    return pl.CostEstimate(flops=0 * us, bytes_accessed=0, transcendentals=0)


def params():
    return pltpu.CompilerParams(vmem_limit_bytes=VMEM_LIMIT)


def send(values, z=0, y=0, x=0, core=0):
    flip_wide, flip_narrow = 2 * z + y, 2 * x + core
    pairs = [
        (w * 4 + n, (w ^ flip_wide) * 4 + (n ^ flip_narrow)) for w in range(8) for n in range(4)
    ]
    return lax.ppermute(values, ALL, pairs)


def position():
    wide, narrow = lax.axis_index("wide"), lax.axis_index("narrow")
    return wide // 2, wide % 2, narrow // 2, narrow % 2


def origin():
    zero = jnp.int32(0)
    return zero, zero, zero, zero


def gather_z(values):
    return [values] + [send(values, z=k) for k in (1, 2, 3)]


def gather_chips(lines):
    return [lines] + [send(lines, x=i, y=j) for i, j in CHIP_STEPS[1:]]


def gather_cores(blocks):
    return blocks + [send(block, core=1) for block in blocks]


def pair_kernel(count, *refs):
    core = lax.rem(lax.axis_index("narrow"), 2)
    more, outs = refs[2 * count : -count], refs[-count:]
    for own, other, out in zip(refs[:count], refs[count : 2 * count], outs):
        rows, columns = own.shape[0] // 2, own.shape[1]
        half = pl.ds(pl.multiple_of(core * rows, rows), rows)

        @pl.when(core == 0)
        def _(own=own, other=other, out=out, half=half, columns=columns):
            out[:, :columns] = own[half, :]
            out[:, columns : 2 * columns] = other[half, :]

        @pl.when(core == 1)
        def _(own=own, other=other, out=out, half=half, columns=columns):
            out[:, :columns] = other[half, :]
            out[:, columns : 2 * columns] = own[half, :]

    for vector in more:
        rest, parts = vector[...], []
        for _ in range(3):
            parts.append(rest.astype(bf16).astype(f32))
            rest = rest - parts[-1]
        outs[0][:, 1152:] = rows_of(48, *parts).astype(bf16)


def pair_up(pieces, others, vectors=None):
    more = [0] * len(pieces)
    rows = ()
    if vectors is not None:
        rows = (jnp.pad(vectors, (0, 384 - vectors.shape[0])).reshape(3, 128),)
        more[0] = 128
    return pl.pallas_call(
        functools.partial(pair_kernel, len(pieces)),
        out_shape=[
            Shape((piece.shape[0] // 2, piece.shape[1] * 2 + extra), piece.dtype)
            for piece, extra in zip(pieces, more)
        ],
        cost_estimate=cost(2),
        name="pair_up",
    )(*pieces, *others, *rows)


def assemble_kernel(widths, *refs):
    blocks, outs, sems = refs[:8], refs[8:-1], refs[-1]
    z, y, x, core = position()
    rows = blocks[0].shape[1]
    copies = []
    for other in range(2):
        for step, (i, j) in enumerate(CHIP_STEPS):
            block = blocks[other * 4 + step]
            for k in range(4):
                row = (((z ^ k) * 2 + (y ^ j)) * 2 + (core ^ other)) * rows
                left = 0
                for width, out in zip(widths, outs):
                    copies.append(
                        pltpu.make_async_copy(
                            block.at[k, :, pl.ds(left, width)],
                            out.at[
                                pl.ds(pl.multiple_of(row, rows), rows),
                                pl.ds(pl.multiple_of((x ^ i) * width, width), width),
                            ],
                            sems.at[len(copies)],
                        )
                    )
                    left += width
    for copy in copies:
        copy.start()
    for copy in copies:
        copy.wait()


def assemble(blocks, widths, name):
    rows = blocks[0].shape[1] * 16
    return pl.pallas_call(
        functools.partial(assemble_kernel, widths),
        out_shape=[Shape((rows, 2 * w), blocks[0].dtype) for w in widths],
        in_specs=[pl.BlockSpec(memory_space=pl.ANY)] * 8,
        out_specs=[pl.BlockSpec(memory_space=pltpu.VMEM)] * len(widths),
        scratch_shapes=[pltpu.SemaphoreType.DMA((32 * len(widths),))],
        compiler_params=params(),
        cost_estimate=cost(4),
        name=name,
    )(*blocks)


def table_kernel(table, out, sems):
    rows, columns = table.shape[1:]
    copies = []
    for w in range(8):
        for n in range(4):
            at = (w * 2 + n % 2) * rows
            copies.append(
                pltpu.make_async_copy(
                    table.at[w * 4 + n],
                    out.at[pl.ds(at, rows), pl.ds(n // 2 * columns, columns)],
                    sems.at[len(copies)],
                )
            )
    for copy in copies:
        copy.start()
    for copy in copies:
        copy.wait()


def assemble_table(table, name):
    rows, columns = table.shape[1:]
    return pl.pallas_call(
        table_kernel,
        out_shape=Shape((16 * rows, 2 * columns), table.dtype),
        in_specs=[pl.BlockSpec(memory_space=pl.ANY)],
        out_specs=pl.BlockSpec(memory_space=pltpu.VMEM),
        scratch_shapes=[pltpu.SemaphoreType.DMA((32,))],
        compiler_params=params(),
        cost_estimate=cost(5),
        name=name,
    )(table)


def place_kernel(*refs):
    z, y, x, core = position()
    out = refs[8]
    for other in range(2):
        for step, (i, j) in enumerate(CHIP_STEPS):
            for k in range(4):
                row = ((z ^ k) * 2 + (y ^ j)) * 4 + (x ^ i) * 2 + (core ^ other)
                parts = refs[other * 4 + step][k].astype(f32)
                out[row] = parts[:3] + parts[3:6] + parts[6:9]


def place_vectors(blocks):
    table = pl.pallas_call(
        place_kernel,
        grid=(1,),
        in_specs=[pl.BlockSpec((4, 16, 128), lambda i: (0, 0, 9))] * 8,
        out_specs=fixed((32, 3, 128)),
        out_shape=Shape((32, 3, 128), f32),
        cost_estimate=cost(1),
        name="place_vectors",
    )(*blocks)
    return table.reshape(32, 384)[:, :288].reshape(12, D)


def wide_sum(*terms):
    return functools.reduce(lambda a, b: a + b, [t.astype(f32) for t in terms])


def chip_parts(kept, received):
    return [wide_sum(kept[s], received[s]).astype(kept.dtype) for s in range(4)]


def chip_sends(parts):
    return [send(parts[s], x=i, y=j) for s, (i, j) in enumerate(CHIP_STEPS) if s]


def line_parts(own, others):
    return [
        wide_sum(own[k], *[other[k] for other in others]).astype(own.dtype) for k in range(4)
    ]


def line_sends(line):
    return [send(line[k], z=k) for k in (1, 2, 3)]


def line_halves(own, others):
    parts = line_parts(own, others)
    return parts[:2], jnp.stack(parts[2:])


def near_parts(near, received):
    return [wide_sum(near[k], received[k]).astype(near[k].dtype) for k in range(2)]


def swap_columns(summed):
    core = lax.axis_index("narrow") % 2
    columns = summed.shape[1] // 2
    left, right = summed[:, :columns], summed[:, columns:]
    mine = jnp.where(core == 0, left, right)
    other = send(jnp.where(core == 0, right, left).astype(bf16), core=1).astype(f32)
    return jnp.concatenate(
        [jnp.where(core == 0, mine, other), jnp.where(core == 0, other, mine)], 0
    )


def dot(left_side, right_side):
    return jnp.dot(left_side, right_side, preferred_element_type=f32)


def dot_t(left_side, right_side):
    return lax.dot_general(
        left_side, right_side, (((1,), (1,)), ((), ())), preferred_element_type=f32
    )


def column_sum(values):
    return jnp.sum(values, 0, keepdims=True)


def normalize(values):
    center = values - jnp.mean(values, -1, keepdims=True)
    inverse = lax.rsqrt(jnp.mean(center * center, -1, keepdims=True) + epsilon)
    return center * inverse, inverse


def normalize_back(grad_norm, normed, inverse):
    return inverse * (
        grad_norm
        - jnp.mean(grad_norm, -1, keepdims=True)
        - normed * jnp.mean(grad_norm * normed, -1, keepdims=True)
    )


def smooth(values):
    density = jnp.exp(-0.5 * values * values) * 0.3989422804014327
    below = 0.5 + 0.5 * lax.erf(values * 0.7071067811865476)
    return values * below, below + values * density


def fixed(shape):
    return pl.BlockSpec(shape, lambda i: (0,) * len(shape))


def tile(columns, rows=TILE):
    return pl.BlockSpec((rows, columns), lambda i: (i, 0))


def rows_of(count, *parts):
    missing = count - sum(part.shape[0] for part in parts)
    return jnp.concatenate(list(parts) + [jnp.zeros((missing, parts[0].shape[1]), f32)], 0)


def segment_marks(segment):
    kinds = lax.broadcasted_iota(jnp.int32, (1, 64), 1)
    mark = (segment.reshape(-1, 1) == kinds).astype(bf16)
    tall = lax.broadcasted_iota(jnp.int32, (1, 64, 1), 1)
    away = (segment[:, None, :] != tall) & (tall < 4)
    return jnp.concatenate([mark, mark], 1), jnp.where(away, -(2.0**30), 0.0).astype(bf16)


def attend_kernel(hidden, weight, vectors, key_marks, query_marks, packed, att, att_t, probs):
    length = hidden.shape[0]
    for part in range(3):
        columns = slice(part * D, (part + 1) * D)
        block = dot(hidden[...], weight[:, columns])
        if part != 1:
            block = block + vectors[part // 2 : part // 2 + 1, :]
        block = block.astype(bf16)
        if part == 0:
            block = block * jnp.asarray(0.125, bf16)
        packed[:, columns] = block
    lanes = lax.broadcasted_iota(jnp.int32, (length, 128), 1)

    def pair(p, _):
        at = pl.multiple_of(p * 128, 128)
        q_t = packed[:, pl.ds(at, 128)].T
        k = packed[:, pl.ds(D + at, 128)]
        v_t = packed[:, pl.ds(2 * D + at, 128)].T
        scores = []
        for odd in range(2):
            keys = jnp.where((lanes >= 64) == bool(odd), k, key_marks[...])
            own = q_t[64 * odd : 64 * odd + 64]
            marks = query_marks[0]
            scores.append(dot(keys, jnp.concatenate([marks, own] if odd else [own, marks], 0)))
        outs = []
        for odd in range(2):
            weights = jnp.exp(scores[odd] - jnp.max(scores[odd], 0, keepdims=True))
            low = (weights * (1.0 / column_sum(weights))).astype(bf16)
            probs[p * 2 + odd] = low
            outs.append(dot(v_t[64 * odd : 64 * odd + 64], low))
        out = jnp.concatenate(outs, 0).astype(bf16)
        att_t[pl.ds(at, 128), :] = out
        att[:, pl.ds(at, 128)] = out.T
        return 0

    lax.fori_loop(0, HEADS // 2, pair, 0, unroll=True)


def attend(hidden, weight, vectors, key_marks, query_marks):
    rows, length = query_marks.shape[0], query_marks.shape[2]
    tokens = rows * length
    return pl.pallas_call(
        attend_kernel,
        grid=(rows,),
        in_specs=[
            tile(D, length),
            fixed((D, 3 * D)),
            fixed((12, D)),
            tile(128, length),
            pl.BlockSpec((1, 64, length), lambda i: (i, 0, 0)),
        ],
        out_specs=[
            tile(3 * D, length),
            tile(D, length),
            pl.BlockSpec((D, length), lambda i: (0, i)),
            pl.BlockSpec((HEADS, length, length), lambda i: (i, 0, 0)),
        ],
        out_shape=[
            Shape((tokens, 3 * D), bf16),
            Shape((tokens, D), bf16),
            Shape((D, tokens), bf16),
            Shape((rows * HEADS, length, length), bf16),
        ],
        compiler_params=params(),
        cost_estimate=cost(20),
        name="attend",
    )(hidden, weight, vectors, key_marks, query_marks)


def inner_kernel(att, hidden, vectors, w_out, w_in, first_low, normed, inverse, activated, slope):
    def row(i):
        return vectors[i : i + 1, :]

    n1, r1 = normalize(hidden[...].astype(f32) + dot(att[...], w_out[...]) + row(2))
    low = (n1 * row(3) + row(4)).astype(bf16)
    first_low[...] = low
    normed[...] = n1
    inverse[...] = jnp.broadcast_to(r1, inverse.shape)
    for c in range(FF // D):
        columns = slice(c * D, c * D + D)
        act, back = smooth(dot(low, w_in[:, columns]) + row(5 + c))
        activated[:, columns] = act.astype(bf16)
        slope[:, columns] = back.astype(bf16)


def inner_forward(att, hidden, vectors, w_out, w_in):
    tokens = hidden.shape[0]
    return pl.pallas_call(
        inner_kernel,
        grid=(tokens // TILE,),
        in_specs=[tile(D)] * 2 + [fixed((12, D)), fixed((D, D)), fixed((D, FF))],
        out_specs=[tile(D), tile(D), tile(128), tile(FF), tile(FF)],
        out_shape=[
            Shape((tokens, D), bf16),
            Shape((tokens, D), f32),
            Shape((tokens, 128), f32),
            Shape((tokens, FF), bf16),
            Shape((tokens, FF), bf16),
        ],
        compiler_params=params(),
        cost_estimate=cost(16),
        name="inner_forward",
    )(att, hidden, vectors, w_out, w_in)


def outer_kernel(place, *refs):
    act, normed, cotangent, vectors, w_back = refs[:5]
    output, grad_second, sums, kept, sent, activated, grad_t = refs[5:]
    step = pl.program_id(0)
    z, y, x, core = place()

    def row(i):
        return vectors[i : i + 1, :]

    here = pl.ds(pl.multiple_of(step * TILE, TILE), TILE)
    activated[here, :] = act[...]
    outward = normed[...] * row(3) + row(4) + dot(act[...], w_back[...]) + row(9)
    n2, r2 = normalize(outward)
    output[...] = (n2 * row(10) + row(11)).astype(bf16)
    cot = cotangent[...].astype(f32)
    g2 = normalize_back(cot * row(10), n2, r2)
    grad_second[...] = g2
    part = rows_of(8, column_sum(g2), column_sum(cot * n2), column_sum(cot))

    @pl.when(step == 0)
    def _():
        sums[...] = part

    @pl.when(step > 0)
    def _():
        sums[...] += part

    g2_t = g2.astype(bf16).T
    for n in range(4):
        at = ((n % 2) ^ core) * 2 + ((n // 2) ^ x)
        piece = g2_t[n * 192 : n * 192 + 192]
        grad_t[pl.ds(pl.multiple_of(at * 192, 192), 192), here] = piece

    @pl.when(step == pl.num_programs(0) - 1)
    def _():
        for k in range(4):
            columns = pl.ds(pl.multiple_of((z ^ k) * D, D), D)
            res = dot(grad_t[...], activated[:, columns]).astype(bf16)
            for other, out in enumerate((kept, sent)):
                for i in range(2):
                    at = (other * 2 + i) * 192
                    for half in range(2):
                        piece = res[at : at + 192, half * 384 : half * 384 + 384]
                        out[i + 2 * (half ^ y), k] = piece


def outer_forward(place, activated, normed, cotangent, vectors, w_back):
    tokens = normed.shape[0]
    return pl.pallas_call(
        functools.partial(outer_kernel, place),
        grid=(tokens // TILE,),
        in_specs=[tile(FF), tile(D), tile(D), fixed((12, D)), fixed((FF, D))],
        out_specs=[tile(D), tile(D), fixed((8, D))] + [fixed((4, 4, 192, 384))] * 2,
        out_shape=[
            Shape((tokens, D), bf16),
            Shape((tokens, D), f32),
            Shape((8, D), f32),
        ]
        + [Shape((4, 4, 192, 384), bf16)] * 2,
        scratch_shapes=[pltpu.VMEM((tokens, FF), bf16), pltpu.VMEM((D, tokens), bf16)],
        compiler_params=params(),
        cost_estimate=cost(18),
        name="outer_forward",
    )(activated, normed, cotangent, vectors, w_back)


def backward_kernel(*refs):
    grad_second, slope, normed, inverse, vectors, w_out, w_in, w_back = refs[:8]
    grad_att, grad_branch, grad_low, inner_low, sums, sums_inner = refs[8:]
    step = pl.program_id(0)
    g2 = grad_second[...]
    g2_low = g2.astype(bf16)
    grad_first = g2
    inner_sums = []
    for c in range(FF // D):
        columns = slice(c * D, c * D + D)
        gi = dot_t(g2_low, w_back[columns, :]) * slope[:, columns].astype(f32)
        inner_sums.append(column_sum(gi))
        gi = gi.astype(bf16)
        inner_low[:, columns] = gi
        grad_first = grad_first + dot_t(gi, w_in[:, columns])
    n1 = normed[...]
    g1 = normalize_back(grad_first * vectors[3:4, :], n1, inverse[:, :1])
    grad_branch[...] = g1
    g1_low = g1.astype(bf16)
    grad_low[...] = g1_low
    grad_att[...] = dot_t(g1_low, w_out[...]).astype(bf16)
    part = rows_of(8, column_sum(g1), column_sum(grad_first * n1), column_sum(grad_first))
    part_inner = rows_of(8, *inner_sums)

    @pl.when(step == 0)
    def _():
        sums[...] = part
        sums_inner[...] = part_inner

    @pl.when(step > 0)
    def _():
        sums[...] += part
        sums_inner[...] += part_inner


def backward(grad_second, slope, normed, inverse, vectors, *weights):
    tokens = normed.shape[0]
    return pl.pallas_call(
        backward_kernel,
        grid=(tokens // TILE,),
        in_specs=[tile(D), tile(FF), tile(D), tile(128)]
        + [fixed(s) for s in ((12, D), (D, D), (D, FF), (FF, D))],
        out_specs=[tile(D), tile(D), tile(D), tile(FF), fixed((8, D)), fixed((8, D))],
        out_shape=[
            Shape((tokens, D), bf16),
            Shape((tokens, D), f32),
            Shape((tokens, D), bf16),
            Shape((tokens, FF), bf16),
            Shape((8, D), f32),
            Shape((8, D), f32),
        ],
        compiler_params=params(),
        cost_estimate=cost(22),
        name="backward",
    )(grad_second, slope, normed, inverse, vectors, *weights)


def grad_in_kernel(place, first_low, inner_low, kept, sent, first_t):
    step = pl.program_id(0)
    z, y, x, core = place()

    @pl.when(step == 0)
    def _():
        low_t = first_low[...].T
        for w in range(8):
            at = ((w % 2) ^ y) * 4 + ((w // 2) ^ z)
            first_t[pl.ds(pl.multiple_of(at * 96, 96), 96), :] = low_t[w * 96 : w * 96 + 96]

    res = dot(first_t[...], inner_low[...]).astype(bf16)
    i = (step // 2) ^ x
    for other, out in enumerate((kept, sent)):

        @pl.when((step % 2) ^ core == other)
        def _(out=out):
            for j in range(2):
                for k in range(4):
                    out[i + 2 * j, k] = res[(j * 4 + k) * 96 : (j * 4 + k) * 96 + 96]


def grad_in(place, first_low, inner_low):
    tokens = first_low.shape[0]
    out = (4, 4, 96, D)
    return pl.pallas_call(
        functools.partial(grad_in_kernel, place),
        grid=(FF // D,),
        in_specs=[fixed((tokens, D)), pl.BlockSpec((tokens, D), lambda i: (0, i))],
        out_specs=[fixed(out)] * 2,
        out_shape=[Shape(out, bf16)] * 2,
        scratch_shapes=[pltpu.VMEM((D, tokens), bf16)],
        compiler_params=params(),
        cost_estimate=cost(10),
        name="grad_in",
    )(first_low, inner_low)


def grad_out_kernel(place, att_t, grad_low, kept, sent, turned):
    _, _, x, _ = place()
    turn_rows(place, att_t, turned)
    res = dot(turned[...], grad_low[...]).astype(bf16)
    for other, out in enumerate((kept, sent)):
        for j in range(2):
            for k in range(4):
                at = (other * 8 + j * 4 + k) * 48
                for half in range(2):
                    piece = res[at : at + 48, half * 384 : half * 384 + 384]
                    out[(half ^ x) + 2 * j, k] = piece


def grad_out(place, att_t, grad_low):
    tokens = grad_low.shape[0]
    return pl.pallas_call(
        functools.partial(grad_out_kernel, place),
        out_shape=[Shape((4, 4, 48, 384), bf16)] * 2,
        scratch_shapes=[pltpu.VMEM((D, tokens), bf16)],
        compiler_params=params(),
        cost_estimate=cost(3),
        name="grad_out",
    )(att_t, grad_low)


def turn_rows(place, source, turned):
    z, y, _, core = place()
    for w in range(8):
        for half in range(2):
            at = (half ^ core) * 8 + ((w % 2) ^ y) * 4 + ((w // 2) ^ z)
            piece = (w * 2 + half) * 48
            turned[pl.ds(pl.multiple_of(at * 48, 48), 48), :] = source[piece : piece + 48, :]


def attend_back_kernel(packed, grad_att, probs, grad_low, sums):
    length = packed.shape[0]
    lanes = lax.broadcasted_iota(jnp.int32, (length, 128), 1)
    zero = jnp.zeros((length, 128), bf16)
    blank = jnp.zeros((64, length), bf16)

    def pair(p, _):
        at = pl.multiple_of(p * 128, 128)
        q = packed[:, pl.ds(at, 128)]
        k_t = packed[:, pl.ds(D + at, 128)].T
        v = packed[:, pl.ds(2 * D + at, 128)]
        g = grad_att[:, pl.ds(at, 128)]
        g_t = g.T
        grad_probs = []
        for odd in range(2):
            own = g_t[64 * odd : 64 * odd + 64]
            grad_probs.append(dot(v, jnp.concatenate([blank, own] if odd else [own, blank], 0)))
        dk = dv = 0.0
        dq_t = []
        for odd in range(2):
            mine = (lanes >= 64) == bool(odd)
            low = probs[p * 2 + odd]
            wide = low.astype(f32)
            gp = grad_probs[odd]
            ds = (wide * (gp - column_sum(wide * gp))).astype(bf16)
            dv = dv + dot(low, jnp.where(mine, g, zero))
            dk = dk + dot(ds, jnp.where(mine, q, zero))
            dq_t.append(dot(k_t[64 * odd : 64 * odd + 64], ds))
        dq = jnp.concatenate(dq_t, 0).T * 0.125
        sums[0, :, pl.ds(at, 128)] = rows_of(8, column_sum(dq), column_sum(dv))
        grad_low[:, pl.ds(at, 128)] = dq.astype(bf16)
        grad_low[:, pl.ds(D + at, 128)] = dk.astype(bf16)
        grad_low[:, pl.ds(2 * D + at, 128)] = dv.astype(bf16)
        return 0

    lax.fori_loop(0, HEADS // 2, pair, 0, unroll=True)


def attend_back(row, packed, grad_att, probs, low=None):
    length = probs.shape[1]
    kernel, more, specs, alias = attend_back_kernel, (), [], {}
    if low is not None:
        more, specs, alias = (low,), [pl.BlockSpec(memory_space=pl.ANY)], {3: 0}

        def kernel(packed, grad_att, probs, low, grad_low, sums):
            attend_back_kernel(packed, grad_att, probs, grad_low, sums)

    return pl.pallas_call(
        kernel,
        grid=(1,),
        in_specs=[
            pl.BlockSpec((length, 3 * D), lambda i: (row, 0)),
            pl.BlockSpec((length, D), lambda i: (row, 0)),
            pl.BlockSpec((HEADS, length, length), lambda i: (row, 0, 0)),
        ]
        + specs,
        out_specs=[
            pl.BlockSpec((length, 3 * D), lambda i: (row, 0)),
            pl.BlockSpec((1, 8, D), lambda i: (0, 0, 0)),
        ],
        out_shape=[Shape(packed.shape, bf16), Shape((1, 8, D), f32)],
        input_output_aliases=alias,
        compiler_params=params(),
        cost_estimate=cost(12),
        name="attend_back",
    )(packed, grad_att, probs, *more)


def grad_qkv_kernel(place, hidden, low, table, kept_out, sent_out, kept, sent, turned):
    z, y, x, core = place()
    turn_rows(place, hidden[...].T, turned)
    for i in range(2):
        columns = pl.ds(pl.multiple_of((x ^ i) * 1152, 128), 1152)
        res = dot(turned[...], low[:, columns]).astype(bf16)
        for other, out, more in ((0, kept, kept_out), (1, sent, sent_out)):
            for j in range(2):
                step = i + 2 * j
                for k in range(4):
                    at = (other * 8 + j * 4 + k) * 48
                    out[step, k, :, :1152] = res[at : at + 48]
                    out[step, k, :, 1152:1536] = more[step, k]
                    device = ((z ^ k) * 2 + (y ^ j)) * 4 + (x ^ i) * 2 + (core ^ other)
                    out[step, k, :16, 1536:] = table[device]
                    out[step, k, 16:, 1536:] = jnp.zeros((32, 128), bf16)


def grad_qkv(place, hidden, low, vectors, out_tables):
    table = jnp.pad(vectors.astype(bf16).reshape(32, 288), ((0, 0), (0, 96)))
    table = jnp.pad(table.reshape(32, 3, 128), ((0, 0), (0, 13), (0, 0)))
    return pl.pallas_call(
        functools.partial(grad_qkv_kernel, place),
        out_shape=[Shape((4, 4, 48, 1664), bf16)] * 2,
        scratch_shapes=[pltpu.VMEM((D, hidden.shape[0]), bf16)],
        compiler_params=params(),
        cost_estimate=cost(9),
        name="grad_qkv",
    )(hidden, low, table, *out_tables)


def hidden_kernel(low, weight, grad_branch, out):
    out[...] = grad_branch[...] + dot_t(low[...], weight[...])


def grad_of_hidden(low, weight, grad_branch):
    tokens = low.shape[0]
    return pl.pallas_call(
        hidden_kernel,
        grid=(tokens // TILE,),
        in_specs=[tile(3 * D), fixed((D, 3 * D)), tile(D)],
        out_specs=tile(D),
        out_shape=Shape((tokens, D), f32),
        compiler_params=params(),
        cost_estimate=cost(9),
        name="grad_hidden",
    )(low, weight, grad_branch)


def gather_plain(w_qkv, w_out, w_in, w_back, vectors):
    def whole(piece):
        return lax.all_gather(
            lax.all_gather(piece, "narrow", axis=1, tiled=True), "wide", axis=0, tiled=True
        )

    full = tuple(whole(piece) for piece in (w_qkv, w_out, w_in, w_back))
    return full + (lax.all_gather(vectors, ALL, axis=0, tiled=True).reshape(12, D),)


def tie(*values):
    return lax.optimization_barrier(values)


def unfold(table, order, shape):
    return table.reshape((2, 2, 2, 4) + table.shape[3:]).transpose(order).reshape(shape)


def scatter_whole(matrix):
    part = lax.psum_scatter(matrix, "wide", scatter_dimension=0, tiled=True)
    part = lax.psum_scatter(part, "narrow", scatter_dimension=1, tiled=True)
    return part.astype(f32)


def per_device(hidden, segment, w_qkv, w_out, w_in, w_back, vectors, cotangent):
    (qkv,) = pair_up([w_qkv], [send(w_qkv, core=1)], vectors)
    rest = [w_out, w_in, w_back]
    other_rest = [send(piece, core=1) for piece in rest]
    qkv, other_rest, segment = tie(qkv, other_rest, segment)
    key_marks, query_marks = segment_marks(segment)
    qkv_line = gather_z(qkv)
    out, inner, back = pair_up(rest, other_rest)
    mid = jnp.concatenate([inner, out], 1)
    qkv_line, mid, back, key_marks, query_marks = tie(
        jnp.stack(qkv_line), mid, back, key_marks, query_marks
    )

    qkv_blocks = gather_chips(qkv_line)
    mid_line = gather_z(mid)
    qkv_blocks, mid_line, back = tie(qkv_blocks, mid_line, back)

    back_table = lax.all_gather(back, ALL, axis=0, tiled=False)
    mid_blocks = gather_chips(jnp.stack(mid_line))
    qkv_blocks = gather_cores(qkv_blocks)
    full_qkv = assemble(qkv_blocks, (1152,), "assemble_qkv")[0]
    all_vectors = place_vectors(qkv_blocks)
    attended = attend(hidden, full_qkv, all_vectors, key_marks, query_marks)
    attended, mid_blocks = tie(attended, mid_blocks)
    packed, att, att_t, probs = attended

    full_in, full_out = assemble(gather_cores(mid_blocks), (1536, 384), "assemble_in")
    inner_outs = inner_forward(att, hidden, all_vectors, full_out, full_in)
    inner_outs, back_table = tie(inner_outs, back_table)
    first_low, normed, inverse, activated, slope = inner_outs

    full_back = assemble_table(back_table, "assemble_back")
    output, grad_second, sums_second, kept_back, sent_back = outer_forward(
        position, activated, normed, cotangent, all_vectors, full_back
    )

    received_back = send(sent_back, core=1)
    back_outs = backward(
        grad_second, slope, normed, inverse, all_vectors, full_out, full_in, full_back
    )
    back_outs, received_back = tie(back_outs, received_back)
    grad_att, grad_branch, branch_low, inner_low, sums_first, sums_inner = back_outs

    parts_back = chip_parts(kept_back, received_back)
    parts_back, inner_low = tie(parts_back, inner_low)
    plane_back = [send(parts_back[1], x=1), send(parts_back[2], y=1)]
    kept_in, sent_in = grad_in(position, first_low, inner_low)
    kept_in, sent_in, plane_back, corner_back = tie(kept_in, sent_in, plane_back, parts_back[3])

    corner_back = send(corner_back, x=1, y=1)
    received_in = send(sent_in, core=1)
    out_tables = grad_out(position, att_t, branch_low)
    out_tables, received_in = tie(out_tables, received_in)

    parts_in = chip_parts(kept_in, received_in)
    parts_in, grad_att, out_tables = tie(parts_in, grad_att, out_tables)
    others_in = chip_sends(parts_in)
    packed_low, sums_zero = attend_back(0, packed, grad_att, probs)
    packed_low, corner_back = tie(packed_low, corner_back)

    near_back, far_back = line_halves(parts_back[0], plane_back + [corner_back])
    near_back, far_back, packed_low = tie(near_back, far_back, packed_low)
    far_back = send(far_back, z=2)
    packed_low, sums_one = attend_back(1, packed, grad_att, probs, packed_low)
    packed_low, far_back, sums_one = tie(packed_low, far_back, sums_one)

    near_back = near_parts(near_back, far_back)
    next_back = send(near_back[1], z=1)
    grad_vectors = jnp.concatenate(
        [(sums_zero + sums_one)[0, :2], sums_first[:3], sums_inner[:4], sums_second[:3]], 0
    )
    kept_qkv, sent_qkv = grad_qkv(position, hidden, packed_low, grad_vectors, out_tables)
    kept_qkv, sent_qkv, next_back, others_in = tie(kept_qkv, sent_qkv, next_back, others_in)

    received_qkv = send(sent_qkv, core=1)
    near_in, far_in = line_halves(parts_in[0], others_in)
    far_in = send(far_in, z=2)
    parts_qkv = chip_parts(kept_qkv, received_qkv)
    parts_qkv, grad_branch = tie(parts_qkv, grad_branch)
    others_qkv = chip_sends(parts_qkv)
    grad_hidden = grad_of_hidden(packed_low, full_qkv, grad_branch)
    own_back = wide_sum(near_back[0], next_back).T
    grad_hidden, far_in, own_back = tie(grad_hidden, far_in, own_back)

    near_in = near_parts(near_in, far_in)
    next_in = send(near_in[1], z=1)
    others_qkv, near_in = tie(others_qkv, near_in)
    line_qkv = line_parts(parts_qkv[0], others_qkv)
    lines_qkv = line_sends(line_qkv)
    own_in = wide_sum(near_in[0], next_in)
    own_in, lines_qkv = tie(own_in, lines_qkv)
    own_qkv = wide_sum(line_qkv[0], *lines_qkv)
    own_vectors = own_qkv[:3, 1536:].reshape(-1)[:288]
    own_out = swap_columns(own_qkv[:, 1152:1536])
    own_qkv = swap_columns(own_qkv[:, :1152])
    return (output, grad_hidden, own_qkv, own_out, own_in, own_back, own_vectors)


def per_device_plain(hidden, segment, w_qkv, w_out, w_in, w_back, vectors, cotangent):
    key_marks, query_marks = segment_marks(segment)
    full_qkv, full_out, full_in, full_back, all_vectors = gather_plain(
        w_qkv, w_out, w_in, w_back, vectors
    )
    packed, att, att_t, probs = attend(hidden, full_qkv, all_vectors, key_marks, query_marks)
    first_low, normed, inverse, activated, slope = inner_forward(
        att, hidden, all_vectors, full_out, full_in
    )
    output, grad_second, sums_second, *back_table = outer_forward(
        origin, activated, normed, cotangent, all_vectors, full_back
    )
    grad_att, grad_branch, branch_low, inner_low, sums_first, sums_inner = backward(
        grad_second, slope, normed, inverse, all_vectors, full_out, full_in, full_back
    )
    in_table = jnp.stack(grad_in(origin, first_low, inner_low))
    out_table = grad_out(origin, att_t, branch_low)
    packed_low, sums_zero = attend_back(0, packed, grad_att, probs)
    packed_low, sums_one = attend_back(1, packed, grad_att, probs, packed_low)
    grad_hidden = grad_of_hidden(packed_low, full_qkv, grad_branch)
    grad_vectors = jnp.concatenate(
        [(sums_zero + sums_one)[0, :2], sums_first[:3], sums_inner[:4], sums_second[:3]], 0
    )
    qkv_table = jnp.stack(grad_qkv(origin, hidden, packed_low, grad_vectors, out_table))
    full_qkv, full_out = qkv_table[..., :1152], qkv_table[..., 1152:1536]
    own_qkv = scatter_whole(unfold(full_qkv, (3, 1, 0, 4, 2, 5), (D, 3 * D)))
    own_out = scatter_whole(unfold(full_out, (3, 1, 0, 4, 2, 5), (D, D)))
    own_in = scatter_whole(unfold(in_table, (3, 1, 4, 2, 0, 5), (D, FF)))
    back_t = unfold(jnp.stack(back_table), (2, 0, 4, 3, 1, 5), (D, FF))
    own_back = scatter_whole(back_t.T)
    own_vectors = lax.psum_scatter(
        grad_vectors.reshape(-1), ALL, scatter_dimension=0, tiled=True
    )
    return (output, grad_hidden, own_qkv, own_out, own_in, own_back, own_vectors)


def solution(mesh):
    trees = mesh.shape["wide"] == 8 and mesh.shape["narrow"] == 4
    return jax.shard_map(
        per_device if trees else per_device_plain,
        mesh=mesh,
        in_specs=(P(ALL, None),) * 2 + (P("wide", "narrow"),) * 4 + (P(ALL), P(ALL, None)),
        out_specs=(P(ALL, None),) * 2 + (P("wide", "narrow"),) * 4 + (P(ALL),),
        check_vma=False,
    )
```

profile of v0, /device:TPU:0, one launch (start us, length us, event | category | flops | bytes accessed | tf_op | source)
XLA Modules:
  0.0 318.5 jit_solution(14318614448464451931)
XLA Ops:
  25.1 3.7 %collective-permute-done.5 = bf16[48,1280]{1,0:T(8,128)(2,1)S(1)} collective-permute-done((bf16[48,1280]{1,0:T(8,128)(2,1)}, bf16[48,1280]{1,0:T(8,128)(2,1)S(1)}, u32[]{:S(2)}, u32[]{:S(2)}) %collective-permute-start.5) | collective-permute-done | bytes 122912 | tf_op jit(solution)/shard_map/ppermute | solution.py:36
  35.4 4.7 %collective-permute-done.10 = bf16[48,1920]{1,0:T(8,128)(2,1)S(1)} collective-permute-done((bf16[48,1920]{1,0:T(8,128)(2,1)S(1)}, bf16[48,1920]{1,0:T(8,128)(2,1)S(1)}, u32[]{:S(2)}, u32[]{:S(2)}) %collective-permute-start.10) | collective-permute-done | bytes 184352 | tf_op jit(solution)/shard_map/ppermute | solution.py:36
  42.0 7.5 %collective-permute-done.11 = bf16[48,1920]{1,0:T(8,128)(2,1)S(1)} collective-permute-done((bf16[48,1920]{1,0:T(8,128)(2,1)S(1)}, bf16[48,1920]{1,0:T(8,128)(2,1)S(1)}, u32[]{:S(2)}, u32[]{:S(2)}) %collective-permute-start.11) | collective-permute-done | bytes 184352 | tf_op jit(solution)/shard_map/ppermute | solution.py:36
  62.9 4.1 %assemble_qkv.1.weight = bf16[768,2304]{1,0:T(8,128)(2,1)} custom-call(bf16[4,48,1280]{2,1,0:T(8,128)(2,1)} %copy-done, bf16[4,48,1280]{2,1,0:T(8,128)(2,1)} %copy-done.4, bf16[4,48,1280]{2,1,0:T(8,128)(2,1)} %copy-done.5, bf16[4,48,1280]{2,1,0:T(8,128)(2,1)} %copy-done.6, bf16[4,48,1280]{2,1,0:T(8,128)(2,1)} %copy-done.7, bf16[4,48,1280]{2,1,0:T(8,128)(2,1)} %copy-done.8, ...), custom_call_target="tpu_custom_call" | custom-call | tf_op jit(solution)/shard_map/assemble_qkv/pallas_call | solution.py:134
  67.0 20.4 %attend.1 = (bf16[1024,2304]{1,0:T(8,128)(2,1)}, bf16[1024,768]{1,0:T(8,128)(2,1)}, bf16[768,1024]{1,0:T(8,128)(2,1)}, bf16[24,512,512]{2,1,0:T(8,128)(2,1)}) custom-call(bf16[1024,768]{1,0:T(8,128)(2,1)} %hidden.5, bf16[768,2304]{1,0:T(8,128)(2,1)} %assemble_qkv.1.weight, f32[12,768]{1,0:T(8,128)} %reshape.162.vectors.refs_3_.refs_4_, ...), custom_call_target="tpu_custom_call" | custom-call | tf_op jit(solution)/shard_map/attend/pallas_call | solution.py:341
  87.5 6.7 %collective-permute-done.19.refs_3_ = bf16[4,48,1920]{2,1,0:T(8,128)(2,1)} collective-permute-done((bf16[4,48,1920]{2,1,0:T(8,128)(2,1)S(1)}, bf16[4,48,1920]{2,1,0:T(8,128)(2,1)}, u32[]{:S(2)}, u32[]{:S(2)}) %collective-permute-start.19) | collective-permute-done | bytes 737312 | tf_op jit(solution)/shard_map/ppermute | solution.py:36
  100.7 5.9 %assemble_in.1 = (bf16[768,3072]{1,0:T(8,128)(2,1)}, bf16[768,768]{1,0:T(8,128)(2,1)}) custom-call(bf16[4,48,1920]{2,1,0:T(8,128)(2,1)} %copy-done.1, bf16[4,48,1920]{2,1,0:T(8,128)(2,1)} %collective-permute-done.17.refs_1_, bf16[4,48,1920]{2,1,0:T(8,128)(2,1)} %collective-permute-done.18.refs_2_, bf16[4,48,1920]{2,1,0:T(8,128)(2,1)} %collective-permute-done.19.refs_3_, ...), custom_call_target="tpu_custom_call" | custom-call | tf_op jit(solution)/shard_map/assemble_in/pallas_call | solution.py:134
  106.6 17.9 %inner_forward.1 = (bf16[1024,768]{1,0:T(8,128)(2,1)}, f32[1024,768]{1,0:T(8,128)}, f32[1024,128]{1,0:T(8,128)}, bf16[1024,3072]{1,0:T(8,128)(2,1)}, bf16[1024,3072]{1,0:T(8,128)(2,1)}) custom-call(bf16[1024,768]{1,0:T(8,128)(2,1)} %get-tuple-element.158.att, bf16[1024,768]{1,0:T(8,128)(2,1)} %hidden.5, f32[12,768]{1,0:T(8,128)} %reshape.162.vectors.refs_3_.refs_4_, ...), custom_call_target="tpu_custom_call" | custom-call | tf_op jit(solution)/shard_map/inner_forward/pallas_call | solution.py:387
  124.4 4.8 %assemble_back.1.refs_4_.refs_7_ = bf16[3072,768]{1,0:T(8,128)(2,1)} custom-call(bf16[32,192,384]{2,1,0:T(8,128)(2,1)} %bitcast.74), custom_call_target="tpu_custom_call" | custom-call | tf_op jit(solution)/shard_map/assemble_back/pallas_call | solution.py:167
  129.3 20.7 %outer_forward.1 = (bf16[1024,768]{1,0:T(8,128)(2,1)}, f32[1024,768]{1,0:T(8,128)}, f32[8,768]{1,0:T(8,128)}, bf16[4,4,192,384]{3,2,1,0:T(8,128)(2,1)}, bf16[4,4,192,384]{3,2,1,0:T(8,128)(2,1)}) custom-call(bf16[1024,3072]{1,0:T(8,128)(2,1)} %get-tuple-element.171.refs_0_, f32[1024,768]{1,0:T(8,128)} %get-tuple-element.172.refs_1_.refs_2_, ...), custom_call_target="tpu_custom_call" | custom-call | tf_op jit(solution)/shard_map/outer_forward/pallas_call | solution.py:453
  150.1 21.0 %backward.1 = (bf16[1024,768]{1,0:T(8,128)(2,1)}, f32[1024,768]{1,0:T(8,128)}, bf16[1024,768]{1,0:T(8,128)(2,1)}, bf16[1024,3072]{1,0:T(8,128)(2,1)}, f32[8,768]{1,0:T(8,128)}, /*index=5*/f32[8,768]{1,0:T(8,128)}) custom-call(f32[1024,768]{1,0:T(8,128)} %get-tuple-element.178.refs_0_, bf16[1024,3072]{1,0:T(8,128)(2,1)} %get-tuple-element.179.refs_1_, ...), custom_call_target="tpu_custom_call" | custom-call | tf_op jit(solution)/shard_map/backward/pallas_call | solution.py:508
  171.2 3.3 %fusion.7 = (bf16[4,192,384]{2,1,0:T(8,128)(2,1)}, bf16[4,192,384]{2,1,0:T(8,128)(2,1)S(1)}, bf16[4,192,384]{2,1,0:T(8,128)(2,1)}, bf16[4,192,384]{2,1,0:T(8,128)(2,1)S(1)}) fusion(bf16[4,4,192,384]{3,2,1,0:T(8,128)(2,1)} %collective-permute-done.24, bf16[4,4,192,384]{3,2,1,0:T(8,128)(2,1)S(1)} %copy-done.3), kind=kLoop, calls=%fused_computation.20 | loop fusion | flops 4718592 | bytes 7077888 | tf_op jit(solution)/shard_map/convert_element_type | solution.py:208
  177.0 10.9 %grad_in.1 = (bf16[4,4,96,768]{3,2,1,0:T(8,128)(2,1)}, bf16[4,4,96,768]{3,2,1,0:T(8,128)(2,1)}) custom-call(bf16[1024,768]{1,0:T(8,128)(2,1)} %get-tuple-element.176.first_low, bf16[1024,3072]{1,0:T(8,128)(2,1)} %get-tuple-element.190.inner_low), custom_call_target="tpu_custom_call" | custom-call | tf_op jit(solution)/shard_map/grad_in/pallas_call | solution.py:553
  193.3 4.3 %grad_out.1 = (bf16[4,4,48,384]{3,2,1,0:T(8,128)(2,1)}, bf16[4,4,48,384]{3,2,1,0:T(8,128)(2,1)}) custom-call(bf16[768,1024]{1,0:T(8,128)(2,1)} %get-tuple-element.197.att_t, bf16[1024,768]{1,0:T(8,128)(2,1)} %get-tuple-element.198.grad_low), custom_call_target="tpu_custom_call" | custom-call | tf_op jit(solution)/shard_map/grad_out/pallas_call | solution.py:581
  197.6 3.2 %fusion.11 = (bf16[4,96,768]{2,1,0:T(8,128)(2,1)}, bf16[4,96,768]{2,1,0:T(8,128)(2,1)}, bf16[4,96,768]{2,1,0:T(8,128)(2,1)}, bf16[4,96,768]{2,1,0:T(8,128)(2,1)S(1)}) fusion(bf16[4,4,96,768]{3,2,1,0:T(8,128)(2,1)} %collective-permute-done.27, bf16[4,4,96,768]{3,2,1,0:T(8,128)(2,1)S(1)} %copy-done.2), kind=kLoop, calls=%fused_computation.24 | loop fusion | flops 4718592 | bytes 7077888 | tf_op jit(solution)/shard_map/convert_element_type | solution.py:208
  200.8 13.3 %attend_back.2 = (bf16[1024,2304]{1,0:T(8,128)(2,1)}, f32[1,8,768]{2,1,0:T(8,128)}) custom-call(bf16[1024,2304]{1,0:T(8,128)(2,1)} %get-tuple-element.175.packed, bf16[1024,768]{1,0:T(8,128)(2,1)} %get-tuple-element.206.grad_att, bf16[24,512,512]{2,1,0:T(8,128)(2,1)} %get-tuple-element.207.probs), custom_call_target="tpu_custom_call" | custom-call | tf_op jit(solution)/shard_map/attend_back/pallas_call | solution.py:647
  216.6 3.6 %collective-permute-start.29 = (bf16[2,192,384]{2,1,0:T(8,128)(2,1)S(1)}, bf16[2,192,384]{2,1,0:T(8,128)(2,1)S(1)}, u32[]{:S(2)}, u32[]{:S(2)}) collective-permute-start(bf16[2,192,384]{2,1,0:T(8,128)(2,1)S(1)} %pad_maximum_fusion.2), channel_id=1, source_target_pairs={{0,16},{1,17},{2,18},{3,19},{4,20},{5,21},{6,22},{7,23},{8,24},{9,... | collective-permute-start | bytes 884744 | tf_op jit(solution)/shard_map/ppermute | solution.py:36
  225.9 13.5 %attend_back.3 = (bf16[1024,2304]{1,0:T(8,128)(2,1)}, f32[1,8,768]{2,1,0:T(8,128)}) custom-call(bf16[1024,2304]{1,0:T(8,128)(2,1)} %get-tuple-element.175.packed, bf16[1024,768]{1,0:T(8,128)(2,1)} %get-tuple-element.206.grad_att, bf16[24,512,512]{2,1,0:T(8,128)(2,1)} %get-tuple-element.207.probs, ...), custom_call_target="tpu_custom_call", output_to_operand_aliasing={{0}: (3, {})} | custom-call | tf_op jit(solution)/shard_map/attend_back/pallas_call | solution.py:647
  241.7 10.1 %grad_qkv.1 = (bf16[4,4,48,1664]{3,2,1,0:T(8,128)(2,1)}, bf16[4,4,48,1664]{3,2,1,0:T(8,128)(2,1)}) custom-call(bf16[1024,768]{1,0:T(8,128)(2,1)} %hidden.5, bf16[1024,2304]{1,0:T(8,128)(2,1)} %get-tuple-element.219.low, bf16[32,16,128]{2,1,0:T(8,128)(2,1)} %pad.14.table, bf16[4,4,48,384]{3,2,1,0:T(8,128)(2,1)} %get-tuple-element.225.kept_out, ...), custom_call_target="tpu_custom_call" | custom-call | tf_op jit(solution)/shard_map/grad_qkv/pallas_call | solution.py:689
  253.4 3.6 %collective-permute-done.34 = bf16[4,4,48,1664]{3,2,1,0:T(8,128)(2,1)S(1)} collective-permute-done((bf16[4,4,48,1664]{3,2,1,0:T(8,128)(2,1)}, bf16[4,4,48,1664]{3,2,1,0:T(8,128)(2,1)S(1)}, u32[]{:S(2)}, u32[]{:S(2)}) %collective-permute-start.34) | collective-permute-done | bytes 2555936 | tf_op jit(solution)/shard_map/ppermute | solution.py:36
  257.0 3.4 %fusion.3 = (bf16[4,48,1664]{2,1,0:T(8,128)(2,1)}, bf16[4,48,1664]{2,1,0:T(8,128)(2,1)}, bf16[4,48,1664]{2,1,0:T(8,128)(2,1)}, bf16[4,48,1664]{2,1,0:T(8,128)(2,1)S(1)}) fusion(bf16[4,4,48,1664]{3,2,1,0:T(8,128)(2,1)S(1)} %collective-permute-done.34, bf16[4,4,48,1664]{3,2,1,0:T(8,128)(2,1)} %get-tuple-element.234), kind=kLoop, calls=%fused_computation.16 | loop fusion | flops 5111808 | bytes 7667712 | tf_op jit(solution)/shard_map/convert_element_type | solution.py:208
  268.2 9.2 %grad_hidden.1 = f32[1024,768]{1,0:T(8,128)} custom-call(bf16[1024,2304]{1,0:T(8,128)(2,1)} %get-tuple-element.219.low, bf16[768,2304]{1,0:T(8,128)(2,1)} %assemble_qkv.1.weight, f32[1024,768]{1,0:T(8,128)} %get-tuple-element.237.grad_branch), custom_call_target="tpu_custom_call" | custom-call | tf_op jit(solution)/shard_map/grad_hidden/pallas_call | solution.py:705
  281.9 8.2 %collective-permute-done.37 = bf16[4,48,1664]{2,1,0:T(8,128)(2,1)S(1)} collective-permute-done((bf16[4,48,1664]{2,1,0:T(8,128)(2,1)}, bf16[4,48,1664]{2,1,0:T(8,128)(2,1)S(1)}, u32[]{:S(2)}, u32[]{:S(2)}) %collective-permute-start.37) | collective-permute-done | bytes 639008 | tf_op jit(solution)/shard_map/ppermute | solution.py:36
  298.9 9.1 %collective-permute-done.41 = bf16[48,1664]{1,0:T(8,128)(2,1)S(1)} collective-permute-done((bf16[48,1664]{1,0:T(8,128)(2,1)S(1)}, bf16[48,1664]{1,0:T(8,128)(2,1)S(1)}, u32[]{:S(2)}, u32[]{:S(2)}) %collective-permute-start.41) | collective-permute-done | bytes 159776 | tf_op jit(solution)/shard_map/ppermute | solution.py:36
  (190 shorter events, 90.6 us)
Async XLA Ops:
  7.2 117.3 %all-gather.3.cloned.1.call-start = ((), (), s32[]{:S(2)}) async-start(), calls=%async_computation | async-start | bytes 4866048 | tf_op jit(solution)/shard_map/all_gather | solution.py:758
  16.1 12.6 %collective-permute-start.5 = (bf16[48,1280]{1,0:T(8,128)(2,1)}, bf16[48,1280]{1,0:T(8,128)(2,1)S(1)}, u32[]{:S(2)}, u32[]{:S(2)}) collective-permute-start(bf16[48,1280]{1,0:T(8,128)(2,1)} %pair_up.2), channel_id=1, source_target_pairs={{0,16},{1,17},{2,18},{3,19},{4,20},{5,21},{6,22},{7,23},{8,24},{9,... | collective-permute-start | bytes 368648 | tf_op jit(solution)/shard_map/ppermute | solution.py:36
  28.8 20.7 %collective-permute-start.7 = (bf16[4,48,1280]{2,1,0:T(8,128)(2,1)S(1)}, bf16[4,48,1280]{2,1,0:T(8,128)(2,1)S(1)}, u32[]{:S(2)}, u32[]{:S(2)}) collective-permute-start(bf16[4,48,1280]{2,1,0:T(8,128)(2,1)S(1)} %pad_maximum_fusion.1.refs_0_), channel_id=1, source_target_pairs={{0,2},{1,3},{2,0},{3,1},{4,6},{5,7},{6,4},{7,5},{8,10},{9,11},{10,... | collective-permute-start | bytes 1474568 | tf_op jit(solution)/shard_map/ppermute | solution.py:36
  30.4 21.3 %collective-permute-start.8 = (bf16[4,48,1280]{2,1,0:T(8,128)(2,1)S(1)}, bf16[4,48,1280]{2,1,0:T(8,128)(2,1)S(1)}, u32[]{:S(2)}, u32[]{:S(2)}) collective-permute-start(bf16[4,48,1280]{2,1,0:T(8,128)(2,1)S(1)} %pad_maximum_fusion.1.refs_0_), channel_id=1, source_target_pairs={{0,4},{1,5},{2,6},{3,7},{4,0},{5,1},{6,2},{7,3},{8,12},{9,13},{10,... | collective-permute-start | bytes 1474568 | tf_op jit(solution)/shard_map/ppermute | solution.py:36
  31.9 19.8 %collective-permute-start.9 = (bf16[4,48,1280]{2,1,0:T(8,128)(2,1)S(1)}, bf16[4,48,1280]{2,1,0:T(8,128)(2,1)S(1)}, u32[]{:S(2)}, u32[]{:S(2)}) collective-permute-start(bf16[4,48,1280]{2,1,0:T(8,128)(2,1)S(1)} %pad_maximum_fusion.1.refs_0_), channel_id=1, source_target_pairs={{0,6},{1,7},{2,4},{3,5},{4,2},{5,3},{6,0},{7,1},{8,14},{9,15},{10,... | collective-permute-start | bytes 1474568 | tf_op jit(solution)/shard_map/ppermute | solution.py:36
  34.4 15.0 %collective-permute-start.11 = (bf16[48,1920]{1,0:T(8,128)(2,1)S(1)}, bf16[48,1920]{1,0:T(8,128)(2,1)S(1)}, u32[]{:S(2)}, u32[]{:S(2)}) collective-permute-start(bf16[48,1920]{1,0:T(8,128)(2,1)S(1)} %pad_maximum_fusion.5), channel_id=1, source_target_pairs={{0,16},{1,17},{2,18},{3,19},{4,20},{5,21},{6,22},{7,23},{8,24},{9,... | collective-permute-start | bytes 552968 | tf_op jit(solution)/shard_map/ppermute | solution.py:36
  53.5 33.9 %collective-permute-start.17 = (bf16[4,48,1920]{2,1,0:T(8,128)(2,1)S(1)}, bf16[4,48,1920]{2,1,0:T(8,128)(2,1)}, u32[]{:S(2)}, u32[]{:S(2)}) collective-permute-start(bf16[4,48,1920]{2,1,0:T(8,128)(2,1)S(1)} %pad_maximum_fusion.refs_0_), channel_id=1, source_target_pairs={{0,2},{1,3},{2,0},{3,1},{4,6},{5,7},{6,4},{7,5},{8,10},{9,11},{10,... | collective-permute-start | bytes 2211848 | tf_op jit(solution)/shard_map/ppermute | solution.py:36
  54.8 32.7 %collective-permute-start.18 = (bf16[4,48,1920]{2,1,0:T(8,128)(2,1)S(1)}, bf16[4,48,1920]{2,1,0:T(8,128)(2,1)}, u32[]{:S(2)}, u32[]{:S(2)}) collective-permute-start(bf16[4,48,1920]{2,1,0:T(8,128)(2,1)S(1)} %pad_maximum_fusion.refs_0_), channel_id=1, source_target_pairs={{0,4},{1,5},{2,6},{3,7},{4,0},{5,1},{6,2},{7,3},{8,12},{9,13},{10,... | collective-permute-start | bytes 2211848 | tf_op jit(solution)/shard_map/ppermute | solution.py:36
  55.6 38.5 %collective-permute-start.19 = (bf16[4,48,1920]{2,1,0:T(8,128)(2,1)S(1)}, bf16[4,48,1920]{2,1,0:T(8,128)(2,1)}, u32[]{:S(2)}, u32[]{:S(2)}) collective-permute-start(bf16[4,48,1920]{2,1,0:T(8,128)(2,1)S(1)} %pad_maximum_fusion.refs_0_), channel_id=1, source_target_pairs={{0,6},{1,7},{2,4},{3,5},{4,2},{5,3},{6,0},{7,1},{8,14},{9,15},{10,... | collective-permute-start | bytes 2211848 | tf_op jit(solution)/shard_map/ppermute | solution.py:36
  149.9 21.2 %collective-permute-start.24 = (bf16[4,4,192,384]{3,2,1,0:T(8,128)(2,1)}, bf16[4,4,192,384]{3,2,1,0:T(8,128)(2,1)}, u32[]{:S(2)}, u32[]{:S(2)}) collective-permute-start(bf16[4,4,192,384]{3,2,1,0:T(8,128)(2,1)} %get-tuple-element.187), channel_id=1, source_target_pairs={{0,1},{1,0},{2,3},{3,2},{4,5},{5,4},{6,7},{7,6},{8,9},{9,8},{10,11... | collective-permute-start | bytes 7077896 | tf_op jit(solution)/shard_map/ppermute | solution.py:36
  174.5 15.8 %collective-permute-start.25 = (bf16[4,192,384]{2,1,0:T(8,128)(2,1)}, bf16[4,192,384]{2,1,0:T(8,128)(2,1)S(1)}, u32[]{:S(2)}, u32[]{:S(2)}) collective-permute-start(bf16[4,192,384]{2,1,0:T(8,128)(2,1)} %get-tuple-element.193), channel_id=1, source_target_pairs={{0,2},{1,3},{2,0},{3,1},{4,6},{5,7},{6,4},{7,5},{8,10},{9,11},{10,... | collective-permute-start | bytes 1769480 | tf_op jit(solution)/shard_map/ppermute | solution.py:36
  175.8 15.3 %collective-permute-start.26 = (bf16[4,192,384]{2,1,0:T(8,128)(2,1)S(1)}, bf16[4,192,384]{2,1,0:T(8,128)(2,1)S(1)}, u32[]{:S(2)}, u32[]{:S(2)}) collective-permute-start(bf16[4,192,384]{2,1,0:T(8,128)(2,1)S(1)} %get-tuple-element.194), channel_id=1, source_target_pairs={{0,4},{1,5},{2,6},{3,7},{4,0},{5,1},{6,2},{7,3},{8,12},{9,13},{10,... | collective-permute-start | bytes 1769480 | tf_op jit(solution)/shard_map/ppermute | solution.py:36
  191.9 22.2 %collective-permute-start.28 = (bf16[4,192,384]{2,1,0:T(8,128)(2,1)}, bf16[4,192,384]{2,1,0:T(8,128)(2,1)}, u32[]{:S(2)}, u32[]{:S(2)}) collective-permute-start(bf16[4,192,384]{2,1,0:T(8,128)(2,1)} %get-tuple-element.212), channel_id=1, source_target_pairs={{0,6},{1,7},{2,4},{3,5},{4,2},{5,3},{6,0},{7,1},{8,14},{9,15},{10,... | collective-permute-start | bytes 1769480 | tf_op jit(solution)/shard_map/ppermute | solution.py:36
  216.6 22.8 %collective-permute-start.29 = (bf16[2,192,384]{2,1,0:T(8,128)(2,1)S(1)}, bf16[2,192,384]{2,1,0:T(8,128)(2,1)S(1)}, u32[]{:S(2)}, u32[]{:S(2)}) collective-permute-start(bf16[2,192,384]{2,1,0:T(8,128)(2,1)S(1)} %pad_maximum_fusion.2), channel_id=1, source_target_pairs={{0,16},{1,17},{2,18},{3,19},{4,20},{5,21},{6,22},{7,23},{8,24},{9,... | collective-permute-start | bytes 884744 | tf_op jit(solution)/shard_map/ppermute | solution.py:36
  220.2 31.7 %collective-permute-start.31 = (bf16[4,96,768]{2,1,0:T(8,128)(2,1)S(1)}, bf16[4,96,768]{2,1,0:T(8,128)(2,1)S(1)}, u32[]{:S(2)}, u32[]{:S(2)}) collective-permute-start(bf16[4,96,768]{2,1,0:T(8,128)(2,1)S(1)} %copy-done.17), channel_id=1, source_target_pairs={{0,2},{1,3},{2,0},{3,1},{4,6},{5,7},{6,4},{7,5},{8,10},{9,11},{10,... | collective-permute-start | bytes 1769480 | tf_op jit(solution)/shard_map/ppermute | solution.py:36
  221.5 30.4 %collective-permute-start.32 = (bf16[4,96,768]{2,1,0:T(8,128)(2,1)S(1)}, bf16[4,96,768]{2,1,0:T(8,128)(2,1)}, u32[]{:S(2)}, u32[]{:S(2)}) collective-permute-start(bf16[4,96,768]{2,1,0:T(8,128)(2,1)S(1)} %copy-done.16), channel_id=1, source_target_pairs={{0,4},{1,5},{2,6},{3,7},{4,0},{5,1},{6,2},{7,3},{8,12},{9,13},{10,... | collective-permute-start | bytes 1769480 | tf_op jit(solution)/shard_map/ppermute | solution.py:36
  222.3 29.6 %collective-permute-start.33 = (bf16[4,96,768]{2,1,0:T(8,128)(2,1)S(1)}, bf16[4,96,768]{2,1,0:T(8,128)(2,1)}, u32[]{:S(2)}, u32[]{:S(2)}) collective-permute-start(bf16[4,96,768]{2,1,0:T(8,128)(2,1)S(1)} %copy-done.15), channel_id=1, source_target_pairs={{0,6},{1,7},{2,4},{3,5},{4,2},{5,3},{6,0},{7,1},{8,14},{9,15},{10,... | collective-permute-start | bytes 1769480 | tf_op jit(solution)/shard_map/ppermute | solution.py:36
  260.3 21.6 %collective-permute-start.36 = (bf16[4,48,1664]{2,1,0:T(8,128)(2,1)}, bf16[4,48,1664]{2,1,0:T(8,128)(2,1)S(1)}, u32[]{:S(2)}, u32[]{:S(2)}) collective-permute-start(bf16[4,48,1664]{2,1,0:T(8,128)(2,1)} %get-tuple-element.246), channel_id=1, source_target_pairs={{0,2},{1,3},{2,0},{3,1},{4,6},{5,7},{6,4},{7,5},{8,10},{9,11},{10,... | collective-permute-start | bytes 1916936 | tf_op jit(solution)/shard_map/ppermute | solution.py:36
  261.6 28.5 %collective-permute-start.37 = (bf16[4,48,1664]{2,1,0:T(8,128)(2,1)}, bf16[4,48,1664]{2,1,0:T(8,128)(2,1)S(1)}, u32[]{:S(2)}, u32[]{:S(2)}) collective-permute-start(bf16[4,48,1664]{2,1,0:T(8,128)(2,1)} %get-tuple-element.247), channel_id=1, source_target_pairs={{0,4},{1,5},{2,6},{3,7},{4,0},{5,1},{6,2},{7,3},{8,12},{9,13},{10,... | collective-permute-start | bytes 1916936 | tf_op jit(solution)/shard_map/ppermute | solution.py:36
  262.5 29.2 %collective-permute-start.38 = (bf16[4,48,1664]{2,1,0:T(8,128)(2,1)}, bf16[4,48,1664]{2,1,0:T(8,128)(2,1)S(1)}, u32[]{:S(2)}, u32[]{:S(2)}) collective-permute-start(bf16[4,48,1664]{2,1,0:T(8,128)(2,1)} %get-tuple-element.248), channel_id=1, source_target_pairs={{0,6},{1,7},{2,4},{3,5},{4,2},{5,3},{6,0},{7,1},{8,14},{9,15},{10,... | collective-permute-start | bytes 1916936 | tf_op jit(solution)/shard_map/ppermute | solution.py:36
  264.6 15.7 %collective-permute-start.35 = (bf16[2,96,768]{2,1,0:T(8,128)(2,1)}, bf16[2,96,768]{2,1,0:T(8,128)(2,1)}, u32[]{:S(2)}, u32[]{:S(2)}) collective-permute-start(bf16[2,96,768]{2,1,0:T(8,128)(2,1)} %pad_maximum_fusion.3), channel_id=1, source_target_pairs={{0,16},{1,17},{2,18},{3,19},{4,20},{5,21},{6,22},{7,23},{8,24},{9,... | collective-permute-start | bytes 884744 | tf_op jit(solution)/shard_map/ppermute | solution.py:36
  281.8 14.6 %collective-permute-start.39 = (bf16[96,768]{1,0:T(8,128)(2,1)S(1)}, bf16[96,768]{1,0:T(8,128)(2,1)S(1)}, u32[]{:S(2)}, u32[]{:S(2)}) collective-permute-start(bf16[96,768]{1,0:T(8,128)(2,1)S(1)} %get-tuple-element.272), channel_id=1, source_target_pairs={{0,8},{1,9},{2,10},{3,11},{4,12},{5,13},{6,14},{7,15},{8,0},{9,1},... | collective-permute-start | bytes 442376 | tf_op jit(solution)/shard_map/ppermute | solution.py:36
  294.0 14.0 %collective-permute-start.41 = (bf16[48,1664]{1,0:T(8,128)(2,1)S(1)}, bf16[48,1664]{1,0:T(8,128)(2,1)S(1)}, u32[]{:S(2)}, u32[]{:S(2)}) collective-permute-start(bf16[48,1664]{1,0:T(8,128)(2,1)S(1)} %get-tuple-element.274), channel_id=1, source_target_pairs={{0,16},{1,17},{2,18},{3,19},{4,20},{5,21},{6,22},{7,23},{8,24},{9,... | collective-permute-start | bytes 479240 | tf_op jit(solution)/shard_map/ppermute | solution.py:36
  294.1 13.9 %collective-permute-start.42 = (bf16[48,1664]{1,0:T(8,128)(2,1)S(1)}, bf16[48,1664]{1,0:T(8,128)(2,1)S(1)}, u32[]{:S(2)}, u32[]{:S(2)}) collective-permute-start(bf16[48,1664]{1,0:T(8,128)(2,1)S(1)} %get-tuple-element.273), channel_id=1, source_target_pairs={{0,24},{1,25},{2,26},{3,27},{4,28},{5,29},{6,30},{7,31},{8,16},{9,... | collective-permute-start | bytes 479240 | tf_op jit(solution)/shard_map/ppermute | solution.py:36
  (54 other events, 389.1 us)
Sparse Core Ops, SparseCore 0:
  51.8 68.0 all-gather.2
where the time goes:
time: 323 us; the launch traced here: 318 us
  Pallas kernels  161 us (50%)
  waiting for transfers between devices  61.2 us (19%)
  starting transfers between devices  42.7 us (13%)
  other arithmetic  26.1 us (8%)
  between operations  14.9 us (5%)
  local copies, waits for them, and re-layouts  12.1 us (4%)
    ppermute x45, waiting for transfers between devices, send(): return lax.ppermute(values, ALL, pairs)  61.2 us
    ppermute x45, starting transfers between devices, send(): return lax.ppermute(values, ALL, pairs)  42.7 us
    pallas_call x2, Pallas kernels, attend_back(): pl.pallas_call(kernel, grid=(1,), in_specs=[pl.BlockSpec((length, 3 * D),...  26.8 us
    pallas_call x1, Pallas kernels, backward(): pl.pallas_call(backward_kernel, grid=(tokens // TILE,), in_specs=[tile(D)...  21 us
    pallas_call x1, Pallas kernels, outer_forward(): pl.pallas_call(functools.partial(outer_kernel, place), grid=(tokens // TI...  20.7 us
    pallas_call x1, Pallas kernels, attend(): pl.pallas_call(attend_kernel, grid=(rows,), in_specs=[tile(D, length), fi...  20.4 us
    pallas_call x1, Pallas kernels, inner_forward(): pl.pallas_call(inner_kernel, grid=(tokens // TILE,), in_specs=[tile(D)] *...  17.9 us
    pallas_call x1, Pallas kernels, grad_in(): pl.pallas_call(functools.partial(grad_in_kernel, place), grid=(FF // D,),...  10.9 us
  transfers between devices with their start and end apart: 46, of which 20 were waited for; matrix products, arithmetic and copies ran while one was open for 7% of the time, Pallas kernels for 43%

commit v1 on v0

v1 whole, which is shorter than its diff:
```python
import functools

import jax
import jax.numpy as jnp
from jax import lax
from jax.experimental import pallas as pl
from jax.experimental.pallas import tpu as pltpu
from jax.sharding import PartitionSpec as P

D = 768
HEADS = 12
FF = 3072
TILE = 256
ALL = ("wide", "narrow")
CHIP_STEPS = ((0, 0), (1, 0), (0, 1), (1, 1))
VMEM_LIMIT = 60 * 2**20
bf16, f32 = jnp.bfloat16, jnp.float32
Shape = jax.ShapeDtypeStruct

epsilon = 1e-06


def cost(us):
    return pl.CostEstimate(flops=0 * us, bytes_accessed=0, transcendentals=0)


def params():
    return pltpu.CompilerParams(vmem_limit_bytes=VMEM_LIMIT)


def send(values, z=0, y=0, x=0, core=0):
    flip_wide, flip_narrow = 2 * z + y, 2 * x + core
    pairs = [
        (w * 4 + n, (w ^ flip_wide) * 4 + (n ^ flip_narrow)) for w in range(8) for n in range(4)
    ]
    return lax.ppermute(values, ALL, pairs)


def position():
    wide, narrow = lax.axis_index("wide"), lax.axis_index("narrow")
    return wide // 2, wide % 2, narrow // 2, narrow % 2


def origin():
    zero = jnp.int32(0)
    return zero, zero, zero, zero


def gather_z(values):
    return [values] + [send(values, z=k) for k in (1, 2, 3)]


def gather_chips(lines):
    return [lines] + [send(lines, x=i, y=j) for i, j in CHIP_STEPS[1:]]


def gather_cores(blocks):
    return blocks + [send(block, core=1) for block in blocks]


def pair_kernel(count, *refs):
    core = lax.rem(lax.axis_index("narrow"), 2)
    more, outs = refs[2 * count : -count], refs[-count:]
    for own, other, out in zip(refs[:count], refs[count : 2 * count], outs):
        rows, columns = own.shape[0] // 2, own.shape[1]
        half = pl.ds(pl.multiple_of(core * rows, rows), rows)

        @pl.when(core == 0)
        def _(own=own, other=other, out=out, half=half, columns=columns):
            out[:, :columns] = own[half, :]
            out[:, columns : 2 * columns] = other[half, :]

        @pl.when(core == 1)
        def _(own=own, other=other, out=out, half=half, columns=columns):
            out[:, :columns] = other[half, :]
            out[:, columns : 2 * columns] = own[half, :]

    for vector in more:
        rest, parts = vector[...], []
        for _ in range(3):
            parts.append(rest.astype(bf16).astype(f32))
            rest = rest - parts[-1]
        outs[0][:, 1152:] = rows_of(48, *parts).astype(bf16)


def pair_up(pieces, others, vectors=None):
    more = [0] * len(pieces)
    rows = ()
    if vectors is not None:
        rows = (jnp.pad(vectors, (0, 384 - vectors.shape[0])).reshape(3, 128),)
        more[0] = 128
    return pl.pallas_call(
        functools.partial(pair_kernel, len(pieces)),
        out_shape=[
            Shape((piece.shape[0] // 2, piece.shape[1] * 2 + extra), piece.dtype)
            for piece, extra in zip(pieces, more)
        ],
        cost_estimate=cost(2),
        name="pair_up",
    )(*pieces, *others, *rows)


def block_copies(place, blocks, left, out, sems):
    z, y, x, core = place()
    rows, width = blocks[0].shape[1], out.shape[1] // 2
    copies = []
    for other in range(2):
        for step, (i, j) in enumerate(CHIP_STEPS):
            for k in range(4):
                row = (((z ^ k) * 2 + (y ^ j)) * 2 + (core ^ other)) * rows
                copies.append(
                    pltpu.make_async_copy(
                        blocks[other * 4 + step].at[k, :, pl.ds(left, width)],
                        out.at[
                            pl.ds(pl.multiple_of(row, rows), rows),
                            pl.ds(pl.multiple_of((x ^ i) * width, width), width),
                        ],
                        sems.at[len(copies)],
                    )
                )
    return copies


def table_copies(table, out, sems):
    rows, columns = table.shape[1:]
    return [
        pltpu.make_async_copy(
            table.at[w * 4 + n],
            out.at[pl.ds((w * 2 + n % 2) * rows, rows), pl.ds(n // 2 * columns, columns)],
            sems.at[w * 4 + n],
        )
        for w in range(8)
        for n in range(4)
    ]


def start(copies):
    for copy in copies:
        copy.start()


def wait(copies):
    for copy in copies:
        copy.wait()


def anywhere(count):
    return [pl.BlockSpec(memory_space=pl.ANY)] * count


def split_blocks(matrix, rows, columns):
    parts = matrix.reshape(4, 2, 2, rows, 2, columns).transpose(2, 1, 4, 0, 3, 5)
    return [parts[other, j, i] for other in range(2) for i, j in CHIP_STEPS]


def place_kernel(*refs):
    z, y, x, core = position()
    out = refs[8]
    for other in range(2):
        for step, (i, j) in enumerate(CHIP_STEPS):
            for k in range(4):
                row = ((z ^ k) * 2 + (y ^ j)) * 4 + (x ^ i) * 2 + (core ^ other)
                parts = refs[other * 4 + step][k].astype(f32)
                out[row] = parts[:3] + parts[3:6] + parts[6:9]


def place_vectors(blocks):
    table = pl.pallas_call(
        place_kernel,
        grid=(1,),
        in_specs=[pl.BlockSpec((4, 16, 128), lambda i: (0, 0, 9))] * 8,
        out_specs=fixed((32, 3, 128)),
        out_shape=Shape((32, 3, 128), f32),
        cost_estimate=cost(1),
        name="place_vectors",
    )(*blocks)
    return table.reshape(32, 384)[:, :288].reshape(12, D)


def wide_sum(*terms):
    return functools.reduce(lambda a, b: a + b, [t.astype(f32) for t in terms])


def chip_parts(kept, received):
    return [wide_sum(kept[s], received[s]).astype(bf16) for s in range(4)]


def chip_kernel(*refs):
    for kept, received, out in zip(refs[:4], refs[4:8], refs[8:]):
        out[...] = wide_sum(kept[...], received[...]).astype(bf16)


def chip_parts_of(kept, received):
    rows, columns = kept[0].shape[1:]
    line = pl.BlockSpec((1, rows, columns), lambda k: (k, 0, 0))
    return pl.pallas_call(
        chip_kernel,
        grid=(4,),
        in_specs=[line] * 8,
        out_specs=[line] * 4,
        out_shape=[Shape((4, rows, columns), bf16)] * 4,
        compiler_params=params(),
        cost_estimate=cost(3),
        name="chip_parts",
    )(*kept, *received)


def chip_sends(parts):
    return [send(parts[s], x=i, y=j) for s, (i, j) in enumerate(CHIP_STEPS) if s]


def line_kernel(far, *refs):
    terms, outs = refs[:4], refs[4:]
    for k in range(4):
        total = wide_sum(*[term[k] for term in terms]).astype(bf16)
        if far and k >= 2:
            outs[2][k - 2] = total
        else:
            outs[k][...] = total


def line_parts(own, others, far=False):
    piece = Shape(own.shape[1:], bf16)
    shapes = [piece] * 2 + [Shape((2,) + own.shape[1:], bf16)] if far else [piece] * 4
    return pl.pallas_call(
        functools.partial(line_kernel, far),
        out_shape=shapes,
        compiler_params=params(),
        cost_estimate=cost(2),
        name="line_parts",
    )(own, *others)


def line_sends(line):
    return [send(line[k], z=k) for k in (1, 2, 3)]


def line_halves(own, others):
    *near, far = line_parts(own, others, True)
    return near, far


def near_parts(near, received):
    return [wide_sum(near[k], received[k]).astype(near[k].dtype) for k in range(2)]


def swap_columns(summed):
    core = lax.axis_index("narrow") % 2
    columns = summed.shape[1] // 2
    left, right = summed[:, :columns], summed[:, columns:]
    mine = jnp.where(core == 0, left, right)
    other = send(jnp.where(core == 0, right, left).astype(bf16), core=1).astype(f32)
    return jnp.concatenate(
        [jnp.where(core == 0, mine, other), jnp.where(core == 0, other, mine)], 0
    )


def dot(left_side, right_side):
    return jnp.dot(left_side, right_side, preferred_element_type=f32)


def dot_t(left_side, right_side):
    return lax.dot_general(
        left_side, right_side, (((1,), (1,)), ((), ())), preferred_element_type=f32
    )


def column_sum(values):
    return jnp.sum(values, 0, keepdims=True)


def normalize(values):
    center = values - jnp.mean(values, -1, keepdims=True)
    inverse = lax.rsqrt(jnp.mean(center * center, -1, keepdims=True) + epsilon)
    return center * inverse, inverse


def normalize_back(grad_norm, normed, inverse):
    return inverse * (
        grad_norm
        - jnp.mean(grad_norm, -1, keepdims=True)
        - normed * jnp.mean(grad_norm * normed, -1, keepdims=True)
    )


def smooth(values):
    density = jnp.exp(-0.5 * values * values) * 0.3989422804014327
    below = 0.5 + 0.5 * lax.erf(values * 0.7071067811865476)
    return values * below, below + values * density


def fixed(shape):
    return pl.BlockSpec(shape, lambda i: (0,) * len(shape))


def tile(columns, rows=TILE):
    return pl.BlockSpec((rows, columns), lambda i: (i, 0))


def rows_of(count, *parts):
    missing = count - sum(part.shape[0] for part in parts)
    return jnp.concatenate(list(parts) + [jnp.zeros((missing, parts[0].shape[1]), f32)], 0)


def segment_marks(segment):
    kinds = lax.broadcasted_iota(jnp.int32, (1, 64), 1)
    mark = (segment.reshape(-1, 1) == kinds).astype(bf16)
    tall = lax.broadcasted_iota(jnp.int32, (1, 64, 1), 1)
    away = (segment[:, None, :] != tall) & (tall < 4)
    return jnp.concatenate([mark, mark], 1), jnp.where(away, -(2.0**30), 0.0).astype(bf16)


def attend_kernel(place, *refs):
    hidden, vectors, key_marks, query_marks = refs[:4]
    blocks, (packed, att, att_t, probs, weight, sems) = refs[4:12], refs[12:]

    @pl.when(pl.program_id(0) == 0)
    def _():
        copies = block_copies(place, blocks, 0, weight, sems)
        start(copies)
        wait(copies)

    length = hidden.shape[0]
    for part in range(3):
        columns = slice(part * D, (part + 1) * D)
        block = dot(hidden[...], weight[:, columns])
        if part != 1:
            block = block + vectors[part // 2 : part // 2 + 1, :]
        block = block.astype(bf16)
        if part == 0:
            block = block * jnp.asarray(0.125, bf16)
        packed[:, columns] = block
    lanes = lax.broadcasted_iota(jnp.int32, (length, 128), 1)

    def pair(p, _):
        at = pl.multiple_of(p * 128, 128)
        q_t = packed[:, pl.ds(at, 128)].T
        k = packed[:, pl.ds(D + at, 128)]
        v_t = packed[:, pl.ds(2 * D + at, 128)].T
        scores = []
        for odd in range(2):
            keys = jnp.where((lanes >= 64) == bool(odd), k, key_marks[...])
            own = q_t[64 * odd : 64 * odd + 64]
            marks = query_marks[0]
            scores.append(dot(keys, jnp.concatenate([marks, own] if odd else [own, marks], 0)))
        outs = []
        for odd in range(2):
            weights = jnp.exp(scores[odd] - jnp.max(scores[odd], 0, keepdims=True))
            low = (weights * (1.0 / column_sum(weights))).astype(bf16)
            probs[p * 2 + odd] = low
            outs.append(dot(v_t[64 * odd : 64 * odd + 64], low))
        out = jnp.concatenate(outs, 0).astype(bf16)
        att_t[pl.ds(at, 128), :] = out
        att[:, pl.ds(at, 128)] = out.T
        return 0

    lax.fori_loop(0, HEADS // 2, pair, 0, unroll=True)


def attend(place, hidden, vectors, key_marks, query_marks, blocks):
    rows, length = query_marks.shape[0], query_marks.shape[2]
    tokens = rows * length
    return pl.pallas_call(
        functools.partial(attend_kernel, place),
        grid=(rows,),
        in_specs=[
            tile(D, length),
            fixed((12, D)),
            tile(128, length),
            pl.BlockSpec((1, 64, length), lambda i: (i, 0, 0)),
        ]
        + anywhere(8),
        scratch_shapes=[pltpu.VMEM((D, 3 * D), bf16), pltpu.SemaphoreType.DMA((32,))],
        out_specs=[
            tile(3 * D, length),
            tile(D, length),
            pl.BlockSpec((D, length), lambda i: (0, i)),
            pl.BlockSpec((HEADS, length, length), lambda i: (i, 0, 0)),
        ],
        out_shape=[
            Shape((tokens, 3 * D), bf16),
            Shape((tokens, D), bf16),
            Shape((D, tokens), bf16),
            Shape((rows * HEADS, length, length), bf16),
        ],
        compiler_params=params(),
        cost_estimate=cost(20),
        name="attend",
    )(hidden, vectors, key_marks, query_marks, *blocks)


def inner_kernel(place, *refs):
    att, hidden, vectors = refs[:3]
    blocks, (first_low, normed, inverse, activated, slope) = refs[3:11], refs[11:16]
    w_in, w_out, in_sems, out_sems = refs[16:]
    first_step = pl.program_id(0) == 0

    def row(i):
        return vectors[i : i + 1, :]

    def copies_in():
        return block_copies(place, blocks, 0, w_in, in_sems)

    @pl.when(first_step)
    def _():
        copies = block_copies(place, blocks, 1536, w_out, out_sems)
        start(copies)
        start(copies_in())
        wait(copies)

    n1, r1 = normalize(hidden[...].astype(f32) + dot(att[...], w_out[...]) + row(2))
    low = (n1 * row(3) + row(4)).astype(bf16)
    first_low[...] = low
    normed[...] = n1
    inverse[...] = jnp.broadcast_to(r1, inverse.shape)

    @pl.when(first_step)
    def _():
        wait(copies_in())

    for c in range(FF // D):
        columns = slice(c * D, c * D + D)
        act, back = smooth(dot(low, w_in[:, columns]) + row(5 + c))
        activated[:, columns] = act.astype(bf16)
        slope[:, columns] = back.astype(bf16)


def inner_forward(place, att, hidden, vectors, blocks):
    tokens = hidden.shape[0]
    return pl.pallas_call(
        functools.partial(inner_kernel, place),
        grid=(tokens // TILE,),
        in_specs=[tile(D)] * 2 + [fixed((12, D))] + anywhere(8),
        out_specs=[tile(D), tile(D), tile(128), tile(FF), tile(FF)],
        out_shape=[
            Shape((tokens, D), bf16),
            Shape((tokens, D), f32),
            Shape((tokens, 128), f32),
            Shape((tokens, FF), bf16),
            Shape((tokens, FF), bf16),
        ],
        scratch_shapes=[
            pltpu.VMEM((D, FF), bf16),
            pltpu.VMEM((D, D), bf16),
            pltpu.SemaphoreType.DMA((32,)),
            pltpu.SemaphoreType.DMA((32,)),
        ],
        compiler_params=params(),
        cost_estimate=cost(16),
        name="inner_forward",
    )(att, hidden, vectors, *blocks)


def outer_kernel(place, *refs):
    act, normed, cotangent, vectors, back_table = refs[:5]
    output, grad_second, sums, kept, sent, w_back, activated, grad_t, sems = refs[5:]
    step = pl.program_id(0)
    z, y, x, core = place()

    def row(i):
        return vectors[i : i + 1, :]

    @pl.when(step == 0)
    def _():
        copies = table_copies(back_table, w_back, sems)
        start(copies)
        wait(copies)

    here = pl.ds(pl.multiple_of(step * TILE, TILE), TILE)
    activated[here, :] = act[...]
    outward = normed[...] * row(3) + row(4) + dot(act[...], w_back[...]) + row(9)
    n2, r2 = normalize(outward)
    output[...] = (n2 * row(10) + row(11)).astype(bf16)
    cot = cotangent[...].astype(f32)
    g2 = normalize_back(cot * row(10), n2, r2)
    grad_second[...] = g2
    part = rows_of(8, column_sum(g2), column_sum(cot * n2), column_sum(cot))

    @pl.when(step == 0)
    def _():
        sums[...] = part

    @pl.when(step > 0)
    def _():
        sums[...] += part

    g2_t = g2.astype(bf16).T
    for n in range(4):
        at = ((n % 2) ^ core) * 2 + ((n // 2) ^ x)
        piece = g2_t[n * 192 : n * 192 + 192]
        grad_t[pl.ds(pl.multiple_of(at * 192, 192), 192), here] = piece

    @pl.when(step == pl.num_programs(0) - 1)
    def _():
        for k in range(4):
            columns = pl.ds(pl.multiple_of((z ^ k) * D, D), D)
            res = dot(grad_t[...], activated[:, columns]).astype(bf16)
            for other, out in enumerate((kept, sent)):
                for i in range(2):
                    at = (other * 2 + i) * 192
                    for half in range(2):
                        piece = res[at : at + 192, half * 384 : half * 384 + 384]
                        out[i + 2 * (half ^ y), k] = piece


def outer_forward(place, activated, normed, cotangent, vectors, back_table):
    tokens = normed.shape[0]
    return pl.pallas_call(
        functools.partial(outer_kernel, place),
        grid=(tokens // TILE,),
        in_specs=[tile(FF), tile(D), tile(D), fixed((12, D))] + anywhere(1),
        out_specs=[tile(D), tile(D), fixed((8, D))] + [fixed((4, 4, 192, 384))] * 2,
        out_shape=[
            Shape((tokens, D), bf16),
            Shape((tokens, D), f32),
            Shape((8, D), f32),
        ]
        + [Shape((4, 4, 192, 384), bf16)] * 2,
        scratch_shapes=[
            pltpu.VMEM((FF, D), bf16),
            pltpu.VMEM((tokens, FF), bf16),
            pltpu.VMEM((D, tokens), bf16),
            pltpu.SemaphoreType.DMA((32,)),
        ],
        compiler_params=params(),
        cost_estimate=cost(18),
        name="outer_forward",
    )(activated, normed, cotangent, vectors, back_table)


def backward_kernel(place, *refs):
    grad_second, slope, normed, inverse, first_low, att_t, vectors = refs[:7]
    blocks, back_table = refs[7:15], refs[15]
    grad_att, grad_branch, sums, sums_inner, kept, sent = refs[16:22]
    w_in, w_out, w_back, inner_low, first_t, grad_low, turned = refs[22:29]
    in_sems, out_sems, back_sems = refs[29:]
    step = pl.program_id(0)
    z, y, x, core = place()
    here = pl.ds(pl.multiple_of(step * TILE, TILE), TILE)

    def compute(first_step):
        if first_step:
            copies_back = table_copies(back_table, w_back, back_sems)
            copies_in = block_copies(place, blocks, 0, w_in, in_sems)
            copies_out = block_copies(place, blocks, 1536, w_out, out_sems)
            start(copies_back)
            start(copies_in)
            start(copies_out)
        g2 = grad_second[...]
        g2_low = g2.astype(bf16)
        grad_first = g2
        inner_sums = []
        for c in range(FF // D):
            columns = slice(c * D, c * D + D)
            if first_step:
                wait(copies_back[c * 8 : c * 8 + 8])
            gi = dot_t(g2_low, w_back[columns, :]) * slope[:, columns].astype(f32)
            inner_sums.append(column_sum(gi))
            gi = gi.astype(bf16)
            inner_low[here, columns] = gi
            if first_step and c == 0:
                wait(copies_in)
            grad_first = grad_first + dot_t(gi, w_in[:, columns])
        n1 = normed[...]
        g1 = normalize_back(grad_first * vectors[3:4, :], n1, inverse[:, :1])
        grad_branch[...] = g1
        g1_low = g1.astype(bf16)
        grad_low[here, :] = g1_low
        if first_step:
            wait(copies_out)
        grad_att[...] = dot_t(g1_low, w_out[...]).astype(bf16)
        part = rows_of(8, column_sum(g1), column_sum(grad_first * n1), column_sum(grad_first))
        part_inner = rows_of(8, *inner_sums)
        if first_step:
            sums[...] = part
            sums_inner[...] = part_inner
        else:
            sums[...] += part
            sums_inner[...] += part_inner
        low_t = first_low[...].T
        for w in range(8):
            at = ((w % 2) ^ y) * 4 + ((w // 2) ^ z)
            piece = low_t[w * 96 : w * 96 + 96]
            first_t[pl.ds(pl.multiple_of(at * 96, 96), 96), here] = piece
        turn_rows(place, att_t, turned, here)

    @pl.when(step == 0)
    def _():
        compute(True)

    @pl.when(step > 0)
    def _():
        compute(False)

    @pl.when(step == pl.num_programs(0) - 1)
    def _():
        for i in range(2):
            for other, out in enumerate((kept, sent)):
                at = ((x ^ i) * 2 + (core ^ other)) * D
                res = dot(first_t[...], inner_low[:, pl.ds(pl.multiple_of(at, D), D)])
                res = res.astype(bf16)
                for j in range(2):
                    for k in range(4):
                        at = (j * 4 + k) * 96
                        out[i + 2 * j, k, :, :D] = res[at : at + 48]
                        out[i + 2 * j, k, :, D : 2 * D] = res[at + 48 : at + 96]
        res = dot(turned[...], grad_low[...]).astype(bf16)
        for other, out in enumerate((kept, sent)):
            for j in range(2):
                for k in range(4):
                    at = (other * 8 + j * 4 + k) * 48
                    for half in range(2):
                        piece = res[at : at + 48, half * 384 : half * 384 + 384]
                        out[(half ^ x) + 2 * j, k, :, 2 * D :] = piece


def backward(place, grad_second, slope, normed, inverse, first_low, att_t, vectors, *weights):
    blocks, back_table = weights
    tokens = normed.shape[0]
    outs = [(4, 4, 48, 1920)] * 2
    return pl.pallas_call(
        functools.partial(backward_kernel, place),
        grid=(tokens // TILE,),
        in_specs=[tile(D), tile(FF), tile(D), tile(128), tile(D)]
        + [pl.BlockSpec((D, TILE), lambda i: (0, i)), fixed((12, D))]
        + anywhere(9),
        out_specs=[tile(D), tile(D)] + [fixed(s) for s in [(8, D)] * 2 + outs],
        out_shape=[Shape((tokens, D), bf16), Shape((tokens, D), f32)]
        + [Shape((8, D), f32)] * 2
        + [Shape(s, bf16) for s in outs],
        scratch_shapes=[
            pltpu.VMEM((D, FF), bf16),
            pltpu.VMEM((D, D), bf16),
            pltpu.VMEM((FF, D), bf16),
            pltpu.VMEM((tokens, FF), bf16),
            pltpu.VMEM((D, tokens), bf16),
            pltpu.VMEM((tokens, D), bf16),
            pltpu.VMEM((D, tokens), bf16),
        ]
        + [pltpu.SemaphoreType.DMA((32,))] * 3,
        compiler_params=params(),
        cost_estimate=cost(22),
        name="backward",
    )(grad_second, slope, normed, inverse, first_low, att_t, vectors, *blocks, back_table)


def turn_rows(place, source, turned, columns=slice(None)):
    z, y, _, core = place()
    for w in range(8):
        for half in range(2):
            at = (half ^ core) * 8 + ((w % 2) ^ y) * 4 + ((w // 2) ^ z)
            piece = (w * 2 + half) * 48
            rows = pl.ds(pl.multiple_of(at * 48, 48), 48)
            turned[rows, columns] = source[piece : piece + 48, :]


def attend_back_kernel(packed, grad_att, probs, grad_low, sums):
    length = packed.shape[0]
    lanes = lax.broadcasted_iota(jnp.int32, (length, 128), 1)
    zero = jnp.zeros((length, 128), bf16)
    blank = jnp.zeros((64, length), bf16)

    def pair(p, _):
        at = pl.multiple_of(p * 128, 128)
        q = packed[:, pl.ds(at, 128)]
        k_t = packed[:, pl.ds(D + at, 128)].T
        v = packed[:, pl.ds(2 * D + at, 128)]
        g = grad_att[:, pl.ds(at, 128)]
        g_t = g.T
        grad_probs = []
        for odd in range(2):
            own = g_t[64 * odd : 64 * odd + 64]
            grad_probs.append(dot(v, jnp.concatenate([blank, own] if odd else [own, blank], 0)))
        dk = dv = 0.0
        dq_t = []
        for odd in range(2):
            mine = (lanes >= 64) == bool(odd)
            low = probs[p * 2 + odd]
            wide = low.astype(f32)
            gp = grad_probs[odd]
            ds = (wide * (gp - column_sum(wide * gp))).astype(bf16)
            dv = dv + dot(low, jnp.where(mine, g, zero))
            dk = dk + dot(ds, jnp.where(mine, q, zero))
            dq_t.append(dot(k_t[64 * odd : 64 * odd + 64], ds))
        dq = jnp.concatenate(dq_t, 0).T * 0.125
        sums[0, :, pl.ds(at, 128)] = rows_of(8, column_sum(dq), column_sum(dv))
        grad_low[:, pl.ds(at, 128)] = dq.astype(bf16)
        grad_low[:, pl.ds(D + at, 128)] = dk.astype(bf16)
        grad_low[:, pl.ds(2 * D + at, 128)] = dv.astype(bf16)
        return 0

    lax.fori_loop(0, HEADS // 2, pair, 0, unroll=True)


def attend_back(row, packed, grad_att, probs, low=None):
    length = probs.shape[1]
    kernel, more, specs, alias = attend_back_kernel, (), [], {}
    if low is not None:
        more, specs, alias = (low,), [pl.BlockSpec(memory_space=pl.ANY)], {3: 0}

        def kernel(packed, grad_att, probs, low, grad_low, sums):
            attend_back_kernel(packed, grad_att, probs, grad_low, sums)

    return pl.pallas_call(
        kernel,
        grid=(1,),
        in_specs=[
            pl.BlockSpec((length, 3 * D), lambda i: (row, 0)),
            pl.BlockSpec((length, D), lambda i: (row, 0)),
            pl.BlockSpec((HEADS, length, length), lambda i: (row, 0, 0)),
        ]
        + specs,
        out_specs=[
            pl.BlockSpec((length, 3 * D), lambda i: (row, 0)),
            pl.BlockSpec((1, 8, D), lambda i: (0, 0, 0)),
        ],
        out_shape=[Shape(packed.shape, bf16), Shape((1, 8, D), f32)],
        input_output_aliases=alias,
        compiler_params=params(),
        cost_estimate=cost(12),
        name="attend_back",
    )(packed, grad_att, probs, *more)


def grad_qkv_kernel(place, hidden, low, *refs):
    sums_zero, sums_one, sums_first, sums_inner, sums_second = refs[:5]
    outs, turned, groups = refs[5:13], refs[13], refs[14]
    z, y, x, core = place()
    turn_rows(place, hidden[...].T, turned)
    rows = [sums_zero[0, i : i + 1, :] + sums_one[0, i : i + 1, :] for i in range(2)]
    rows += [sums_first[i : i + 1, :] for i in range(3)]
    rows += [sums_inner[i : i + 1, :] for i in range(4)]
    rows += [sums_second[i : i + 1, :] for i in range(3)]
    for group in range(72):
        column = group % 6 * 128
        groups[group] = rows[group // 6][:, column : column + 128]
    for group in range(72, 76):
        groups[group] = jnp.zeros((1, 128), f32)
    for i in range(2):
        columns = pl.ds(pl.multiple_of((x ^ i) * 1152, 128), 1152)
        res = dot(turned[...], low[:, columns]).astype(bf16)
        for other in range(2):
            for j in range(2):
                out = outs[other * 4 + i + 2 * j]
                for k in range(4):
                    at = (other * 8 + j * 4 + k) * 48
                    out[k, :, :1152] = res[at : at + 48]
                    device = ((z ^ k) * 2 + (y ^ j)) * 4 + (x ^ i) * 2 + (core ^ other)
                    group = (9 * device) // 4
                    part = jnp.concatenate([groups[group + q] for q in range(4)], 0)
                    out[k, :16, 1152:] = rows_of(16, part).astype(bf16)
                    out[k, 16:, 1152:] = jnp.zeros((32, 128), bf16)


def grad_qkv(place, hidden, low, *sums):
    return pl.pallas_call(
        functools.partial(grad_qkv_kernel, place),
        out_shape=[Shape((4, 48, 1280), bf16)] * 8,
        scratch_shapes=[pltpu.VMEM((D, hidden.shape[0]), bf16), pltpu.VMEM((80, 1, 128), f32)],
        compiler_params=params(),
        cost_estimate=cost(9),
        name="grad_qkv",
    )(hidden, low, *sums)


def cut_vectors(place, groups):
    z, y, x, core = place()
    at = (((z * 2 + y) * 4 + x * 2 + core) * 288) % 128
    return lax.dynamic_slice(groups.reshape(-1), (at,), (288,))


def hidden_kernel(place, *refs):
    low, grad_branch, blocks, out, weight, sems = *refs[:2], refs[2:10], *refs[10:]

    @pl.when(pl.program_id(0) == 0)
    def _():
        copies = block_copies(place, blocks, 0, weight, sems)
        start(copies)
        wait(copies)

    out[...] = grad_branch[...] + dot_t(low[...], weight[...])


def grad_of_hidden(place, low, grad_branch, blocks):
    tokens = low.shape[0]
    return pl.pallas_call(
        functools.partial(hidden_kernel, place),
        grid=(tokens // TILE,),
        in_specs=[tile(3 * D), tile(D)] + anywhere(8),
        out_specs=tile(D),
        out_shape=Shape((tokens, D), f32),
        scratch_shapes=[pltpu.VMEM((D, 3 * D), bf16), pltpu.SemaphoreType.DMA((32,))],
        compiler_params=params(),
        cost_estimate=cost(9),
        name="grad_hidden",
    )(low, grad_branch, *blocks)


def gather_plain(w_qkv, w_out, w_in, w_back, vectors):
    def whole(piece):
        return lax.all_gather(
            lax.all_gather(piece, "narrow", axis=1, tiled=True), "wide", axis=0, tiled=True
        )

    full = tuple(whole(piece) for piece in (w_qkv, w_out, w_in, w_back))
    return full + (lax.all_gather(vectors, ALL, axis=0, tiled=True).reshape(12, D),)


def tie(*values):
    return lax.optimization_barrier(values)


def unfold(table, order, shape):
    return table.reshape((2, 2, 2, 4) + table.shape[3:]).transpose(order).reshape(shape)


def scatter_whole(matrix):
    part = lax.psum_scatter(matrix, "wide", scatter_dimension=0, tiled=True)
    part = lax.psum_scatter(part, "narrow", scatter_dimension=1, tiled=True)
    return part.astype(f32)


def per_device(hidden, segment, w_qkv, w_out, w_in, w_back, vectors, cotangent):
    (qkv,) = pair_up([w_qkv], [send(w_qkv, core=1)], vectors)
    rest = [w_out, w_in, w_back]
    other_rest = [send(piece, core=1) for piece in rest]
    qkv, other_rest, segment = tie(qkv, other_rest, segment)
    key_marks, query_marks = segment_marks(segment)
    qkv_line = gather_z(qkv)
    out, inner, back = pair_up(rest, other_rest)
    mid = jnp.concatenate([inner, out], 1)
    qkv_line, mid, back, key_marks, query_marks = tie(
        jnp.stack(qkv_line), mid, back, key_marks, query_marks
    )

    qkv_blocks = gather_chips(qkv_line)
    mid_line = gather_z(mid)
    qkv_blocks, mid_line, back = tie(qkv_blocks, mid_line, back)

    back_table = lax.all_gather(back, ALL, axis=0, tiled=False)
    mid_blocks = gather_chips(jnp.stack(mid_line))
    qkv_blocks = gather_cores(qkv_blocks)
    all_vectors = place_vectors(qkv_blocks)
    attended = attend(position, hidden, all_vectors, key_marks, query_marks, qkv_blocks)
    attended, mid_blocks = tie(attended, mid_blocks)
    packed, att, att_t, probs = attended

    mid_blocks = gather_cores(mid_blocks)
    inner_outs = inner_forward(position, att, hidden, all_vectors, mid_blocks)
    inner_outs, back_table = tie(inner_outs, back_table)
    first_low, normed, inverse, activated, slope = inner_outs

    output, grad_second, sums_second, kept_back, sent_back = outer_forward(
        position, activated, normed, cotangent, all_vectors, back_table
    )

    received_back = send(sent_back, core=1)
    back_outs = backward(
        position,
        grad_second,
        slope,
        normed,
        inverse,
        first_low,
        att_t,
        all_vectors,
        mid_blocks,
        back_table,
    )
    back_outs, received_back = tie(back_outs, received_back)
    grad_att, grad_branch, sums_first, sums_inner, kept_mid, sent_mid = back_outs

    received_mid = send(sent_mid, core=1)
    parts_back = chip_parts(kept_back, received_back)
    parts_back, received_mid = tie(parts_back, received_mid)

    others_back = chip_sends(parts_back)
    parts_mid = chip_parts(kept_mid, received_mid)
    parts_mid, grad_att = tie(parts_mid, grad_att)
    plane_mid = [send(parts_mid[1], x=1), send(parts_mid[2], y=1)]
    packed_low, sums_zero = attend_back(0, packed, grad_att, probs)
    packed_low, sums_one = attend_back(1, packed, grad_att, probs, packed_low)
    packed_low, sums_one, others_back, corner_mid = tie(
        packed_low, sums_one, others_back, parts_mid[3]
    )

    near_back, far_back = line_halves(parts_back[0], others_back)
    near_back, far_back, corner_mid, packed_low = tie(near_back, far_back, corner_mid, packed_low)
    corner_mid = send(corner_mid, x=1, y=1)
    far_back = send(far_back, z=2)
    tables_qkv = grad_qkv(
        position, hidden, packed_low, sums_zero, sums_one, sums_first, sums_inner, sums_second
    )
    tables_qkv, far_back, plane_mid = tie(tables_qkv, far_back, plane_mid)
    kept_qkv, sent_qkv = tables_qkv[:4], tables_qkv[4:]

    received_qkv = [send(block, core=1) for block in sent_qkv]
    parts_qkv = chip_parts_of(kept_qkv, received_qkv)
    parts_qkv, grad_branch, near_back, corner_mid = tie(
        parts_qkv, grad_branch, near_back, corner_mid
    )
    others_qkv = chip_sends(parts_qkv)
    near_mid, far_mid = line_halves(parts_mid[0], plane_mid + [corner_mid])
    far_mid = send(far_mid, z=2)
    near_back = near_parts(near_back, far_back)
    next_back = send(near_back[1], z=1)
    near_back, grad_branch = tie(near_back, grad_branch)
    grad_hidden = grad_of_hidden(position, packed_low, grad_branch, qkv_blocks)
    grad_hidden, far_mid, next_back = tie(grad_hidden, far_mid, next_back)

    own_back = wide_sum(near_back[0], next_back).T
    near_mid = near_parts(near_mid, far_mid)
    next_mid = send(near_mid[1], z=1)
    others_qkv, near_mid = tie(others_qkv, near_mid)
    line_qkv = line_parts(parts_qkv[0], others_qkv)
    lines_qkv = line_sends(line_qkv)
    own_mid = wide_sum(near_mid[0], next_mid)
    own_in = jnp.concatenate([own_mid[:, :D], own_mid[:, D : 2 * D]], 0)
    own_out = swap_columns(own_mid[:, 2 * D :])
    own_in, own_out, own_back, lines_qkv = tie(own_in, own_out, own_back, lines_qkv)
    own_qkv = wide_sum(line_qkv[0], *lines_qkv)
    own_vectors = cut_vectors(position, own_qkv[:4, 1152:])
    own_qkv = swap_columns(own_qkv[:, :1152])
    return (output, grad_hidden, own_qkv, own_out, own_in, own_back, own_vectors)


def per_device_plain(hidden, segment, w_qkv, w_out, w_in, w_back, vectors, cotangent):
    key_marks, query_marks = segment_marks(segment)
    full_qkv, full_out, full_in, full_back, all_vectors = gather_plain(
        w_qkv, w_out, w_in, w_back, vectors
    )
    qkv_blocks = split_blocks(full_qkv, 48, 1152)
    mid_blocks = [
        jnp.concatenate(pair, 2)
        for pair in zip(split_blocks(full_in, 48, 1536), split_blocks(full_out, 48, 384))
    ]
    back_pieces = full_back.reshape(8, 2, 192, 2, 384).transpose(0, 3, 1, 2, 4)
    back_pieces = back_pieces.reshape(32, 192, 384)
    packed, att, att_t, probs = attend(
        origin, hidden, all_vectors, key_marks, query_marks, qkv_blocks
    )
    first_low, normed, inverse, activated, slope = inner_forward(
        origin, att, hidden, all_vectors, mid_blocks
    )
    output, grad_second, sums_second, *back_table = outer_forward(
        origin, activated, normed, cotangent, all_vectors, back_pieces
    )
    grad_att, grad_branch, sums_first, sums_inner, *tables = backward(
        origin,
        grad_second,
        slope,
        normed,
        inverse,
        first_low,
        att_t,
        all_vectors,
        mid_blocks,
        back_pieces,
    )
    mid_table = jnp.stack(tables)
    packed_low, sums_zero = attend_back(0, packed, grad_att, probs)
    packed_low, sums_one = attend_back(1, packed, grad_att, probs, packed_low)
    grad_hidden = grad_of_hidden(origin, packed_low, grad_branch, qkv_blocks)
    tables = grad_qkv(
        origin, hidden, packed_low, sums_zero, sums_one, sums_first, sums_inner, sums_second
    )
    grad_vectors = jnp.concatenate(
        [(sums_zero + sums_one)[0, :2], sums_first[:3], sums_inner[:4], sums_second[:3]], 0
    )
    qkv_table = jnp.stack(tables)
    qkv_table = qkv_table.reshape(2, 4, 4, 48, 1280)
    halves = jnp.stack([mid_table[..., :D], mid_table[..., D : 2 * D]], 4)
    own_qkv = scatter_whole(unfold(qkv_table[..., :1152], (3, 1, 0, 4, 2, 5), (D, 3 * D)))
    own_out = scatter_whole(unfold(mid_table[..., 2 * D :], (3, 1, 0, 4, 2, 5), (D, D)))
    own_in = scatter_whole(unfold(halves, (3, 1, 4, 5, 2, 0, 6), (D, FF)))
    back_t = unfold(jnp.stack(back_table), (2, 0, 4, 3, 1, 5), (D, FF))
    own_back = scatter_whole(back_t.T)
    own_vectors = lax.psum_scatter(
        grad_vectors.reshape(-1), ALL, scatter_dimension=0, tiled=True
    )
    return (output, grad_hidden, own_qkv, own_out, own_in, own_back, own_vectors)


def solution(mesh):
    trees = mesh.shape["wide"] == 8 and mesh.shape["narrow"] == 4
    return jax.shard_map(
        per_device if trees else per_device_plain,
        mesh=mesh,
        in_specs=(P(ALL, None),) * 2 + (P("wide", "narrow"),) * 4 + (P(ALL), P(ALL, None)),
        out_specs=(P(ALL, None),) * 2 + (P("wide", "narrow"),) * 4 + (P(ALL),),
        check_vma=False,
    )
```

time: 323 us -> 311 us (0.963)
  other arithmetic: 26.1 us -> 13.5 us
  waiting for transfers between devices: 61.2 us -> 64.7 us
    convert_element_type x5 -> x2, other arithmetic: 13.7 us -> 5.22 us  [chip_parts(): return [wide_sum(kept[s], received[s]).astype(bf16) for s in range(4)]]
    pallas_call x9 -> x8, Pallas kernels: 98.4 us -> 94.5 us  [the longest x1 31.6 us: backward(): pl.pallas_call(functools.partial(backward_kernel, place), grid=(tokens //...]
    ppermute x45 -> x48, waiting for transfers between devices: 61.2 us -> 64.7 us  [send(): return lax.ppermute(values, ALL, pairs)]
    ppermute x45 -> x48, starting transfers between devices: 42.7 us -> 45.6 us  [send(): return lax.ppermute(values, ALL, pairs)]
    unnamed x67 -> x75, local copies, waits for them, and re-layouts: 6.51 us -> 7.59 us
  transfers between devices with their start and end apart: 46 -> 49, of which waited for: 20 -> 22; matrix products, arithmetic and copies ran while one was open for 7% -> 5% of each run, Pallas kernels for 43% -> 43%
where the time goes in v1:
time: 311 us; the launch traced here: 307 us
  Pallas kernels  158 us (51%)
  waiting for transfers between devices  64.7 us (21%)
  starting transfers between devices  45.6 us (15%)
  between operations  14.8 us (5%)
  other arithmetic  13.5 us (4%)
  local copies, waits for them, and re-layouts  10.2 us (3%)
    ppermute x48, waiting for transfers between devices, send(): return lax.ppermute(values, ALL, pairs)  64.7 us
    ppermute x48, starting transfers between devices, send(): return lax.ppermute(values, ALL, pairs)  45.6 us
    pallas_call x1, Pallas kernels, backward(): pl.pallas_call(functools.partial(backward_kernel, place), grid=(tokens //...  31.6 us
    pallas_call x2, Pallas kernels, attend_back(): pl.pallas_call(kernel, grid=(1,), in_specs=[pl.BlockSpec((length, 3 * D),...  26.7 us
    pallas_call x1, Pallas kernels, outer_forward(): pl.pallas_call(functools.partial(outer_kernel, place), grid=(tokens // TI...  22.4 us
    pallas_call x1, Pallas kernels, attend(): pl.pallas_call(functools.partial(attend_kernel, place), grid=(rows,), in_...  21.2 us
    pallas_call x1, Pallas kernels, inner_forward(): pl.pallas_call(functools.partial(inner_kernel, place), grid=(tokens // TI...  19.5 us
    pallas_call x1, Pallas kernels, grad_of_hidden(): pl.pallas_call(functools.partial(hidden_kernel, place), grid=(tokens // T...  10 us
  transfers between devices with their start and end apart: 49, of which 22 were waited for; matrix products, arithmetic and copies ran while one was open for 5% of the time, Pallas kernels for 43%

profile of v1, /device:TPU:0, one launch (start us, length us, event | category | flops | bytes accessed | tf_op | source)
XLA Modules:
  0.0 307.3 jit_solution(1010913457303774482)
XLA Ops:
  13.1 3.1 collective-permute-start.4
  16.1 2.6 collective-permute-start.5
  25.1 3.6 %collective-permute-done.5 = bf16[48,1280]{1,0:T(8,128)(2,1)S(1)} collective-permute-done((bf16[48,1280]{1,0:T(8,128)(2,1)}, bf16[48,1280]{1,0:T(8,128)(2,1)S(1)}, u32[]{:S(2)}, u32[]{:S(2)}) %collective-permute-start.5) | collective-permute-done | bytes 122912 | tf_op jit(solution)/shard_map/ppermute | solution.py:36
  35.4 4.8 %collective-permute-done.10 = bf16[48,1920]{1,0:T(8,128)(2,1)} collective-permute-done((bf16[48,1920]{1,0:T(8,128)(2,1)S(1)}, bf16[48,1920]{1,0:T(8,128)(2,1)}, u32[]{:S(2)}, u32[]{:S(2)}) %collective-permute-start.10) | collective-permute-done | bytes 184352 | tf_op jit(solution)/shard_map/ppermute | solution.py:36
  42.1 7.5 %collective-permute-done.11 = bf16[48,1920]{1,0:T(8,128)(2,1)} collective-permute-done((bf16[48,1920]{1,0:T(8,128)(2,1)S(1)}, bf16[48,1920]{1,0:T(8,128)(2,1)}, u32[]{:S(2)}, u32[]{:S(2)}) %collective-permute-start.11) | collective-permute-done | bytes 184352 | tf_op jit(solution)/shard_map/ppermute | solution.py:36
  62.9 21.2 %attend.1 = (bf16[1024,2304]{1,0:T(8,128)(2,1)}, bf16[1024,768]{1,0:T(8,128)(2,1)}, bf16[768,1024]{1,0:T(8,128)(2,1)}, bf16[24,512,512]{2,1,0:T(8,128)(2,1)}) custom-call(bf16[1024,768]{1,0:T(8,128)(2,1)} %hidden.1, f32[12,768]{1,0:T(8,128)} %reshape.76.refs_1_.refs_2_.refs_3_.refs_6_, bf16[1024,128]{1,0:T(8,128)(2,1)} %add_convert_fusion.8.refs_2_, ...), custom_call_target="tpu_custom_call" | custom-call | tf_op jit(solution)/shard_map/attend/pallas_call | solution.py:363
  84.1 10.0 %collective-permute-done.19.refs_6_.refs_10_ = bf16[4,48,1920]{2,1,0:T(8,128)(2,1)} collective-permute-done((bf16[4,48,1920]{2,1,0:T(8,128)(2,1)S(1)}, bf16[4,48,1920]{2,1,0:T(8,128)(2,1)}, u32[]{:S(2)}, u32[]{:S(2)}) %collective-permute-start.19) | collective-permute-done | bytes 737312 | tf_op jit(solution)/shard_map/ppermute | solution.py:36
  100.7 19.5 %inner_forward.1 = (bf16[1024,768]{1,0:T(8,128)(2,1)}, f32[1024,768]{1,0:T(8,128)}, f32[1024,128]{1,0:T(8,128)}, bf16[1024,3072]{1,0:T(8,128)(2,1)}, bf16[1024,3072]{1,0:T(8,128)(2,1)}) custom-call(bf16[1024,768]{1,0:T(8,128)(2,1)} %get-tuple-element.176.refs_0_, bf16[1024,768]{1,0:T(8,128)(2,1)} %hidden.1, ...), custom_call_target="tpu_custom_call" | custom-call | tf_op jit(solution)/shard_map/inner_forward/pallas_call | solution.py:430
  120.2 22.4 %outer_forward.1 = (bf16[1024,768]{1,0:T(8,128)(2,1)}, f32[1024,768]{1,0:T(8,128)}, f32[8,768]{1,0:T(8,128)}, bf16[4,4,192,384]{3,2,1,0:T(8,128)(2,1)}, bf16[4,4,192,384]{3,2,1,0:T(8,128)(2,1)}) custom-call(bf16[1024,3072]{1,0:T(8,128)(2,1)} %get-tuple-element.187.refs_0_, f32[1024,768]{1,0:T(8,128)} %get-tuple-element.188.refs_1_.refs_2_, ...), custom_call_target="tpu_custom_call" | custom-call | tf_op jit(solution)/shard_map/outer_forward/pallas_call | solution.py:508
  142.8 31.6 %backward.1 = (bf16[1024,768]{1,0:T(8,128)(2,1)}, f32[1024,768]{1,0:T(8,128)}, f32[8,768]{1,0:T(8,128)}, f32[8,768]{1,0:T(8,128)}, bf16[4,4,48,1920]{3,2,1,0:T(8,128)(2,1)}, /*index=5*/bf16[4,4,48,1920]{3,2,1,0:T(8,128)(2,1)}) custom-call(f32[1024,768]{1,0:T(8,128)} %get-tuple-element.192.refs_0_, bf16[1024,3072]{1,0:T(8,128)(2,1)} %get-tuple-element.193.refs_1_, ...), custom_call_target="tpu_custom_call" | custom-call | tf_op jit(solution)/shard_map/backward/pallas_call | solution.py:621
  174.9 3.4 %fusion.7 = (bf16[4,192,384]{2,1,0:T(8,128)(2,1)S(1)}, bf16[4,192,384]{2,1,0:T(8,128)(2,1)}, bf16[4,192,384]{2,1,0:T(8,128)(2,1)}, bf16[4,192,384]{2,1,0:T(8,128)(2,1)}) fusion(bf16[4,4,192,384]{3,2,1,0:T(8,128)(2,1)} %collective-permute-done.24, bf16[4,4,192,384]{3,2,1,0:T(8,128)(2,1)S(1)} %copy-done.13), kind=kLoop, calls=%fused_computation.16 | loop fusion | flops 4718592 | bytes 7077888 | tf_op jit(solution)/shard_map/convert_element_type | solution.py:185
  187.3 13.3 %attend_back.2 = (bf16[1024,2304]{1,0:T(8,128)(2,1)}, f32[1,8,768]{2,1,0:T(8,128)}) custom-call(bf16[1024,2304]{1,0:T(8,128)(2,1)} %get-tuple-element.207.packed, bf16[1024,768]{1,0:T(8,128)(2,1)} %get-tuple-element.211.grad_att, bf16[24,512,512]{2,1,0:T(8,128)(2,1)} %get-tuple-element.212.probs), custom_call_target="tpu_custom_call" | custom-call | tf_op jit(solution)/shard_map/attend_back/pallas_call | solution.py:704
  200.5 13.5 %attend_back.3 = (bf16[1024,2304]{1,0:T(8,128)(2,1)}, f32[1,8,768]{2,1,0:T(8,128)}) custom-call(bf16[1024,2304]{1,0:T(8,128)(2,1)} %get-tuple-element.207.packed, bf16[1024,768]{1,0:T(8,128)(2,1)} %get-tuple-element.211.grad_att, bf16[24,512,512]{2,1,0:T(8,128)(2,1)} %get-tuple-element.212.probs, ...), custom_call_target="tpu_custom_call", output_to_operand_aliasing={{0}: (3, {})} | custom-call | tf_op jit(solution)/shard_map/attend_back/pallas_call | solution.py:704
  214.0 2.6 line_parts.3
  216.6 4.2 %collective-permute-start.29 = (bf16[2,192,384]{2,1,0:T(8,128)(2,1)}, bf16[2,192,384]{2,1,0:T(8,128)(2,1)S(1)}, u32[]{:S(2)}, u32[]{:S(2)}) collective-permute-start(bf16[2,192,384]{2,1,0:T(8,128)(2,1)} %get-tuple-element.242), channel_id=1, source_target_pairs={{0,16},{1,17},{2,18},{3,19},{4,20},{5,21},{6,22},{7,23},{8,24},{9,... | collective-permute-start | bytes 884744 | tf_op jit(solution)/shard_map/ppermute | solution.py:36
  222.5 9.4 %grad_qkv.1 = (bf16[4,48,1280]{2,1,0:T(8,128)(2,1)}, bf16[4,48,1280]{2,1,0:T(8,128)(2,1)}, bf16[4,48,1280]{2,1,0:T(8,128)(2,1)}, bf16[4,48,1280]{2,1,0:T(8,128)(...) custom-call(bf16[1024,768]{1,0:T(8,128)(2,1)} %hidden.1, ...), custom_call_target="tpu_custom_call" | custom-call | tf_op jit(solution)/shard_map/grad_qkv/pallas_call | solution.py:756
  232.0 9.0 %collective-permute-done.31.refs_2_ = bf16[4,48,1920]{2,1,0:T(8,128)(2,1)S(1)} collective-permute-done((bf16[4,48,1920]{2,1,0:T(8,128)(2,1)S(1)}, bf16[4,48,1920]{2,1,0:T(8,128)(2,1)S(1)}, u32[]{:S(2)}, u32[]{:S(2)}) %collective-permute-start.31) | collective-permute-done | bytes 737312 | tf_op jit(solution)/shard_map/ppermute | solution.py:36
  246.0 4.2 %chip_parts.1 = (bf16[4,48,1280]{2,1,0:T(8,128)(2,1)}, bf16[4,48,1280]{2,1,0:T(8,128)(2,1)}, bf16[4,48,1280]{2,1,0:T(8,128)(2,1)}, bf16[4,48,1280]{2,1,0:T(8,128)(2,1)}) custom-call(bf16[4,48,1280]{2,1,0:T(8,128)(2,1)} %get-tuple-element.245.refs_0_, bf16[4,48,1280]{2,1,0:T(8,128)(2,1)} %get-tuple-element.246.refs_1_, ...), custom_call_target="tpu_custom_call" | custom-call | tf_op jit(solution)/shard_map/chip_parts/pallas_call | solution.py:196
  251.1 2.9 line_parts.4
  254.1 3.7 %collective-permute-start.37 = (bf16[2,48,1920]{2,1,0:T(8,128)(2,1)}, bf16[2,48,1920]{2,1,0:T(8,128)(2,1)S(1)}, u32[]{:S(2)}, u32[]{:S(2)}) collective-permute-start(bf16[2,48,1920]{2,1,0:T(8,128)(2,1)} %get-tuple-element.270), channel_id=1, source_target_pairs={{0,16},{1,17},{2,18},{3,19},{4,20},{5,21},{6,22},{7,23},{8,24},{9,... | collective-permute-start | bytes 1105928 | tf_op jit(solution)/shard_map/ppermute | solution.py:36
  261.6 10.0 %grad_hidden.1 = f32[1024,768]{1,0:T(8,128)} custom-call(bf16[1024,2304]{1,0:T(8,128)(2,1)} %get-tuple-element.228.low.refs_0_, f32[1024,768]{1,0:T(8,128)} %get-tuple-element.265.refs_1_, bf16[4,48,1280]{2,1,0:T(8,128)(2,1)} %copy-done, bf16[4,48,1280]{2,1,0:T(8,128)(2,1)} %copy-done.2, bf16[4,48,1280]{2,1,0:T(8,128)(2,1)} %copy-done.3, ...), custom_call_target="tpu_custom_call" | custom-call | tf_op jit(solution)/shard_map/grad_hidden/pallas_call | solution.py:786
  271.6 3.1 %collective-permute-done.37 = bf16[2,48,1920]{2,1,0:T(8,128)(2,1)S(1)} collective-permute-done((bf16[2,48,1920]{2,1,0:T(8,128)(2,1)}, bf16[2,48,1920]{2,1,0:T(8,128)(2,1)S(1)}, u32[]{:S(2)}, u32[]{:S(2)}) %collective-permute-start.37) | collective-permute-done | bytes 368672 | tf_op jit(solution)/shard_map/ppermute | solution.py:36
  275.7 7.3 %collective-permute-done.40.refs_2_ = bf16[4,48,1280]{2,1,0:T(8,128)(2,1)S(1)} collective-permute-done((bf16[4,48,1280]{2,1,0:T(8,128)(2,1)}, bf16[4,48,1280]{2,1,0:T(8,128)(2,1)S(1)}, u32[]{:S(2)}, u32[]{:S(2)}) %collective-permute-start.40) | collective-permute-done | bytes 491552 | tf_op jit(solution)/shard_map/ppermute | solution.py:36
  294.0 3.9 %collective-permute-done.45 = bf16[48,1280]{1,0:T(8,128)(2,1)S(1)} collective-permute-done((bf16[48,1280]{1,0:T(8,128)(2,1)}, bf16[48,1280]{1,0:T(8,128)(2,1)S(1)}, u32[]{:S(2)}, u32[]{:S(2)}) %collective-permute-start.45) | collective-permute-done | bytes 122912 | tf_op jit(solution)/shard_map/ppermute | solution.py:36
  (191 shorter events, 75.6 us)
Async XLA Ops:
  7.2 113.1 %all-gather.3.cloned.1.call-start = ((), (), s32[]{:S(2)}) async-start(), calls=%async_computation | async-start | bytes 4866048 | tf_op jit(solution)/shard_map/all_gather | solution.py:840
  13.1 12.0 %collective-permute-start.4 = (bf16[48,1280]{1,0:T(8,128)(2,1)}, bf16[48,1280]{1,0:T(8,128)(2,1)S(1)}, u32[]{:S(2)}, u32[]{:S(2)}) collective-permute-start(bf16[48,1280]{1,0:T(8,128)(2,1)} %pair_up.2), channel_id=1, source_target_pairs={{0,8},{1,9},{2,10},{3,11},{4,12},{5,13},{6,14},{7,15},{8,0},{9,1},... | collective-permute-start | bytes 368648 | tf_op jit(solution)/shard_map/ppermute | solution.py:36
  16.1 12.6 %collective-permute-start.5 = (bf16[48,1280]{1,0:T(8,128)(2,1)}, bf16[48,1280]{1,0:T(8,128)(2,1)S(1)}, u32[]{:S(2)}, u32[]{:S(2)}) collective-permute-start(bf16[48,1280]{1,0:T(8,128)(2,1)} %pair_up.2), channel_id=1, source_target_pairs={{0,16},{1,17},{2,18},{3,19},{4,20},{5,21},{6,22},{7,23},{8,24},{9,... | collective-permute-start | bytes 368648 | tf_op jit(solution)/shard_map/ppermute | solution.py:36
  28.8 20.8 %collective-permute-start.7 = (bf16[4,48,1280]{2,1,0:T(8,128)(2,1)S(1)}, bf16[4,48,1280]{2,1,0:T(8,128)(2,1)S(1)}, u32[]{:S(2)}, u32[]{:S(2)}) collective-permute-start(bf16[4,48,1280]{2,1,0:T(8,128)(2,1)S(1)} %pad_maximum_fusion.1.refs_0_.refs_4_.refs_2_), channel_id=1, source_target_pairs={{0,2},{1,3},{2,0},{3,1},{4,6},{5,7},{6,4},{7,5},{8,10},{9,11},{10,... | collective-permute-start | bytes 1474568 | tf_op jit(solution)/shard_map/ppermute | solution.py:36
  30.4 21.3 %collective-permute-start.8 = (bf16[4,48,1280]{2,1,0:T(8,128)(2,1)S(1)}, bf16[4,48,1280]{2,1,0:T(8,128)(2,1)S(1)}, u32[]{:S(2)}, u32[]{:S(2)}) collective-permute-start(bf16[4,48,1280]{2,1,0:T(8,128)(2,1)S(1)} %pad_maximum_fusion.1.refs_0_.refs_4_.refs_2_), channel_id=1, source_target_pairs={{0,4},{1,5},{2,6},{3,7},{4,0},{5,1},{6,2},{7,3},{8,12},{9,13},{10,... | collective-permute-start | bytes 1474568 | tf_op jit(solution)/shard_map/ppermute | solution.py:36
  31.9 19.8 %collective-permute-start.9 = (bf16[4,48,1280]{2,1,0:T(8,128)(2,1)S(1)}, bf16[4,48,1280]{2,1,0:T(8,128)(2,1)S(1)}, u32[]{:S(2)}, u32[]{:S(2)}) collective-permute-start(bf16[4,48,1280]{2,1,0:T(8,128)(2,1)S(1)} %pad_maximum_fusion.1.refs_0_.refs_4_.refs_2_), channel_id=1, source_target_pairs={{0,6},{1,7},{2,4},{3,5},{4,2},{5,3},{6,0},{7,1},{8,14},{9,15},{10,... | collective-permute-start | bytes 1474568 | tf_op jit(solution)/shard_map/ppermute | solution.py:36
  34.4 15.1 %collective-permute-start.11 = (bf16[48,1920]{1,0:T(8,128)(2,1)S(1)}, bf16[48,1920]{1,0:T(8,128)(2,1)}, u32[]{:S(2)}, u32[]{:S(2)}) collective-permute-start(bf16[48,1920]{1,0:T(8,128)(2,1)S(1)} %pad_maximum_fusion.4), channel_id=1, source_target_pairs={{0,16},{1,17},{2,18},{3,19},{4,20},{5,21},{6,22},{7,23},{8,24},{9,... | collective-permute-start | bytes 552968 | tf_op jit(solution)/shard_map/ppermute | solution.py:36
  53.5 30.6 %collective-permute-start.17 = (bf16[4,48,1920]{2,1,0:T(8,128)(2,1)S(1)}, bf16[4,48,1920]{2,1,0:T(8,128)(2,1)}, u32[]{:S(2)}, u32[]{:S(2)}) collective-permute-start(bf16[4,48,1920]{2,1,0:T(8,128)(2,1)S(1)} %pad_maximum_fusion.refs_3_.refs_7_), channel_id=1, source_target_pairs={{0,2},{1,3},{2,0},{3,1},{4,6},{5,7},{6,4},{7,5},{8,10},{9,11},{10,... | collective-permute-start | bytes 2211848 | tf_op jit(solution)/shard_map/ppermute | solution.py:36
  54.8 29.3 %collective-permute-start.18 = (bf16[4,48,1920]{2,1,0:T(8,128)(2,1)S(1)}, bf16[4,48,1920]{2,1,0:T(8,128)(2,1)}, u32[]{:S(2)}, u32[]{:S(2)}) collective-permute-start(bf16[4,48,1920]{2,1,0:T(8,128)(2,1)S(1)} %pad_maximum_fusion.refs_3_.refs_7_), channel_id=1, source_target_pairs={{0,4},{1,5},{2,6},{3,7},{4,0},{5,1},{6,2},{7,3},{8,12},{9,13},{10,... | collective-permute-start | bytes 2211848 | tf_op jit(solution)/shard_map/ppermute | solution.py:36
  55.6 38.5 %collective-permute-start.19 = (bf16[4,48,1920]{2,1,0:T(8,128)(2,1)S(1)}, bf16[4,48,1920]{2,1,0:T(8,128)(2,1)}, u32[]{:S(2)}, u32[]{:S(2)}) collective-permute-start(bf16[4,48,1920]{2,1,0:T(8,128)(2,1)S(1)} %pad_maximum_fusion.refs_3_.refs_7_), channel_id=1, source_target_pairs={{0,6},{1,7},{2,4},{3,5},{4,2},{5,3},{6,0},{7,1},{8,14},{9,15},{10,... | collective-permute-start | bytes 2211848 | tf_op jit(solution)/shard_map/ppermute | solution.py:36
  142.6 31.9 %collective-permute-start.24 = (bf16[4,4,192,384]{3,2,1,0:T(8,128)(2,1)}, bf16[4,4,192,384]{3,2,1,0:T(8,128)(2,1)}, u32[]{:S(2)}, u32[]{:S(2)}) collective-permute-start(bf16[4,4,192,384]{3,2,1,0:T(8,128)(2,1)} %get-tuple-element.203), channel_id=1, source_target_pairs={{0,1},{1,0},{2,3},{3,2},{4,5},{5,4},{6,7},{7,6},{8,9},{9,8},{10,11... | collective-permute-start | bytes 7077896 | tf_op jit(solution)/shard_map/ppermute | solution.py:36
  180.1 33.9 %collective-permute-start.26 = (bf16[4,192,384]{2,1,0:T(8,128)(2,1)}, bf16[4,192,384]{2,1,0:T(8,128)(2,1)}, u32[]{:S(2)}, u32[]{:S(2)}) collective-permute-start(bf16[4,192,384]{2,1,0:T(8,128)(2,1)} %get-tuple-element.216), channel_id=1, source_target_pairs={{0,2},{1,3},{2,0},{3,1},{4,6},{5,7},{6,4},{7,5},{8,10},{9,11},{10,... | collective-permute-start | bytes 1769480 | tf_op jit(solution)/shard_map/ppermute | solution.py:36
  181.3 32.7 %collective-permute-start.27 = (bf16[4,192,384]{2,1,0:T(8,128)(2,1)}, bf16[4,192,384]{2,1,0:T(8,128)(2,1)}, u32[]{:S(2)}, u32[]{:S(2)}) collective-permute-start(bf16[4,192,384]{2,1,0:T(8,128)(2,1)} %get-tuple-element.217), channel_id=1, source_target_pairs={{0,4},{1,5},{2,6},{3,7},{4,0},{5,1},{6,2},{7,3},{8,12},{9,13},{10,... | collective-permute-start | bytes 1769480 | tf_op jit(solution)/shard_map/ppermute | solution.py:36
  181.9 32.1 %collective-permute-start.28 = (bf16[4,192,384]{2,1,0:T(8,128)(2,1)S(1)}, bf16[4,192,384]{2,1,0:T(8,128)(2,1)}, u32[]{:S(2)}, u32[]{:S(2)}) collective-permute-start(bf16[4,192,384]{2,1,0:T(8,128)(2,1)S(1)} %get-tuple-element.218), channel_id=1, source_target_pairs={{0,6},{1,7},{2,4},{3,5},{4,2},{5,3},{6,0},{7,1},{8,14},{9,15},{10,... | collective-permute-start | bytes 1769480 | tf_op jit(solution)/shard_map/ppermute | solution.py:36
  185.5 46.5 %collective-permute-start.30 = (bf16[4,48,1920]{2,1,0:T(8,128)(2,1)}, bf16[4,48,1920]{2,1,0:T(8,128)(2,1)S(1)}, u32[]{:S(2)}, u32[]{:S(2)}) collective-permute-start(bf16[4,48,1920]{2,1,0:T(8,128)(2,1)} %get-tuple-element.243), channel_id=1, source_target_pairs={{0,2},{1,3},{2,0},{3,1},{4,6},{5,7},{6,4},{7,5},{8,10},{9,11},{10,... | collective-permute-start | bytes 2211848 | tf_op jit(solution)/shard_map/ppermute | solution.py:36
  186.7 54.3 %collective-permute-start.31 = (bf16[4,48,1920]{2,1,0:T(8,128)(2,1)S(1)}, bf16[4,48,1920]{2,1,0:T(8,128)(2,1)S(1)}, u32[]{:S(2)}, u32[]{:S(2)}) collective-permute-start(bf16[4,48,1920]{2,1,0:T(8,128)(2,1)S(1)} %get-tuple-element.244), channel_id=1, source_target_pairs={{0,4},{1,5},{2,6},{3,7},{4,0},{5,1},{6,2},{7,3},{8,12},{9,13},{10,... | collective-permute-start | bytes 2211848 | tf_op jit(solution)/shard_map/ppermute | solution.py:36
  216.6 24.3 %collective-permute-start.29 = (bf16[2,192,384]{2,1,0:T(8,128)(2,1)}, bf16[2,192,384]{2,1,0:T(8,128)(2,1)S(1)}, u32[]{:S(2)}, u32[]{:S(2)}) collective-permute-start(bf16[2,192,384]{2,1,0:T(8,128)(2,1)} %get-tuple-element.242), channel_id=1, source_target_pairs={{0,16},{1,17},{2,18},{3,19},{4,20},{5,21},{6,22},{7,23},{8,24},{9,... | collective-permute-start | bytes 884744 | tf_op jit(solution)/shard_map/ppermute | solution.py:36
  220.8 29.4 %collective-permute-start.36 = (bf16[4,48,1920]{2,1,0:T(8,128)(2,1)S(1)}, bf16[4,48,1920]{2,1,0:T(8,128)(2,1)S(1)}, u32[]{:S(2)}, u32[]{:S(2)}) collective-permute-start(bf16[4,48,1920]{2,1,0:T(8,128)(2,1)S(1)} %get-tuple-element.260), channel_id=1, source_target_pairs={{0,6},{1,7},{2,4},{3,5},{4,2},{5,3},{6,0},{7,1},{8,14},{9,15},{10,... | collective-permute-start | bytes 2211848 | tf_op jit(solution)/shard_map/ppermute | solution.py:36
  254.1 20.7 %collective-permute-start.37 = (bf16[2,48,1920]{2,1,0:T(8,128)(2,1)}, bf16[2,48,1920]{2,1,0:T(8,128)(2,1)S(1)}, u32[]{:S(2)}, u32[]{:S(2)}) collective-permute-start(bf16[2,48,1920]{2,1,0:T(8,128)(2,1)} %get-tuple-element.270), channel_id=1, source_target_pairs={{0,16},{1,17},{2,18},{3,19},{4,20},{5,21},{6,22},{7,23},{8,24},{9,... | collective-permute-start | bytes 1105928 | tf_op jit(solution)/shard_map/ppermute | solution.py:36
  257.9 13.8 %collective-permute-start.38 = (bf16[192,384]{1,0:T(8,128)(2,1)S(1)}, bf16[192,384]{1,0:T(8,128)(2,1)S(1)}, u32[]{:S(2)}, u32[]{:S(2)}) collective-permute-start(bf16[192,384]{1,0:T(8,128)(2,1)S(1)} %get-tuple-element.311), channel_id=1, source_target_pairs={{0,8},{1,9},{2,10},{3,11},{4,12},{5,13},{6,14},{7,15},{8,0},{9,1},... | collective-permute-start | bytes 442376 | tf_op jit(solution)/shard_map/ppermute | solution.py:36
  258.0 17.7 %collective-permute-start.39 = (bf16[4,48,1280]{2,1,0:T(8,128)(2,1)}, bf16[4,48,1280]{2,1,0:T(8,128)(2,1)S(1)}, u32[]{:S(2)}, u32[]{:S(2)}) collective-permute-start(bf16[4,48,1280]{2,1,0:T(8,128)(2,1)} %get-tuple-element.273), channel_id=1, source_target_pairs={{0,2},{1,3},{2,0},{3,1},{4,6},{5,7},{6,4},{7,5},{8,10},{9,11},{10,... | collective-permute-start | bytes 1474568 | tf_op jit(solution)/shard_map/ppermute | solution.py:36
  259.5 23.4 %collective-permute-start.40 = (bf16[4,48,1280]{2,1,0:T(8,128)(2,1)}, bf16[4,48,1280]{2,1,0:T(8,128)(2,1)S(1)}, u32[]{:S(2)}, u32[]{:S(2)}) collective-permute-start(bf16[4,48,1280]{2,1,0:T(8,128)(2,1)} %get-tuple-element.274), channel_id=1, source_target_pairs={{0,4},{1,5},{2,6},{3,7},{4,0},{5,1},{6,2},{7,3},{8,12},{9,13},{10,... | collective-permute-start | bytes 1474568 | tf_op jit(solution)/shard_map/ppermute | solution.py:36
  260.1 22.9 %collective-permute-start.41 = (bf16[4,48,1280]{2,1,0:T(8,128)(2,1)S(1)}, bf16[4,48,1280]{2,1,0:T(8,128)(2,1)S(1)}, u32[]{:S(2)}, u32[]{:S(2)}) collective-permute-start(bf16[4,48,1280]{2,1,0:T(8,128)(2,1)S(1)} %copy-done.35), channel_id=1, source_target_pairs={{0,6},{1,7},{2,4},{3,5},{4,2},{5,3},{6,0},{7,1},{8,14},{9,15},{10,... | collective-permute-start | bytes 1474568 | tf_op jit(solution)/shard_map/ppermute | solution.py:36
  274.9 15.8 %collective-permute-start.42 = (bf16[48,1920]{1,0:T(8,128)(2,1)S(1)}, bf16[48,1920]{1,0:T(8,128)(2,1)S(1)}, u32[]{:S(2)}, u32[]{:S(2)}) collective-permute-start(bf16[48,1920]{1,0:T(8,128)(2,1)S(1)} %get-tuple-element.308), channel_id=1, source_target_pairs={{0,8},{1,9},{2,10},{3,11},{4,12},{5,13},{6,14},{7,15},{8,0},{9,1},... | collective-permute-start | bytes 552968 | tf_op jit(solution)/shard_map/ppermute | solution.py:36
  (61 other events, 441.9 us)
Sparse Core Ops, SparseCore 0:
  51.8 68.0 all-gather.2

commit v2 on v1

--- a/solution.py
+++ b/solution.py
@@ -13,7 +13,6 @@
 TILE = 256
 ALL = ("wide", "narrow")
 CHIP_STEPS = ((0, 0), (1, 0), (0, 1), (1, 1))
-VMEM_LIMIT = 60 * 2**20
 bf16, f32 = jnp.bfloat16, jnp.float32
 Shape = jax.ShapeDtypeStruct
 
@@ -24,8 +23,8 @@
     return pl.CostEstimate(flops=0 * us, bytes_accessed=0, transcendentals=0)
 
 
-def params():
-    return pltpu.CompilerParams(vmem_limit_bytes=VMEM_LIMIT)
+def params(mib=60):
+    return pltpu.CompilerParams(vmem_limit_bytes=mib * 2**20)
 
 
 def send(values, z=0, y=0, x=0, core=0):
@@ -199,7 +198,7 @@
         in_specs=[line] * 8,
         out_specs=[line] * 4,
         out_shape=[Shape((4, rows, columns), bf16)] * 4,
-        compiler_params=params(),
+        compiler_params=params(32),
         cost_estimate=cost(3),
         name="chip_parts",
     )(*kept, *received)
@@ -225,7 +224,7 @@
     return pl.pallas_call(
         functools.partial(line_kernel, far),
         out_shape=shapes,
-        compiler_params=params(),
+        compiler_params=params(32),
         cost_estimate=cost(2),
         name="line_parts",
     )(own, *others)
@@ -383,7 +382,7 @@
             Shape((D, tokens), bf16),
             Shape((rows * HEADS, length, length), bf16),
         ],
-        compiler_params=params(),
+        compiler_params=params(60),
         cost_estimate=cost(20),
         name="attend",
     )(hidden, vectors, key_marks, query_marks, *blocks)
@@ -445,7 +444,7 @@
             pltpu.SemaphoreType.DMA((32,)),
             pltpu.SemaphoreType.DMA((32,)),
         ],
-        compiler_params=params(),
+        compiler_params=params(60),
         cost_estimate=cost(16),
         name="inner_forward",
     )(att, hidden, vectors, *blocks)
@@ -453,7 +452,8 @@
 
 def outer_kernel(place, *refs):
     act, normed, cotangent, vectors, back_table = refs[:5]
-    output, grad_second, sums, kept, sent, w_back, activated, grad_t, sems = refs[5:]
+    output, grad_second, sums = refs[5:8]
+    outs, (w_back, activated, grad_t, sems) = refs[8:16], refs[16:]
     step = pl.program_id(0)
     z, y, x, core = place()
 
@@ -495,12 +495,16 @@
         for k in range(4):
             columns = pl.ds(pl.multiple_of((z ^ k) * D, D), D)
             res = dot(grad_t[...], activated[:, columns]).astype(bf16)
-            for other, out in enumerate((kept, sent)):
+            for other in range(2):
                 for i in range(2):
                     at = (other * 2 + i) * 192
-                    for half in range(2):
-                        piece = res[at : at + 192, half * 384 : half * 384 + 384]
-                        out[i + 2 * (half ^ y), k] = piece
+                    pieces = [res[at : at + 192, half * 384 : half * 384 + 384] for half in range(2)]
+                    for bit in range(2):
+
+                        @pl.when(y == bit)
+                        def _(other=other, i=i, k=k, pieces=pieces, bit=bit):
+                            outs[other * 4 + i][k] = pieces[bit]
+                            outs[other * 4 + i + 2][k] = pieces[1 - bit]
 
 
 def outer_forward(place, activated, normed, cotangent, vectors, back_table):
@@ -509,20 +513,20 @@
         functools.partial(outer_kernel, place),
         grid=(tokens // TILE,),
         in_specs=[tile(FF), tile(D), tile(D), fixed((12, D))] + anywhere(1),
-        out_specs=[tile(D), tile(D), fixed((8, D))] + [fixed((4, 4, 192, 384))] * 2,
+        out_specs=[tile(D), tile(D), fixed((8, D))] + [fixed((4, 192, 384))] * 8,
         out_shape=[
             Shape((tokens, D), bf16),
             Shape((tokens, D), f32),
             Shape((8, D), f32),
         ]
-        + [Shape((4, 4, 192, 384), bf16)] * 2,
+        + [Shape((4, 192, 384), bf16)] * 8,
         scratch_shapes=[
             pltpu.VMEM((FF, D), bf16),
             pltpu.VMEM((tokens, FF), bf16),
             pltpu.VMEM((D, tokens), bf16),
             pltpu.SemaphoreType.DMA((32,)),
         ],
-        compiler_params=params(),
+        compiler_params=params(60),
         cost_estimate=cost(18),
         name="outer_forward",
     )(activated, normed, cotangent, vectors, back_table)
@@ -638,7 +642,7 @@
             pltpu.VMEM((D, tokens), bf16),
         ]
         + [pltpu.SemaphoreType.DMA((32,))] * 3,
-        compiler_params=params(),
+        compiler_params=params(32),
         cost_estimate=cost(22),
         name="backward",
     )(grad_second, slope, normed, inverse, first_low, att_t, vectors, *blocks, back_table)
@@ -716,7 +720,7 @@
         ],
         out_shape=[Shape(packed.shape, bf16), Shape((1, 8, D), f32)],
         input_output_aliases=alias,
-        compiler_params=params(),
+        compiler_params=params(32),
         cost_estimate=cost(12),
         name="attend_back",
     )(packed, grad_att, probs, *more)
@@ -757,7 +761,7 @@
         functools.partial(grad_qkv_kernel, place),
         out_shape=[Shape((4, 48, 1280), bf16)] * 8,
         scratch_shapes=[pltpu.VMEM((D, hidden.shape[0]), bf16), pltpu.VMEM((80, 1, 128), f32)],
-        compiler_params=params(),
+        compiler_params=params(32),
         cost_estimate=cost(9),
         name="grad_qkv",
     )(hidden, low, *sums)
@@ -790,7 +794,7 @@
         out_specs=tile(D),
         out_shape=Shape((tokens, D), f32),
         scratch_shapes=[pltpu.VMEM((D, 3 * D), bf16), pltpu.SemaphoreType.DMA((32,))],
-        compiler_params=params(),
+        compiler_params=params(32),
         cost_estimate=cost(9),
         name="grad_hidden",
     )(low, grad_branch, *blocks)
@@ -850,11 +854,14 @@
     inner_outs, back_table = tie(inner_outs, back_table)
     first_low, normed, inverse, activated, slope = inner_outs
 
-    output, grad_second, sums_second, kept_back, sent_back = outer_forward(
+    output, grad_second, sums_second, *tables_back = outer_forward(
         position, activated, normed, cotangent, all_vectors, back_table
     )
 
-    received_back = send(sent_back, core=1)
+    received_back = [send(block, core=1) for block in tables_back[4:]]
+    parts_back = chip_parts(tables_back[:4], received_back)
+    parts_back, grad_second = tie(parts_back, grad_second)
+    others_back = chip_sends(parts_back)
     back_outs = backward(
         position,
         grad_second,
@@ -867,27 +874,19 @@
         mid_blocks,
         back_table,
     )
-    back_outs, received_back = tie(back_outs, received_back)
+    back_outs, others_back = tie(back_outs, others_back)
     grad_att, grad_branch, sums_first, sums_inner, kept_mid, sent_mid = back_outs
 
     received_mid = send(sent_mid, core=1)
-    parts_back = chip_parts(kept_back, received_back)
-    parts_back, received_mid = tie(parts_back, received_mid)
-
-    others_back = chip_sends(parts_back)
+    near_back, far_back = line_halves(parts_back[0], others_back)
     parts_mid = chip_parts(kept_mid, received_mid)
-    parts_mid, grad_att = tie(parts_mid, grad_att)
+    parts_mid, grad_att, near_back, far_back = tie(parts_mid, grad_att, near_back, far_back)
+
     plane_mid = [send(parts_mid[1], x=1), send(parts_mid[2], y=1)]
+    corner_mid = send(parts_mid[3], x=1, y=1)
+    far_back = send(far_back, z=2)
     packed_low, sums_zero = attend_back(0, packed, grad_att, probs)
     packed_low, sums_one = attend_back(1, packed, grad_att, probs, packed_low)
-    packed_low, sums_one, others_back, corner_mid = tie(
-        packed_low, sums_one, others_back, parts_mid[3]
-    )
-
-    near_back, far_back = line_halves(parts_back[0], others_back)
-    near_back, far_back, corner_mid, packed_low = tie(near_back, far_back, corner_mid, packed_low)
-    corner_mid = send(corner_mid, x=1, y=1)
-    far_back = send(far_back, z=2)
     tables_qkv = grad_qkv(
         position, hidden, packed_low, sums_zero, sums_one, sums_first, sums_inner, sums_second
     )
@@ -973,7 +972,8 @@
     own_qkv = scatter_whole(unfold(qkv_table[..., :1152], (3, 1, 0, 4, 2, 5), (D, 3 * D)))
     own_out = scatter_whole(unfold(mid_table[..., 2 * D :], (3, 1, 0, 4, 2, 5), (D, D)))
     own_in = scatter_whole(unfold(halves, (3, 1, 4, 5, 2, 0, 6), (D, FF)))
-    back_t = unfold(jnp.stack(back_table), (2, 0, 4, 3, 1, 5), (D, FF))
+    back_table = jnp.stack(back_table).reshape(2, 4, 4, 192, 384)
+    back_t = unfold(back_table, (2, 0, 4, 3, 1, 5), (D, FF))
     own_back = scatter_whole(back_t.T)
     own_vectors = lax.psum_scatter(
         grad_vectors.reshape(-1), ALL, scatter_dimension=0, tiled=True

time: 311 us -> 288 us (0.926)
  Pallas kernels: 158 us -> 134 us
  waiting for transfers between devices: 64.7 us -> 55.4 us
  local copies, waits for them, and re-layouts: 10.2 us -> 15.3 us
  other arithmetic: 13.5 us -> 16.8 us
    ppermute x48 -> x51, waiting for transfers between devices: 64.7 us -> 55.3 us  [send(): return lax.ppermute(values, ALL, pairs)]
    pallas_call x3, Pallas kernels: 7.92 us -> 1.49 us  [line_parts(): pl.pallas_call(functools.partial(line_kernel, far), out_shape=shapes, com...]
    unnamed x75 -> x111, local copies, waits for them, and re-layouts: 7.59 us -> 12.6 us
    pallas_call x1, Pallas kernels: 9.42 us -> 4.69 us  [grad_qkv(): pl.pallas_call(functools.partial(grad_qkv_kernel, place), out_shape=[Shap...]
    pallas_call x2, Pallas kernels: 26.7 us -> 22.1 us  [attend_back(): pl.pallas_call(kernel, grid=(1,), in_specs=[pl.BlockSpec((length, 3 * D),...]
    pallas_call x1, Pallas kernels: 31.6 us -> 27.2 us  [backward(): pl.pallas_call(functools.partial(backward_kernel, place), grid=(tokens //...]
    pallas_call x1, Pallas kernels: 4.17 us -> 0.5 us  [chip_parts_of(): pl.pallas_call(chip_kernel, grid=(4,), in_specs=[line] * 8, out_specs=[li...]
    ppermute x48 -> x51, starting transfers between devices: 45.6 us -> 47.3 us  [send(): return lax.ppermute(values, ALL, pairs)]
  transfers between devices with their start and end apart: 49 -> 52, of which waited for: 22 -> 23; matrix products, arithmetic and copies ran while one was open for 5% -> 6% of each run, Pallas kernels for 43% -> 38%
where the time goes in v2:
time: 288 us; the launch traced here: 284 us
  Pallas kernels  134 us (47%)
  waiting for transfers between devices  55.4 us (19%)
  starting transfers between devices  47.3 us (16%)
  other arithmetic  16.8 us (6%)
  local copies, waits for them, and re-layouts  15.3 us (5%)
  between operations  15 us (5%)
    ppermute x51, waiting for transfers between devices, send(): return lax.ppermute(values, ALL, pairs)  55.3 us
    ppermute x51, starting transfers between devices, send(): return lax.ppermute(values, ALL, pairs)  47.3 us
    pallas_call x1, Pallas kernels, backward(): pl.pallas_call(functools.partial(backward_kernel, place), grid=(tokens //...  27.2 us
    pallas_call x1, Pallas kernels, outer_forward(): pl.pallas_call(functools.partial(outer_kernel, place), grid=(tokens // TI...  24.7 us
    pallas_call x2, Pallas kernels, attend_back(): pl.pallas_call(kernel, grid=(1,), in_specs=[pl.BlockSpec((length, 3 * D),...  22.1 us
    pallas_call x1, Pallas kernels, attend(): pl.pallas_call(functools.partial(attend_kernel, place), grid=(rows,), in_...  21.2 us
    pallas_call x1, Pallas kernels, inner_forward(): pl.pallas_call(functools.partial(inner_kernel, place), grid=(tokens // TI...  19.5 us
    unnamed x111, local copies, waits for them, and re-layouts  12.6 us
  transfers between devices with their start and end apart: 52, of which 23 were waited for; matrix products, arithmetic and copies ran while one was open for 6% of the time, Pallas kernels for 38%

profile of v2, /device:TPU:0, one launch (start us, length us, event | category | flops | bytes accessed | tf_op | source)
XLA Modules:
  0.0 284.2 jit_solution(11582473676664712905)
XLA Ops:
  13.1 3.1 %collective-permute-start.4 = (bf16[48,1280]{1,0:T(8,128)(2,1)}, bf16[48,1280]{1,0:T(8,128)(2,1)S(1)}, u32[]{:S(2)}, u32[]{:S(2)}) collective-permute-start(bf16[48,1280]{1,0:T(8,128)(2,1)} %pair_up.2), channel_id=1, source_target_pairs={{0,8},{1,9},{2,10},{3,11},{4,12},{5,13},{6,14},{7,15},{8,0},{9,1},... | collective-permute-start | bytes 368648 | tf_op jit(solution)/shard_map/ppermute | solution.py:35
  16.1 2.6 collective-permute-start.5
  20.9 2.1 pair_up.3
  25.1 3.7 %collective-permute-done.5 = bf16[48,1280]{1,0:T(8,128)(2,1)S(1)} collective-permute-done((bf16[48,1280]{1,0:T(8,128)(2,1)}, bf16[48,1280]{1,0:T(8,128)(2,1)S(1)}, u32[]{:S(2)}, u32[]{:S(2)}) %collective-permute-start.5) | collective-permute-done | bytes 122912 | tf_op jit(solution)/shard_map/ppermute | solution.py:35
  35.4 4.8 %collective-permute-done.10 = bf16[48,1920]{1,0:T(8,128)(2,1)} collective-permute-done((bf16[48,1920]{1,0:T(8,128)(2,1)S(1)}, bf16[48,1920]{1,0:T(8,128)(2,1)}, u32[]{:S(2)}, u32[]{:S(2)}) %collective-permute-start.10) | collective-permute-done | bytes 184352 | tf_op jit(solution)/shard_map/ppermute | solution.py:35
  42.1 7.4 %collective-permute-done.11 = bf16[48,1920]{1,0:T(8,128)(2,1)S(1)} collective-permute-done((bf16[48,1920]{1,0:T(8,128)(2,1)S(1)}, bf16[48,1920]{1,0:T(8,128)(2,1)S(1)}, u32[]{:S(2)}, u32[]{:S(2)}) %collective-permute-start.11) | collective-permute-done | bytes 184352 | tf_op jit(solution)/shard_map/ppermute | solution.py:35
  49.5 2.2 collective-permute-done.8.refs_2_.refs_6_.refs_4_
  62.9 21.2 %attend.1 = (bf16[1024,2304]{1,0:T(8,128)(2,1)}, bf16[1024,768]{1,0:T(8,128)(2,1)}, bf16[768,1024]{1,0:T(8,128)(2,1)}, bf16[24,512,512]{2,1,0:T(8,128)(2,1)}) custom-call(bf16[1024,768]{1,0:T(8,128)(2,1)} %hidden.1, f32[12,768]{1,0:T(8,128)} %reshape.60.refs_1_.refs_2_.refs_3_.refs_6_, bf16[1024,128]{1,0:T(8,128)(2,1)} %add_convert_fusion.8.refs_2_, ...), custom_call_target="tpu_custom_call" | custom-call | tf_op jit(solution)/shard_map/attend/pallas_call | solution.py:362
  84.2 10.0 %collective-permute-done.19.refs_6_.refs_10_ = bf16[4,48,1920]{2,1,0:T(8,128)(2,1)} collective-permute-done((bf16[4,48,1920]{2,1,0:T(8,128)(2,1)S(1)}, bf16[4,48,1920]{2,1,0:T(8,128)(2,1)}, u32[]{:S(2)}, u32[]{:S(2)}) %collective-permute-start.19) | collective-permute-done | bytes 737312 | tf_op jit(solution)/shard_map/ppermute | solution.py:35
  95.2 2.2 collective-permute-done.20.refs_7_.refs_11_
  100.7 19.5 %inner_forward.1 = (bf16[1024,768]{1,0:T(8,128)(2,1)}, f32[1024,768]{1,0:T(8,128)}, f32[1024,128]{1,0:T(8,128)}, bf16[1024,3072]{1,0:T(8,128)(2,1)}, bf16[1024,3072]{1,0:T(8,128)(2,1)}) custom-call(bf16[1024,768]{1,0:T(8,128)(2,1)} %get-tuple-element.176.refs_0_, bf16[1024,768]{1,0:T(8,128)(2,1)} %hidden.1, ...), custom_call_target="tpu_custom_call" | custom-call | tf_op jit(solution)/shard_map/inner_forward/pallas_call | solution.py:429
  120.2 24.7 %outer_forward.1 = (bf16[1024,768]{1,0:T(8,128)(2,1)}, f32[1024,768]{1,0:T(8,128)}, f32[8,768]{1,0:T(8,128)}, bf16[4,192,384]{2,1,0:T(8,128)(2,1)}, bf16[4,192,3...) custom-call(bf16[1024,3072]{1,0:T(8,128)(2,1)} %get-tuple-element.18, ...), custom_call_target="tpu_custom_call" | custom-call | tf_op jit(solution)/shard_map/outer_forward/pallas_call | solution.py:512
  156.1 27.2 %backward.1 = (bf16[1024,768]{1,0:T(8,128)(2,1)S(1)}, f32[1024,768]{1,0:T(8,128)S(1)}, f32[8,768]{1,0:T(8,128)S(1)}, f32[8,768]{1,0:T(8,128)S(1)}, bf16[4,4,48,1...) custom-call(f32[1024,768]{1,0:T(8,128)} %get-tuple-element.201.refs_0_, ...), custom_call_target="tpu_custom_call" | custom-call | tf_op jit(solution)/shard_map/backward/pallas_call | solution.py:625
  185.5 5.0 %collective-permute-done.31 = bf16[4,4,48,1920]{3,2,1,0:T(8,128)(2,1)S(1)} collective-permute-done((bf16[4,4,48,1920]{3,2,1,0:T(8,128)(2,1)S(1)}, bf16[4,4,48,1920]{3,2,1,0:T(8,128)(2,1)S(1)}, u32[]{:S(2)}, u32[]{:S(2)}) %collective-permute-start.31) | collective-permute-done | bytes 2949152 | tf_op jit(solution)/shard_map/ppermute | solution.py:35
  193.1 4.2 %collective-permute-start.32 = (bf16[2,192,384]{2,1,0:T(8,128)(2,1)S(1)}, bf16[2,192,384]{2,1,0:T(8,128)(2,1)S(1)}, u32[]{:S(2)}, u32[]{:S(2)}) collective-permute-start(bf16[2,192,384]{2,1,0:T(8,128)(2,1)S(1)} %get-tuple-element.242), channel_id=1, source_target_pairs={{0,16},{1,17},{2,18},{3,19},{4,20},{5,21},{6,22},{7,23},{8,24},{9,... | collective-permute-start | bytes 884744 | tf_op jit(solution)/shard_map/ppermute | solution.py:35
  199.0 10.9 %attend_back.2 = (bf16[1024,2304]{1,0:T(8,128)(2,1)S(1)}, f32[1,8,768]{2,1,0:T(8,128)S(1)}) custom-call(bf16[1024,2304]{1,0:T(8,128)(2,1)S(1)} %bitcast.43, bf16[1024,768]{1,0:T(8,128)(2,1)S(1)} %get-tuple-element.225.grad_att, bf16[24,512,512]{2,1,0:T(8,128)(2,1)} %get-tuple-element.226.probs), custom_call_target="tpu_custom_call" | custom-call | tf_op jit(solution)/shard_map/attend_back/pallas_call | solution.py:708
  209.9 11.2 %attend_back.3 = (bf16[1024,2304]{1,0:T(8,128)(2,1)S(1)}, f32[1,8,768]{2,1,0:T(8,128)S(1)}) custom-call(bf16[1024,2304]{1,0:T(8,128)(2,1)S(1)} %bitcast.43, bf16[1024,768]{1,0:T(8,128)(2,1)S(1)} %get-tuple-element.225.grad_att, bf16[24,512,512]{2,1,0:T(8,128)(2,1)} %get-tuple-element.226.probs, ...), custom_call_target="tpu_custom_call", output_to_operand_aliasing={{0}: (3, {})} | custom-call | tf_op jit(solution)/shard_map/attend_back/pallas_call | solution.py:708
  221.1 4.7 %grad_qkv.1 = (bf16[4,48,1280]{2,1,0:T(8,128)(2,1)S(1)}, bf16[4,48,1280]{2,1,0:T(8,128)(2,1)S(1)}, bf16[4,48,1280]{2,1,0:T(8,128)(2,1)S(1)}, bf16[4,48,1280]{2,1...) custom-call(bf16[1024,768]{1,0:T(8,128)(2,1)S(1)} %copy-done.2, ...), custom_call_target="tpu_custom_call" | custom-call | tf_op jit(solution)/shard_map/grad_qkv/pallas_call | solution.py:760
  233.7 3.7 %collective-permute-start.40 = (bf16[2,48,1920]{2,1,0:T(8,128)(2,1)}, bf16[2,48,1920]{2,1,0:T(8,128)(2,1)}, u32[]{:S(2)}, u32[]{:S(2)}) collective-permute-start(bf16[2,48,1920]{2,1,0:T(8,128)(2,1)} %get-tuple-element.270), channel_id=1, source_target_pairs={{0,16},{1,17},{2,18},{3,19},{4,20},{5,21},{6,22},{7,23},{8,24},{9,... | collective-permute-start | bytes 1105928 | tf_op jit(solution)/shard_map/ppermute | solution.py:35
  241.7 2.3 copy-done.1
  245.9 7.6 %grad_hidden.1 = f32[1024,768]{1,0:T(8,128)} custom-call(bf16[1024,2304]{1,0:T(8,128)(2,1)S(1)} %copy-done.1, f32[1024,768]{1,0:T(8,128)S(1)} %copy-done.20, bf16[4,48,1280]{2,1,0:T(8,128)(2,1)S(1)} %copy-done.4, bf16[4,48,1280]{2,1,0:T(8,128)(2,1)S(1)} %copy-done.8, bf16[4,48,1280]{2,1,0:T(8,128)(2,1)S(1)} %copy-done.10, ...), custom_call_target="tpu_custom_call" | custom-call | tf_op jit(solution)/shard_map/grad_hidden/pallas_call | solution.py:790
  258.5 4.6 %collective-permute-done.43.refs_2_ = bf16[4,48,1280]{2,1,0:T(8,128)(2,1)S(1)} collective-permute-done((bf16[4,48,1280]{2,1,0:T(8,128)(2,1)}, bf16[4,48,1280]{2,1,0:T(8,128)(2,1)S(1)}, u32[]{:S(2)}, u32[]{:S(2)}) %collective-permute-start.43) | collective-permute-done | bytes 491552 | tf_op jit(solution)/shard_map/ppermute | solution.py:35
  265.4 2.4 collective-permute-start.49
  270.9 4.0 %collective-permute-done.48 = bf16[48,1280]{1,0:T(8,128)(2,1)S(1)} collective-permute-done((bf16[48,1280]{1,0:T(8,128)(2,1)S(1)}, bf16[48,1280]{1,0:T(8,128)(2,1)S(1)}, u32[]{:S(2)}, u32[]{:S(2)}) %collective-permute-start.48) | collective-permute-done | bytes 122912 | tf_op jit(solution)/shard_map/ppermute | solution.py:35
  (237 shorter events, 78.0 us)
Async XLA Ops:
  7.2 113.0 %all-gather.3.cloned.1.call-start = ((), (), s32[]{:S(2)}) async-start(), calls=%async_computation | async-start | bytes 4866048 | tf_op jit(solution)/shard_map/all_gather | solution.py:844
  13.1 12.0 %collective-permute-start.4 = (bf16[48,1280]{1,0:T(8,128)(2,1)}, bf16[48,1280]{1,0:T(8,128)(2,1)S(1)}, u32[]{:S(2)}, u32[]{:S(2)}) collective-permute-start(bf16[48,1280]{1,0:T(8,128)(2,1)} %pair_up.2), channel_id=1, source_target_pairs={{0,8},{1,9},{2,10},{3,11},{4,12},{5,13},{6,14},{7,15},{8,0},{9,1},... | collective-permute-start | bytes 368648 | tf_op jit(solution)/shard_map/ppermute | solution.py:35
  16.1 12.6 %collective-permute-start.5 = (bf16[48,1280]{1,0:T(8,128)(2,1)}, bf16[48,1280]{1,0:T(8,128)(2,1)S(1)}, u32[]{:S(2)}, u32[]{:S(2)}) collective-permute-start(bf16[48,1280]{1,0:T(8,128)(2,1)} %pair_up.2), channel_id=1, source_target_pairs={{0,16},{1,17},{2,18},{3,19},{4,20},{5,21},{6,22},{7,23},{8,24},{9,... | collective-permute-start | bytes 368648 | tf_op jit(solution)/shard_map/ppermute | solution.py:35
  18.7 10.0 %collective-permute-start.6 = (bf16[48,1280]{1,0:T(8,128)(2,1)}, bf16[48,1280]{1,0:T(8,128)(2,1)S(1)}, u32[]{:S(2)}, u32[]{:S(2)}) collective-permute-start(bf16[48,1280]{1,0:T(8,128)(2,1)} %pair_up.2), channel_id=1, source_target_pairs={{0,24},{1,25},{2,26},{3,27},{4,28},{5,29},{6,30},{7,31},{8,16},{9,... | collective-permute-start | bytes 368648 | tf_op jit(solution)/shard_map/ppermute | solution.py:35
  28.8 20.7 %collective-permute-start.7 = (bf16[4,48,1280]{2,1,0:T(8,128)(2,1)S(1)}, bf16[4,48,1280]{2,1,0:T(8,128)(2,1)S(1)}, u32[]{:S(2)}, u32[]{:S(2)}) collective-permute-start(bf16[4,48,1280]{2,1,0:T(8,128)(2,1)S(1)} %pad_maximum_fusion.1.refs_0_.refs_4_.refs_2_), channel_id=1, source_target_pairs={{0,2},{1,3},{2,0},{3,1},{4,6},{5,7},{6,4},{7,5},{8,10},{9,11},{10,... | collective-permute-start | bytes 1474568 | tf_op jit(solution)/shard_map/ppermute | solution.py:35
  30.4 21.3 %collective-permute-start.8 = (bf16[4,48,1280]{2,1,0:T(8,128)(2,1)S(1)}, bf16[4,48,1280]{2,1,0:T(8,128)(2,1)S(1)}, u32[]{:S(2)}, u32[]{:S(2)}) collective-permute-start(bf16[4,48,1280]{2,1,0:T(8,128)(2,1)S(1)} %pad_maximum_fusion.1.refs_0_.refs_4_.refs_2_), channel_id=1, source_target_pairs={{0,4},{1,5},{2,6},{3,7},{4,0},{5,1},{6,2},{7,3},{8,12},{9,13},{10,... | collective-permute-start | bytes 1474568 | tf_op jit(solution)/shard_map/ppermute | solution.py:35
  31.9 19.8 %collective-permute-start.9 = (bf16[4,48,1280]{2,1,0:T(8,128)(2,1)S(1)}, bf16[4,48,1280]{2,1,0:T(8,128)(2,1)S(1)}, u32[]{:S(2)}, u32[]{:S(2)}) collective-permute-start(bf16[4,48,1280]{2,1,0:T(8,128)(2,1)S(1)} %pad_maximum_fusion.1.refs_0_.refs_4_.refs_2_), channel_id=1, source_target_pairs={{0,6},{1,7},{2,4},{3,5},{4,2},{5,3},{6,0},{7,1},{8,14},{9,15},{10,... | collective-permute-start | bytes 1474568 | tf_op jit(solution)/shard_map/ppermute | solution.py:35
  34.4 15.0 %collective-permute-start.11 = (bf16[48,1920]{1,0:T(8,128)(2,1)S(1)}, bf16[48,1920]{1,0:T(8,128)(2,1)S(1)}, u32[]{:S(2)}, u32[]{:S(2)}) collective-permute-start(bf16[48,1920]{1,0:T(8,128)(2,1)S(1)} %pad_maximum_fusion.4), channel_id=1, source_target_pairs={{0,16},{1,17},{2,18},{3,19},{4,20},{5,21},{6,22},{7,23},{8,24},{9,... | collective-permute-start | bytes 552968 | tf_op jit(solution)/shard_map/ppermute | solution.py:35
  53.5 30.6 %collective-permute-start.17 = (bf16[4,48,1920]{2,1,0:T(8,128)(2,1)S(1)}, bf16[4,48,1920]{2,1,0:T(8,128)(2,1)}, u32[]{:S(2)}, u32[]{:S(2)}) collective-permute-start(bf16[4,48,1920]{2,1,0:T(8,128)(2,1)S(1)} %pad_maximum_fusion.refs_3_.refs_7_), channel_id=1, source_target_pairs={{0,2},{1,3},{2,0},{3,1},{4,6},{5,7},{6,4},{7,5},{8,10},{9,11},{10,... | collective-permute-start | bytes 2211848 | tf_op jit(solution)/shard_map/ppermute | solution.py:35
  54.8 29.4 %collective-permute-start.18 = (bf16[4,48,1920]{2,1,0:T(8,128)(2,1)S(1)}, bf16[4,48,1920]{2,1,0:T(8,128)(2,1)}, u32[]{:S(2)}, u32[]{:S(2)}) collective-permute-start(bf16[4,48,1920]{2,1,0:T(8,128)(2,1)S(1)} %pad_maximum_fusion.refs_3_.refs_7_), channel_id=1, source_target_pairs={{0,4},{1,5},{2,6},{3,7},{4,0},{5,1},{6,2},{7,3},{8,12},{9,13},{10,... | collective-permute-start | bytes 2211848 | tf_op jit(solution)/shard_map/ppermute | solution.py:35
  55.6 38.5 %collective-permute-start.19 = (bf16[4,48,1920]{2,1,0:T(8,128)(2,1)S(1)}, bf16[4,48,1920]{2,1,0:T(8,128)(2,1)}, u32[]{:S(2)}, u32[]{:S(2)}) collective-permute-start(bf16[4,48,1920]{2,1,0:T(8,128)(2,1)S(1)} %pad_maximum_fusion.refs_3_.refs_7_), channel_id=1, source_target_pairs={{0,6},{1,7},{2,4},{3,5},{4,2},{5,3},{6,0},{7,1},{8,14},{9,15},{10,... | collective-permute-start | bytes 2211848 | tf_op jit(solution)/shard_map/ppermute | solution.py:35
  152.5 32.5 %collective-permute-start.28 = (bf16[4,192,384]{2,1,0:T(8,128)(2,1)S(1)}, bf16[4,192,384]{2,1,0:T(8,128)(2,1)S(1)}, u32[]{:S(2)}, u32[]{:S(2)}) collective-permute-start(bf16[4,192,384]{2,1,0:T(8,128)(2,1)S(1)} %add_convert_fusion.6), channel_id=1, source_target_pairs={{0,2},{1,3},{2,0},{3,1},{4,6},{5,7},{6,4},{7,5},{8,10},{9,11},{10,... | collective-permute-start | bytes 1769480 | tf_op jit(solution)/shard_map/ppermute | solution.py:35
  153.7 31.4 %collective-permute-start.29 = (bf16[4,192,384]{2,1,0:T(8,128)(2,1)S(1)}, bf16[4,192,384]{2,1,0:T(8,128)(2,1)S(1)}, u32[]{:S(2)}, u32[]{:S(2)}) collective-permute-start(bf16[4,192,384]{2,1,0:T(8,128)(2,1)S(1)} %add_convert_fusion.5), channel_id=1, source_target_pairs={{0,4},{1,5},{2,6},{3,7},{4,0},{5,1},{6,2},{7,3},{8,12},{9,13},{10,... | collective-permute-start | bytes 1769480 | tf_op jit(solution)/shard_map/ppermute | solution.py:35
  154.4 30.6 %collective-permute-start.30 = (bf16[4,192,384]{2,1,0:T(8,128)(2,1)S(1)}, bf16[4,192,384]{2,1,0:T(8,128)(2,1)S(1)}, u32[]{:S(2)}, u32[]{:S(2)}) collective-permute-start(bf16[4,192,384]{2,1,0:T(8,128)(2,1)S(1)} %add_convert_fusion.4), channel_id=1, source_target_pairs={{0,6},{1,7},{2,4},{3,5},{4,2},{5,3},{6,0},{7,1},{8,14},{9,15},{10,... | collective-permute-start | bytes 1769480 | tf_op jit(solution)/shard_map/ppermute | solution.py:35
  191.2 34.7 %collective-permute-start.33 = (bf16[4,48,1920]{2,1,0:T(8,128)(2,1)S(1)}, bf16[4,48,1920]{2,1,0:T(8,128)(2,1)S(1)}, u32[]{:S(2)}, u32[]{:S(2)}) collective-permute-start(bf16[4,48,1920]{2,1,0:T(8,128)(2,1)S(1)} %get-tuple-element.243), channel_id=1, source_target_pairs={{0,2},{1,3},{2,0},{3,1},{4,6},{5,7},{6,4},{7,5},{8,10},{9,11},{10,... | collective-permute-start | bytes 2211848 | tf_op jit(solution)/shard_map/ppermute | solution.py:35
  192.4 34.0 %collective-permute-start.34 = (bf16[4,48,1920]{2,1,0:T(8,128)(2,1)S(1)}, bf16[4,48,1920]{2,1,0:T(8,128)(2,1)S(1)}, u32[]{:S(2)}, u32[]{:S(2)}) collective-permute-start(bf16[4,48,1920]{2,1,0:T(8,128)(2,1)S(1)} %get-tuple-element.244), channel_id=1, source_target_pairs={{0,4},{1,5},{2,6},{3,7},{4,0},{5,1},{6,2},{7,3},{8,12},{9,13},{10,... | collective-permute-start | bytes 2211848 | tf_op jit(solution)/shard_map/ppermute | solution.py:35
  193.1 32.8 %collective-permute-start.32 = (bf16[2,192,384]{2,1,0:T(8,128)(2,1)S(1)}, bf16[2,192,384]{2,1,0:T(8,128)(2,1)S(1)}, u32[]{:S(2)}, u32[]{:S(2)}) collective-permute-start(bf16[2,192,384]{2,1,0:T(8,128)(2,1)S(1)} %get-tuple-element.242), channel_id=1, source_target_pairs={{0,16},{1,17},{2,18},{3,19},{4,20},{5,21},{6,22},{7,23},{8,24},{9,... | collective-permute-start | bytes 884744 | tf_op jit(solution)/shard_map/ppermute | solution.py:35
  197.2 33.7 %collective-permute-start.39 = (bf16[4,48,1920]{2,1,0:T(8,128)(2,1)S(1)}, bf16[4,48,1920]{2,1,0:T(8,128)(2,1)S(1)}, u32[]{:S(2)}, u32[]{:S(2)}) collective-permute-start(bf16[4,48,1920]{2,1,0:T(8,128)(2,1)S(1)} %get-tuple-element.260), channel_id=1, source_target_pairs={{0,6},{1,7},{2,4},{3,5},{4,2},{5,3},{6,0},{7,1},{8,14},{9,15},{10,... | collective-permute-start | bytes 2211848 | tf_op jit(solution)/shard_map/ppermute | solution.py:35
  233.7 20.8 %collective-permute-start.40 = (bf16[2,48,1920]{2,1,0:T(8,128)(2,1)}, bf16[2,48,1920]{2,1,0:T(8,128)(2,1)}, u32[]{:S(2)}, u32[]{:S(2)}) collective-permute-start(bf16[2,48,1920]{2,1,0:T(8,128)(2,1)} %get-tuple-element.270), channel_id=1, source_target_pairs={{0,16},{1,17},{2,18},{3,19},{4,20},{5,21},{6,22},{7,23},{8,24},{9,... | collective-permute-start | bytes 1105928 | tf_op jit(solution)/shard_map/ppermute | solution.py:35
  238.1 15.4 %collective-permute-start.41 = (bf16[192,384]{1,0:T(8,128)(2,1)}, bf16[192,384]{1,0:T(8,128)(2,1)}, u32[]{:S(2)}, u32[]{:S(2)}) collective-permute-start(bf16[192,384]{1,0:T(8,128)(2,1)} %get-tuple-element.307), channel_id=1, source_target_pairs={{0,8},{1,9},{2,10},{3,11},{4,12},{5,13},{6,14},{7,15},{8,0},{9,1},... | collective-permute-start | bytes 442376 | tf_op jit(solution)/shard_map/ppermute | solution.py:35
  238.1 20.3 %collective-permute-start.42 = (bf16[4,48,1280]{2,1,0:T(8,128)(2,1)}, bf16[4,48,1280]{2,1,0:T(8,128)(2,1)S(1)}, u32[]{:S(2)}, u32[]{:S(2)}) collective-permute-start(bf16[4,48,1280]{2,1,0:T(8,128)(2,1)} %copy-done.42), channel_id=1, source_target_pairs={{0,2},{1,3},{2,0},{3,1},{4,6},{5,7},{6,4},{7,5},{8,10},{9,11},{10,... | collective-permute-start | bytes 1474568 | tf_op jit(solution)/shard_map/ppermute | solution.py:35
  239.6 23.4 %collective-permute-start.43 = (bf16[4,48,1280]{2,1,0:T(8,128)(2,1)}, bf16[4,48,1280]{2,1,0:T(8,128)(2,1)S(1)}, u32[]{:S(2)}, u32[]{:S(2)}) collective-permute-start(bf16[4,48,1280]{2,1,0:T(8,128)(2,1)} %copy-done.41), channel_id=1, source_target_pairs={{0,4},{1,5},{2,6},{3,7},{4,0},{5,1},{6,2},{7,3},{8,12},{9,13},{10,... | collective-permute-start | bytes 1474568 | tf_op jit(solution)/shard_map/ppermute | solution.py:35
  240.1 22.9 %collective-permute-start.44 = (bf16[4,48,1280]{2,1,0:T(8,128)(2,1)}, bf16[4,48,1280]{2,1,0:T(8,128)(2,1)S(1)}, u32[]{:S(2)}, u32[]{:S(2)}) collective-permute-start(bf16[4,48,1280]{2,1,0:T(8,128)(2,1)} %copy-done.40), channel_id=1, source_target_pairs={{0,6},{1,7},{2,4},{3,5},{4,2},{5,3},{6,0},{7,1},{8,14},{9,15},{10,... | collective-permute-start | bytes 1474568 | tf_op jit(solution)/shard_map/ppermute | solution.py:35
  255.6 12.2 %collective-permute-start.45 = (bf16[48,1920]{1,0:T(8,128)(2,1)S(1)}, bf16[48,1920]{1,0:T(8,128)(2,1)S(1)}, u32[]{:S(2)}, u32[]{:S(2)}) collective-permute-start(bf16[48,1920]{1,0:T(8,128)(2,1)S(1)} %get-tuple-element.304), channel_id=1, source_target_pairs={{0,8},{1,9},{2,10},{3,11},{4,12},{5,13},{6,14},{7,15},{8,0},{9,1},... | collective-permute-start | bytes 552968 | tf_op jit(solution)/shard_map/ppermute | solution.py:35
  (82 other events, 561.8 us)
Sparse Core Ops, SparseCore 0:
  51.8 68.0 all-gather.2

commit v3 on v2

--- a/solution.py
+++ b/solution.py
@@ -410,7 +410,7 @@
     n1, r1 = normalize(hidden[...].astype(f32) + dot(att[...], w_out[...]) + row(2))
     low = (n1 * row(3) + row(4)).astype(bf16)
     first_low[...] = low
-    normed[...] = n1
+    normed[...] = n1.astype(bf16)
     inverse[...] = jnp.broadcast_to(r1, inverse.shape)
 
     @pl.when(first_step)
@@ -433,7 +433,7 @@
         out_specs=[tile(D), tile(D), tile(128), tile(FF), tile(FF)],
         out_shape=[
             Shape((tokens, D), bf16),
-            Shape((tokens, D), f32),
+            Shape((tokens, D), bf16),
             Shape((tokens, 128), f32),
             Shape((tokens, FF), bf16),
             Shape((tokens, FF), bf16),
@@ -468,12 +468,12 @@
 
     here = pl.ds(pl.multiple_of(step * TILE, TILE), TILE)
     activated[here, :] = act[...]
-    outward = normed[...] * row(3) + row(4) + dot(act[...], w_back[...]) + row(9)
+    outward = normed[...].astype(f32) * row(3) + row(4) + dot(act[...], w_back[...]) + row(9)
     n2, r2 = normalize(outward)
     output[...] = (n2 * row(10) + row(11)).astype(bf16)
     cot = cotangent[...].astype(f32)
     g2 = normalize_back(cot * row(10), n2, r2)
-    grad_second[...] = g2
+    grad_second[...] = g2.astype(bf16)
     part = rows_of(8, column_sum(g2), column_sum(cot * n2), column_sum(cot))
 
     @pl.when(step == 0)
@@ -516,7 +516,7 @@
         out_specs=[tile(D), tile(D), fixed((8, D))] + [fixed((4, 192, 384))] * 8,
         out_shape=[
             Shape((tokens, D), bf16),
-            Shape((tokens, D), f32),
+            Shape((tokens, D), bf16),
             Shape((8, D), f32),
         ]
         + [Shape((4, 192, 384), bf16)] * 8,
@@ -526,7 +526,7 @@
             pltpu.VMEM((D, tokens), bf16),
             pltpu.SemaphoreType.DMA((32,)),
         ],
-        compiler_params=params(60),
+        compiler_params=params(40),
         cost_estimate=cost(18),
         name="outer_forward",
     )(activated, normed, cotangent, vectors, back_table)
@@ -535,9 +535,10 @@
 def backward_kernel(place, *refs):
     grad_second, slope, normed, inverse, first_low, att_t, vectors = refs[:7]
     blocks, back_table = refs[7:15], refs[15]
-    grad_att, grad_branch, sums, sums_inner, kept, sent = refs[16:22]
-    w_in, w_out, w_back, inner_low, first_t, grad_low, turned = refs[22:29]
-    in_sems, out_sems, back_sems = refs[29:]
+    grad_att, grad_branch, sums, sums_inner = refs[16:20]
+    outs = refs[20:28]
+    w_in, w_out, w_back, inner_low, first_t, grad_low, turned = refs[28:35]
+    in_sems, out_sems, back_sems = refs[35:]
     step = pl.program_id(0)
     z, y, x, core = place()
     here = pl.ds(pl.multiple_of(step * TILE, TILE), TILE)
@@ -550,9 +551,8 @@
             start(copies_back)
             start(copies_in)
             start(copies_out)
-        g2 = grad_second[...]
-        g2_low = g2.astype(bf16)
-        grad_first = g2
+        g2_low = grad_second[...]
+        grad_first = g2_low.astype(f32)
         inner_sums = []
         for c in range(FF // D):
             columns = slice(c * D, c * D + D)
@@ -565,10 +565,10 @@
             if first_step and c == 0:
                 wait(copies_in)
             grad_first = grad_first + dot_t(gi, w_in[:, columns])
-        n1 = normed[...]
+        n1 = normed[...].astype(f32)
         g1 = normalize_back(grad_first * vectors[3:4, :], n1, inverse[:, :1])
-        grad_branch[...] = g1
         g1_low = g1.astype(bf16)
+        grad_branch[...] = g1_low
         grad_low[here, :] = g1_low
         if first_step:
             wait(copies_out)
@@ -599,29 +599,33 @@
     @pl.when(step == pl.num_programs(0) - 1)
     def _():
         for i in range(2):
-            for other, out in enumerate((kept, sent)):
+            for other in range(2):
                 at = ((x ^ i) * 2 + (core ^ other)) * D
                 res = dot(first_t[...], inner_low[:, pl.ds(pl.multiple_of(at, D), D)])
                 res = res.astype(bf16)
                 for j in range(2):
                     for k in range(4):
                         at = (j * 4 + k) * 96
-                        out[i + 2 * j, k, :, :D] = res[at : at + 48]
-                        out[i + 2 * j, k, :, D : 2 * D] = res[at + 48 : at + 96]
+                        outs[other * 4 + i + 2 * j][k, :, :D] = res[at : at + 48]
+                        outs[other * 4 + i + 2 * j][k, :, D : 2 * D] = res[at + 48 : at + 96]
         res = dot(turned[...], grad_low[...]).astype(bf16)
-        for other, out in enumerate((kept, sent)):
-            for j in range(2):
-                for k in range(4):
-                    at = (other * 8 + j * 4 + k) * 48
-                    for half in range(2):
-                        piece = res[at : at + 48, half * 384 : half * 384 + 384]
-                        out[(half ^ x) + 2 * j, k, :, 2 * D :] = piece
+        for bit in range(2):
+
+            @pl.when(x == bit)
+            def _(bit=bit):
+                for other in range(2):
+                    for j in range(2):
+                        for k in range(4):
+                            at = (other * 8 + j * 4 + k) * 48
+                            for half in range(2):
+                                piece = res[at : at + 48, half * 384 : half * 384 + 384]
+                                outs[other * 4 + (half ^ bit) + 2 * j][k, :, 2 * D :] = piece
 
 
 def backward(place, grad_second, slope, normed, inverse, first_low, att_t, vectors, *weights):
     blocks, back_table = weights
     tokens = normed.shape[0]
-    outs = [(4, 4, 48, 1920)] * 2
+    outs = [(4, 48, 1920)] * 8
     return pl.pallas_call(
         functools.partial(backward_kernel, place),
         grid=(tokens // TILE,),
@@ -629,7 +633,7 @@
         + [pl.BlockSpec((D, TILE), lambda i: (0, i)), fixed((12, D))]
         + anywhere(9),
         out_specs=[tile(D), tile(D)] + [fixed(s) for s in [(8, D)] * 2 + outs],
-        out_shape=[Shape((tokens, D), bf16), Shape((tokens, D), f32)]
+        out_shape=[Shape((tokens, D), bf16), Shape((tokens, D), bf16)]
         + [Shape((8, D), f32)] * 2
         + [Shape(s, bf16) for s in outs],
         scratch_shapes=[
@@ -782,7 +786,7 @@
         start(copies)
         wait(copies)
 
-    out[...] = grad_branch[...] + dot_t(low[...], weight[...])
+    out[...] = grad_branch[...].astype(f32) + dot_t(low[...], weight[...])
 
 
 def grad_of_hidden(place, low, grad_branch, blocks):
@@ -794,7 +798,7 @@
         out_specs=tile(D),
         out_shape=Shape((tokens, D), f32),
         scratch_shapes=[pltpu.VMEM((D, 3 * D), bf16), pltpu.SemaphoreType.DMA((32,))],
-        compiler_params=params(32),
+        compiler_params=params(60),
         cost_estimate=cost(9),
         name="grad_hidden",
     )(low, grad_branch, *blocks)
@@ -875,11 +879,11 @@
         back_table,
     )
     back_outs, others_back = tie(back_outs, others_back)
-    grad_att, grad_branch, sums_first, sums_inner, kept_mid, sent_mid = back_outs
-
-    received_mid = send(sent_mid, core=1)
+    grad_att, grad_branch, sums_first, sums_inner, *tables_mid = back_outs
+
+    received_mid = [send(block, core=1) for block in tables_mid[4:]]
     near_back, far_back = line_halves(parts_back[0], others_back)
-    parts_mid = chip_parts(kept_mid, received_mid)
+    parts_mid = chip_parts(tables_mid[:4], received_mid)
     parts_mid, grad_att, near_back, far_back = tie(parts_mid, grad_att, near_back, far_back)
 
     plane_mid = [send(parts_mid[1], x=1), send(parts_mid[2], y=1)]
@@ -956,7 +960,7 @@
         mid_blocks,
         back_pieces,
     )
-    mid_table = jnp.stack(tables)
+    mid_table = jnp.stack(tables).reshape(2, 4, 4, 48, 1920)
     packed_low, sums_zero = attend_back(0, packed, grad_att, probs)
     packed_low, sums_one = attend_back(1, packed, grad_att, probs, packed_low)
     grad_hidden = grad_of_hidden(origin, packed_low, grad_branch, qkv_blocks)

time: 288 us -> 281 us (0.976)
  waiting for transfers between devices: 55.4 us -> 61.2 us
  other arithmetic: 16.8 us -> 11 us
  Pallas kernels: 134 us -> 131 us
    convert_element_type x5 -> x8, other arithmetic: 5.96 us -> 1.29 us  [chip_parts(): return [wide_sum(kept[s], received[s]).astype(bf16) for s in range(4)]]
    ppermute x51 -> x54, waiting for transfers between devices: 55.3 us -> 60 us  [send(): return lax.ppermute(values, ALL, pairs)]
    pallas_call x1, Pallas kernels: 24.7 us -> 20.2 us  [outer_forward(): pl.pallas_call(functools.partial(outer_kernel, place), grid=(tokens // TI...]
    ppermute x51 -> x54, starting transfers between devices: 47.3 us -> 44.9 us  [send(): return lax.ppermute(values, ALL, pairs)]
    unnamed x111 -> x81, local copies, waits for them, and re-layouts: 12.6 us -> 10.9 us
  transfers between devices with their start and end apart: 52 -> 55, of which waited for: 23 -> 30; matrix products, arithmetic and copies ran while one was open for 6% -> 5% of each run, Pallas kernels for 38% -> 40%
where the time goes in v3:
time: 281 us; the launch traced here: 277 us
  Pallas kernels  131 us (47%)
  waiting for transfers between devices  61.2 us (22%)
  starting transfers between devices  45 us (16%)
  between operations  14.9 us (5%)
  local copies, waits for them, and re-layouts  13.6 us (5%)
  other arithmetic  11 us (4%)
    ppermute x54, waiting for transfers between devices, send(): return lax.ppermute(values, ALL, pairs)  60 us
    ppermute x54, starting transfers between devices, send(): return lax.ppermute(values, ALL, pairs)  44.9 us
    pallas_call x1, Pallas kernels, backward(): pl.pallas_call(functools.partial(backward_kernel, place), grid=(tokens //...  26.6 us
    pallas_call x2, Pallas kernels, attend_back(): pl.pallas_call(kernel, grid=(1,), in_specs=[pl.BlockSpec((length, 3 * D),...  22.1 us
    pallas_call x1, Pallas kernels, attend(): pl.pallas_call(functools.partial(attend_kernel, place), grid=(rows,), in_...  21.2 us
    pallas_call x1, Pallas kernels, outer_forward(): pl.pallas_call(functools.partial(outer_kernel, place), grid=(tokens // TI...  20.2 us
    pallas_call x1, Pallas kernels, inner_forward(): pl.pallas_call(functools.partial(inner_kernel, place), grid=(tokens // TI...  19.6 us
    unnamed x81, local copies, waits for them, and re-layouts  10.9 us
  transfers between devices with their start and end apart: 55, of which 30 were waited for; matrix products, arithmetic and copies ran while one was open for 5% of the time, Pallas kernels for 40%

profile of v3, /device:TPU:0, one launch (start us, length us, event | category | flops | bytes accessed | tf_op | source)
XLA Modules:
  0.0 277.1 jit_solution(12645733850892450313)
XLA Ops:
  13.1 3.1 %collective-permute-start.4 = (bf16[48,1280]{1,0:T(8,128)(2,1)}, bf16[48,1280]{1,0:T(8,128)(2,1)S(1)}, u32[]{:S(2)}, u32[]{:S(2)}) collective-permute-start(bf16[48,1280]{1,0:T(8,128)(2,1)} %pair_up.2), channel_id=1, source_target_pairs={{0,8},{1,9},{2,10},{3,11},{4,12},{5,13},{6,14},{7,15},{8,0},{9,1},... | collective-permute-start | bytes 368648 | tf_op jit(solution)/shard_map/ppermute | solution.py:35
  16.1 2.6 collective-permute-start.5
  20.9 2.1 pair_up.3
  25.1 3.6 %collective-permute-done.5 = bf16[48,1280]{1,0:T(8,128)(2,1)S(1)} collective-permute-done((bf16[48,1280]{1,0:T(8,128)(2,1)}, bf16[48,1280]{1,0:T(8,128)(2,1)S(1)}, u32[]{:S(2)}, u32[]{:S(2)}) %collective-permute-start.5) | collective-permute-done | bytes 122912 | tf_op jit(solution)/shard_map/ppermute | solution.py:35
  35.4 4.8 %collective-permute-done.10 = bf16[48,1920]{1,0:T(8,128)(2,1)S(1)} collective-permute-done((bf16[48,1920]{1,0:T(8,128)(2,1)S(1)}, bf16[48,1920]{1,0:T(8,128)(2,1)S(1)}, u32[]{:S(2)}, u32[]{:S(2)}) %collective-permute-start.10) | collective-permute-done | bytes 184352 | tf_op jit(solution)/shard_map/ppermute | solution.py:35
  42.0 7.4 %collective-permute-done.11 = bf16[48,1920]{1,0:T(8,128)(2,1)S(1)} collective-permute-done((bf16[48,1920]{1,0:T(8,128)(2,1)S(1)}, bf16[48,1920]{1,0:T(8,128)(2,1)S(1)}, u32[]{:S(2)}, u32[]{:S(2)}) %collective-permute-start.11) | collective-permute-done | bytes 184352 | tf_op jit(solution)/shard_map/ppermute | solution.py:35
  49.4 2.3 collective-permute-done.8.refs_2_.refs_6_.refs_4_
  62.8 21.2 %attend.1 = (bf16[1024,2304]{1,0:T(8,128)(2,1)}, bf16[1024,768]{1,0:T(8,128)(2,1)}, bf16[768,1024]{1,0:T(8,128)(2,1)}, bf16[24,512,512]{2,1,0:T(8,128)(2,1)}) custom-call(bf16[1024,768]{1,0:T(8,128)(2,1)} %hidden.1, f32[12,768]{1,0:T(8,128)} %reshape.44.refs_1_.refs_2_.refs_3_.refs_6_, bf16[1024,128]{1,0:T(8,128)(2,1)} %add_convert_fusion.8.refs_2_, ...), custom_call_target="tpu_custom_call" | custom-call | tf_op jit(solution)/shard_map/attend/pallas_call | solution.py:362
  84.0 9.7 %collective-permute-done.19.refs_6_.refs_10_ = bf16[4,48,1920]{2,1,0:T(8,128)(2,1)S(1)} collective-permute-done((bf16[4,48,1920]{2,1,0:T(8,128)(2,1)S(1)}, bf16[4,48,1920]{2,1,0:T(8,128)(2,1)S(1)}, u32[]{:S(2)}, u32[]{:S(2)}) %collective-permute-start.19) | collective-permute-done | bytes 737312 | tf_op jit(solution)/shard_map/ppermute | solution.py:35
  96.0 2.1 collective-permute-done.21.refs_8_.refs_12_
  100.0 19.6 %inner_forward.1 = (bf16[1024,768]{1,0:T(8,128)(2,1)}, bf16[1024,768]{1,0:T(8,128)(2,1)}, f32[1024,128]{1,0:T(8,128)}, bf16[1024,3072]{1,0:T(8,128)(2,1)}, bf16[1024,3072]{1,0:T(8,128)(2,1)}) custom-call(bf16[1024,768]{1,0:T(8,128)(2,1)} %get-tuple-element.188.refs_0_, bf16[1024,768]{1,0:T(8,128)(2,1)} %hidden.1, ...), custom_call_target="tpu_custom_call" | custom-call | tf_op jit(solution)/shard_map/inner_forward/pallas_call | solution.py:429
  120.8 2.3 copy-done.1
  126.0 20.2 %outer_forward.1 = (bf16[1024,768]{1,0:T(8,128)(2,1)}, bf16[1024,768]{1,0:T(8,128)(2,1)S(1)}, f32[8,768]{1,0:T(8,128)S(1)}, bf16[4,192,384]{2,1,0:T(8,128)(2,1)S...) custom-call(bf16[1024,3072]{1,0:T(8,128)(2,1)} %get-tuple-element.19, ...), custom_call_target="tpu_custom_call" | custom-call | tf_op jit(solution)/shard_map/outer_forward/pallas_call | solution.py:512
  154.6 26.6 %backward.1 = (bf16[1024,768]{1,0:T(8,128)(2,1)S(1)}, bf16[1024,768]{1,0:T(8,128)(2,1)S(1)}, f32[8,768]{1,0:T(8,128)S(1)}, f32[8,768]{1,0:T(8,128)S(1)}, bf16[4,...) custom-call(bf16[1024,768]{1,0:T(8,128)(2,1)S(1)} %get-tuple-element, ...), custom_call_target="tpu_custom_call" | custom-call | tf_op jit(solution)/shard_map/backward/pallas_call | solution.py:629
  188.9 2.4 collective-permute-start.35
  193.4 10.9 %attend_back.2 = (bf16[1024,2304]{1,0:T(8,128)(2,1)S(1)}, f32[1,8,768]{2,1,0:T(8,128)S(1)}) custom-call(bf16[1024,2304]{1,0:T(8,128)(2,1)S(1)} %bitcast.37, bf16[1024,768]{1,0:T(8,128)(2,1)S(1)} %get-tuple-element.249.grad_att, bf16[24,512,512]{2,1,0:T(8,128)(2,1)} %get-tuple-element.250.probs), custom_call_target="tpu_custom_call" | custom-call | tf_op jit(solution)/shard_map/attend_back/pallas_call | solution.py:712
  204.4 11.2 %attend_back.3 = (bf16[1024,2304]{1,0:T(8,128)(2,1)S(1)}, f32[1,8,768]{2,1,0:T(8,128)S(1)}) custom-call(bf16[1024,2304]{1,0:T(8,128)(2,1)S(1)} %bitcast.37, bf16[1024,768]{1,0:T(8,128)(2,1)S(1)} %get-tuple-element.249.grad_att, bf16[24,512,512]{2,1,0:T(8,128)(2,1)} %get-tuple-element.250.probs, ...), custom_call_target="tpu_custom_call", output_to_operand_aliasing={{0}: (3, {})} | custom-call | tf_op jit(solution)/shard_map/attend_back/pallas_call | solution.py:712
  215.6 4.7 %grad_qkv.1 = (bf16[4,48,1280]{2,1,0:T(8,128)(2,1)S(1)}, bf16[4,48,1280]{2,1,0:T(8,128)(2,1)S(1)}, bf16[4,48,1280]{2,1,0:T(8,128)(2,1)S(1)}, bf16[4,48,1280]{2,1...) custom-call(bf16[1024,768]{1,0:T(8,128)(2,1)S(1)} %copy-done.2, ...), custom_call_target="tpu_custom_call" | custom-call | tf_op jit(solution)/shard_map/grad_qkv/pallas_call | solution.py:764
  227.8 2.4 collective-permute-start.43
  234.7 9.7 %grad_hidden.1 = f32[1024,768]{1,0:T(8,128)} custom-call(bf16[1024,2304]{1,0:T(8,128)(2,1)} %copy-done, bf16[1024,768]{1,0:T(8,128)(2,1)} %copy-done.19, bf16[4,48,1280]{2,1,0:T(8,128)(2,1)} %copy-done.25, bf16[4,48,1280]{2,1,0:T(8,128)(2,1)} %collective-permute-done.7.refs_1_.refs_5_.refs_3_, bf16[4,48,1280]{2,1,0:T(8,128)(2,1)} %copy-done.26, ...), custom_call_target="tpu_custom_call" | custom-call | tf_op jit(solution)/shard_map/grad_hidden/pallas_call | solution.py:794
  244.5 3.1 %collective-permute-done.43 = bf16[2,48,1920]{2,1,0:T(8,128)(2,1)} collective-permute-done((bf16[2,48,1920]{2,1,0:T(8,128)(2,1)}, bf16[2,48,1920]{2,1,0:T(8,128)(2,1)}, u32[]{:S(2)}, u32[]{:S(2)}) %collective-permute-start.43) | collective-permute-done | bytes 368672 | tf_op jit(solution)/shard_map/ppermute | solution.py:35
  250.4 5.0 %collective-permute-done.46.refs_2_ = bf16[4,48,1280]{2,1,0:T(8,128)(2,1)S(1)} collective-permute-done((bf16[4,48,1280]{2,1,0:T(8,128)(2,1)S(1)}, bf16[4,48,1280]{2,1,0:T(8,128)(2,1)S(1)}, u32[]{:S(2)}, u32[]{:S(2)}) %collective-permute-start.46) | collective-permute-done | bytes 491552 | tf_op jit(solution)/shard_map/ppermute | solution.py:35
  257.8 2.4 collective-permute-start.52
  262.6 5.1 %collective-permute-done.51 = bf16[48,1280]{1,0:T(8,128)(2,1)S(1)} collective-permute-done((bf16[48,1280]{1,0:T(8,128)(2,1)S(1)}, bf16[48,1280]{1,0:T(8,128)(2,1)S(1)}, u32[]{:S(2)}, u32[]{:S(2)}) %collective-permute-start.51) | collective-permute-done | bytes 122912 | tf_op jit(solution)/shard_map/ppermute | solution.py:35
  (216 shorter events, 77.7 us)
Async XLA Ops:
  7.2 113.7 %all-gather.3.cloned.1.call-start = ((), (), s32[]{:S(2)}) async-start(), calls=%async_computation | async-start | bytes 4866048 | tf_op jit(solution)/shard_map/all_gather | solution.py:848
  13.1 12.0 %collective-permute-start.4 = (bf16[48,1280]{1,0:T(8,128)(2,1)}, bf16[48,1280]{1,0:T(8,128)(2,1)S(1)}, u32[]{:S(2)}, u32[]{:S(2)}) collective-permute-start(bf16[48,1280]{1,0:T(8,128)(2,1)} %pair_up.2), channel_id=1, source_target_pairs={{0,8},{1,9},{2,10},{3,11},{4,12},{5,13},{6,14},{7,15},{8,0},{9,1},... | collective-permute-start | bytes 368648 | tf_op jit(solution)/shard_map/ppermute | solution.py:35
  16.1 12.6 %collective-permute-start.5 = (bf16[48,1280]{1,0:T(8,128)(2,1)}, bf16[48,1280]{1,0:T(8,128)(2,1)S(1)}, u32[]{:S(2)}, u32[]{:S(2)}) collective-permute-start(bf16[48,1280]{1,0:T(8,128)(2,1)} %pair_up.2), channel_id=1, source_target_pairs={{0,16},{1,17},{2,18},{3,19},{4,20},{5,21},{6,22},{7,23},{8,24},{9,... | collective-permute-start | bytes 368648 | tf_op jit(solution)/shard_map/ppermute | solution.py:35
  28.8 20.6 %collective-permute-start.7 = (bf16[4,48,1280]{2,1,0:T(8,128)(2,1)S(1)}, bf16[4,48,1280]{2,1,0:T(8,128)(2,1)}, u32[]{:S(2)}, u32[]{:S(2)}) collective-permute-start(bf16[4,48,1280]{2,1,0:T(8,128)(2,1)S(1)} %pad_maximum_fusion.1.refs_0_.refs_4_.refs_2_), channel_id=1, source_target_pairs={{0,2},{1,3},{2,0},{3,1},{4,6},{5,7},{6,4},{7,5},{8,10},{9,11},{10,... | collective-permute-start | bytes 1474568 | tf_op jit(solution)/shard_map/ppermute | solution.py:35
  30.4 21.3 %collective-permute-start.8 = (bf16[4,48,1280]{2,1,0:T(8,128)(2,1)S(1)}, bf16[4,48,1280]{2,1,0:T(8,128)(2,1)S(1)}, u32[]{:S(2)}, u32[]{:S(2)}) collective-permute-start(bf16[4,48,1280]{2,1,0:T(8,128)(2,1)S(1)} %pad_maximum_fusion.1.refs_0_.refs_4_.refs_2_), channel_id=1, source_target_pairs={{0,4},{1,5},{2,6},{3,7},{4,0},{5,1},{6,2},{7,3},{8,12},{9,13},{10,... | collective-permute-start | bytes 1474568 | tf_op jit(solution)/shard_map/ppermute | solution.py:35
  31.9 20.6 %collective-permute-start.9 = (bf16[4,48,1280]{2,1,0:T(8,128)(2,1)S(1)}, bf16[4,48,1280]{2,1,0:T(8,128)(2,1)}, u32[]{:S(2)}, u32[]{:S(2)}) collective-permute-start(bf16[4,48,1280]{2,1,0:T(8,128)(2,1)S(1)} %pad_maximum_fusion.1.refs_0_.refs_4_.refs_2_), channel_id=1, source_target_pairs={{0,6},{1,7},{2,4},{3,5},{4,2},{5,3},{6,0},{7,1},{8,14},{9,15},{10,... | collective-permute-start | bytes 1474568 | tf_op jit(solution)/shard_map/ppermute | solution.py:35
  34.4 15.0 %collective-permute-start.11 = (bf16[48,1920]{1,0:T(8,128)(2,1)S(1)}, bf16[48,1920]{1,0:T(8,128)(2,1)S(1)}, u32[]{:S(2)}, u32[]{:S(2)}) collective-permute-start(bf16[48,1920]{1,0:T(8,128)(2,1)S(1)} %pad_maximum_fusion.4), channel_id=1, source_target_pairs={{0,16},{1,17},{2,18},{3,19},{4,20},{5,21},{6,22},{7,23},{8,24},{9,... | collective-permute-start | bytes 552968 | tf_op jit(solution)/shard_map/ppermute | solution.py:35
  53.2 30.8 %collective-permute-start.17 = (bf16[4,48,1920]{2,1,0:T(8,128)(2,1)S(1)}, bf16[4,48,1920]{2,1,0:T(8,128)(2,1)S(1)}, u32[]{:S(2)}, u32[]{:S(2)}) collective-permute-start(bf16[4,48,1920]{2,1,0:T(8,128)(2,1)S(1)} %pad_maximum_fusion.refs_3_.refs_7_), channel_id=1, source_target_pairs={{0,2},{1,3},{2,0},{3,1},{4,6},{5,7},{6,4},{7,5},{8,10},{9,11},{10,... | collective-permute-start | bytes 2211848 | tf_op jit(solution)/shard_map/ppermute | solution.py:35
  53.8 30.2 %collective-permute-start.18 = (bf16[4,48,1920]{2,1,0:T(8,128)(2,1)S(1)}, bf16[4,48,1920]{2,1,0:T(8,128)(2,1)S(1)}, u32[]{:S(2)}, u32[]{:S(2)}) collective-permute-start(bf16[4,48,1920]{2,1,0:T(8,128)(2,1)S(1)} %pad_maximum_fusion.refs_3_.refs_7_), channel_id=1, source_target_pairs={{0,4},{1,5},{2,6},{3,7},{4,0},{5,1},{6,2},{7,3},{8,12},{9,13},{10,... | collective-permute-start | bytes 2211848 | tf_op jit(solution)/shard_map/ppermute | solution.py:35
  55.3 38.4 %collective-permute-start.19 = (bf16[4,48,1920]{2,1,0:T(8,128)(2,1)S(1)}, bf16[4,48,1920]{2,1,0:T(8,128)(2,1)S(1)}, u32[]{:S(2)}, u32[]{:S(2)}) collective-permute-start(bf16[4,48,1920]{2,1,0:T(8,128)(2,1)S(1)} %pad_maximum_fusion.refs_3_.refs_7_), channel_id=1, source_target_pairs={{0,6},{1,7},{2,4},{3,5},{4,2},{5,3},{6,0},{7,1},{8,14},{9,15},{10,... | collective-permute-start | bytes 2211848 | tf_op jit(solution)/shard_map/ppermute | solution.py:35
  151.0 30.3 %collective-permute-start.28 = (bf16[4,192,384]{2,1,0:T(8,128)(2,1)S(1)}, bf16[4,192,384]{2,1,0:T(8,128)(2,1)S(1)}, u32[]{:S(2)}, u32[]{:S(2)}) collective-permute-start(bf16[4,192,384]{2,1,0:T(8,128)(2,1)S(1)} %add_convert_fusion.6), channel_id=1, source_target_pairs={{0,2},{1,3},{2,0},{3,1},{4,6},{5,7},{6,4},{7,5},{8,10},{9,11},{10,... | collective-permute-start | bytes 1769480 | tf_op jit(solution)/shard_map/ppermute | solution.py:35
  152.5 28.8 %collective-permute-start.29 = (bf16[4,192,384]{2,1,0:T(8,128)(2,1)S(1)}, bf16[4,192,384]{2,1,0:T(8,128)(2,1)S(1)}, u32[]{:S(2)}, u32[]{:S(2)}) collective-permute-start(bf16[4,192,384]{2,1,0:T(8,128)(2,1)S(1)} %add_convert_fusion.5), channel_id=1, source_target_pairs={{0,4},{1,5},{2,6},{3,7},{4,0},{5,1},{6,2},{7,3},{8,12},{9,13},{10,... | collective-permute-start | bytes 1769480 | tf_op jit(solution)/shard_map/ppermute | solution.py:35
  153.1 28.2 %collective-permute-start.30 = (bf16[4,192,384]{2,1,0:T(8,128)(2,1)S(1)}, bf16[4,192,384]{2,1,0:T(8,128)(2,1)S(1)}, u32[]{:S(2)}, u32[]{:S(2)}) collective-permute-start(bf16[4,192,384]{2,1,0:T(8,128)(2,1)S(1)} %add_convert_fusion.4), channel_id=1, source_target_pairs={{0,6},{1,7},{2,4},{3,5},{4,2},{5,3},{6,0},{7,1},{8,14},{9,15},{10,... | collective-permute-start | bytes 1769480 | tf_op jit(solution)/shard_map/ppermute | solution.py:35
  186.9 33.5 %collective-permute-start.36 = (bf16[4,48,1920]{2,1,0:T(8,128)(2,1)S(1)}, bf16[4,48,1920]{2,1,0:T(8,128)(2,1)S(1)}, u32[]{:S(2)}, u32[]{:S(2)}) collective-permute-start(bf16[4,48,1920]{2,1,0:T(8,128)(2,1)S(1)} %add_convert_fusion.2), channel_id=1, source_target_pairs={{0,2},{1,3},{2,0},{3,1},{4,6},{5,7},{6,4},{7,5},{8,10},{9,11},{10,... | collective-permute-start | bytes 2211848 | tf_op jit(solution)/shard_map/ppermute | solution.py:35
  188.3 34.0 %collective-permute-start.37 = (bf16[4,48,1920]{2,1,0:T(8,128)(2,1)S(1)}, bf16[4,48,1920]{2,1,0:T(8,128)(2,1)S(1)}, u32[]{:S(2)}, u32[]{:S(2)}) collective-permute-start(bf16[4,48,1920]{2,1,0:T(8,128)(2,1)S(1)} %add_convert_fusion.1), channel_id=1, source_target_pairs={{0,4},{1,5},{2,6},{3,7},{4,0},{5,1},{6,2},{7,3},{8,12},{9,13},{10,... | collective-permute-start | bytes 2211848 | tf_op jit(solution)/shard_map/ppermute | solution.py:35
  188.9 31.4 %collective-permute-start.35 = (bf16[2,192,384]{2,1,0:T(8,128)(2,1)S(1)}, bf16[2,192,384]{2,1,0:T(8,128)(2,1)S(1)}, u32[]{:S(2)}, u32[]{:S(2)}) collective-permute-start(bf16[2,192,384]{2,1,0:T(8,128)(2,1)S(1)} %get-tuple-element.266), channel_id=1, source_target_pairs={{0,16},{1,17},{2,18},{3,19},{4,20},{5,21},{6,22},{7,23},{8,24},{9,... | collective-permute-start | bytes 884744 | tf_op jit(solution)/shard_map/ppermute | solution.py:35
  191.4 35.5 %collective-permute-start.42 = (bf16[4,48,1920]{2,1,0:T(8,128)(2,1)S(1)}, bf16[4,48,1920]{2,1,0:T(8,128)(2,1)S(1)}, u32[]{:S(2)}, u32[]{:S(2)}) collective-permute-start(bf16[4,48,1920]{2,1,0:T(8,128)(2,1)S(1)} %add_convert_fusion), channel_id=1, source_target_pairs={{0,6},{1,7},{2,4},{3,5},{4,2},{5,3},{6,0},{7,1},{8,14},{9,15},{10,... | collective-permute-start | bytes 2211848 | tf_op jit(solution)/shard_map/ppermute | solution.py:35
  227.8 19.7 %collective-permute-start.43 = (bf16[2,48,1920]{2,1,0:T(8,128)(2,1)}, bf16[2,48,1920]{2,1,0:T(8,128)(2,1)}, u32[]{:S(2)}, u32[]{:S(2)}) collective-permute-start(bf16[2,48,1920]{2,1,0:T(8,128)(2,1)} %get-tuple-element.294), channel_id=1, source_target_pairs={{0,16},{1,17},{2,18},{3,19},{4,20},{5,21},{6,22},{7,23},{8,24},{9,... | collective-permute-start | bytes 1105928 | tf_op jit(solution)/shard_map/ppermute | solution.py:35
  231.0 13.5 %collective-permute-start.44 = (bf16[192,384]{1,0:T(8,128)(2,1)}, bf16[192,384]{1,0:T(8,128)(2,1)}, u32[]{:S(2)}, u32[]{:S(2)}) collective-permute-start(bf16[192,384]{1,0:T(8,128)(2,1)} %get-tuple-element.327), channel_id=1, source_target_pairs={{0,8},{1,9},{2,10},{3,11},{4,12},{5,13},{6,14},{7,15},{8,0},{9,1},... | collective-permute-start | bytes 442376 | tf_op jit(solution)/shard_map/ppermute | solution.py:35
  231.3 19.2 %collective-permute-start.45 = (bf16[4,48,1280]{2,1,0:T(8,128)(2,1)S(1)}, bf16[4,48,1280]{2,1,0:T(8,128)(2,1)S(1)}, u32[]{:S(2)}, u32[]{:S(2)}) collective-permute-start(bf16[4,48,1280]{2,1,0:T(8,128)(2,1)S(1)} %get-tuple-element.297), channel_id=1, source_target_pairs={{0,2},{1,3},{2,0},{3,1},{4,6},{5,7},{6,4},{7,5},{8,10},{9,11},{10,... | collective-permute-start | bytes 1474568 | tf_op jit(solution)/shard_map/ppermute | solution.py:35
  232.2 23.2 %collective-permute-start.46 = (bf16[4,48,1280]{2,1,0:T(8,128)(2,1)S(1)}, bf16[4,48,1280]{2,1,0:T(8,128)(2,1)S(1)}, u32[]{:S(2)}, u32[]{:S(2)}) collective-permute-start(bf16[4,48,1280]{2,1,0:T(8,128)(2,1)S(1)} %get-tuple-element.298), channel_id=1, source_target_pairs={{0,4},{1,5},{2,6},{3,7},{4,0},{5,1},{6,2},{7,3},{8,12},{9,13},{10,... | collective-permute-start | bytes 1474568 | tf_op jit(solution)/shard_map/ppermute | solution.py:35
  233.4 22.1 %collective-permute-start.47 = (bf16[4,48,1280]{2,1,0:T(8,128)(2,1)S(1)}, bf16[4,48,1280]{2,1,0:T(8,128)(2,1)S(1)}, u32[]{:S(2)}, u32[]{:S(2)}) collective-permute-start(bf16[4,48,1280]{2,1,0:T(8,128)(2,1)S(1)} %get-tuple-element.299), channel_id=1, source_target_pairs={{0,6},{1,7},{2,4},{3,5},{4,2},{5,3},{6,0},{7,1},{8,14},{9,15},{10,... | collective-permute-start | bytes 1474568 | tf_op jit(solution)/shard_map/ppermute | solution.py:35
  248.7 11.4 %collective-permute-start.48 = (bf16[48,1920]{1,0:T(8,128)(2,1)S(1)}, bf16[48,1920]{1,0:T(8,128)(2,1)S(1)}, u32[]{:S(2)}, u32[]{:S(2)}) collective-permute-start(bf16[48,1920]{1,0:T(8,128)(2,1)S(1)} %get-tuple-element.324), channel_id=1, source_target_pairs={{0,8},{1,9},{2,10},{3,11},{4,12},{5,13},{6,14},{7,15},{8,0},{9,1},... | collective-permute-start | bytes 552968 | tf_op jit(solution)/shard_map/ppermute | solution.py:35
  257.5 10.3 %collective-permute-start.51 = (bf16[48,1280]{1,0:T(8,128)(2,1)S(1)}, bf16[48,1280]{1,0:T(8,128)(2,1)S(1)}, u32[]{:S(2)}, u32[]{:S(2)}) collective-permute-start(bf16[48,1280]{1,0:T(8,128)(2,1)S(1)} %get-tuple-element.311), channel_id=1, source_target_pairs={{0,16},{1,17},{2,18},{3,19},{4,20},{5,21},{6,22},{7,23},{8,24},{9,... | collective-permute-start | bytes 368648 | tf_op jit(solution)/shard_map/ppermute | solution.py:35
  (70 other events, 568.9 us)
Sparse Core Ops, SparseCore 0:
  52.6 68.1 all-gather.2

commit v4 on v3

--- a/solution.py
+++ b/solution.py
@@ -118,19 +118,6 @@
                     )
                 )
     return copies
-
-
-def table_copies(table, out, sems):
-    rows, columns = table.shape[1:]
-    return [
-        pltpu.make_async_copy(
-            table.at[w * 4 + n],
-            out.at[pl.ds((w * 2 + n % 2) * rows, rows), pl.ds(n // 2 * columns, columns)],
-            sems.at[w * 4 + n],
-        )
-        for w in range(8)
-        for n in range(4)
-    ]
 
 
 def start(copies):
@@ -451,9 +438,9 @@
 
 
 def outer_kernel(place, *refs):
-    act, normed, cotangent, vectors, back_table = refs[:5]
-    output, grad_second, sums = refs[5:8]
-    outs, (w_back, activated, grad_t, sems) = refs[8:16], refs[16:]
+    act, normed, cotangent, vectors = refs[:4]
+    blocks, (output, grad_second, sums) = refs[4:12], refs[12:15]
+    outs, (w_back, activated, grad_t, sems) = refs[15:23], refs[23:]
     step = pl.program_id(0)
     z, y, x, core = place()
 
@@ -462,7 +449,7 @@
 
     @pl.when(step == 0)
     def _():
-        copies = table_copies(back_table, w_back, sems)
+        copies = block_copies(place, blocks, 0, w_back, sems)
         start(copies)
         wait(copies)
 
@@ -507,12 +494,12 @@
                             outs[other * 4 + i + 2][k] = pieces[1 - bit]
 
 
-def outer_forward(place, activated, normed, cotangent, vectors, back_table):
+def outer_forward(place, activated, normed, cotangent, vectors, blocks):
     tokens = normed.shape[0]
     return pl.pallas_call(
         functools.partial(outer_kernel, place),
         grid=(tokens // TILE,),
-        in_specs=[tile(FF), tile(D), tile(D), fixed((12, D))] + anywhere(1),
+        in_specs=[tile(FF), tile(D), tile(D), fixed((12, D))] + anywhere(8),
         out_specs=[tile(D), tile(D), fixed((8, D))] + [fixed((4, 192, 384))] * 8,
         out_shape=[
             Shape((tokens, D), bf16),
@@ -529,23 +516,23 @@
         compiler_params=params(40),
         cost_estimate=cost(18),
         name="outer_forward",
-    )(activated, normed, cotangent, vectors, back_table)
+    )(activated, normed, cotangent, vectors, *blocks)
 
 
 def backward_kernel(place, *refs):
     grad_second, slope, normed, inverse, first_low, att_t, vectors = refs[:7]
-    blocks, back_table = refs[7:15], refs[15]
-    grad_att, grad_branch, sums, sums_inner = refs[16:20]
-    outs = refs[20:28]
-    w_in, w_out, w_back, inner_low, first_t, grad_low, turned = refs[28:35]
-    in_sems, out_sems, back_sems = refs[35:]
+    blocks, back_blocks = refs[7:15], refs[15:23]
+    grad_att, grad_branch, sums, sums_inner = refs[23:27]
+    outs = refs[27:35]
+    w_in, w_out, w_back, inner_low, first_t, grad_low, turned = refs[35:42]
+    in_sems, out_sems, back_sems = refs[42:]
     step = pl.program_id(0)
     z, y, x, core = place()
     here = pl.ds(pl.multiple_of(step * TILE, TILE), TILE)
 
     def compute(first_step):
         if first_step:
-            copies_back = table_copies(back_table, w_back, back_sems)
+            copies_back = block_copies(place, back_blocks, 0, w_back, back_sems)
             copies_in = block_copies(place, blocks, 0, w_in, in_sems)
             copies_out = block_copies(place, blocks, 1536, w_out, out_sems)
             start(copies_back)
@@ -556,8 +543,8 @@
         inner_sums = []
         for c in range(FF // D):
             columns = slice(c * D, c * D + D)
-            if first_step:
-                wait(copies_back[c * 8 : c * 8 + 8])
+            if first_step and c == 0:
+                wait(copies_back)
             gi = dot_t(g2_low, w_back[columns, :]) * slope[:, columns].astype(f32)
             inner_sums.append(column_sum(gi))
             gi = gi.astype(bf16)
@@ -623,7 +610,7 @@
 
 
 def backward(place, grad_second, slope, normed, inverse, first_low, att_t, vectors, *weights):
-    blocks, back_table = weights
+    blocks, back_blocks = weights
     tokens = normed.shape[0]
     outs = [(4, 48, 1920)] * 8
     return pl.pallas_call(
@@ -631,7 +618,7 @@
         grid=(tokens // TILE,),
         in_specs=[tile(D), tile(FF), tile(D), tile(128), tile(D)]
         + [pl.BlockSpec((D, TILE), lambda i: (0, i)), fixed((12, D))]
-        + anywhere(9),
+        + anywhere(16),
         out_specs=[tile(D), tile(D)] + [fixed(s) for s in [(8, D)] * 2 + outs],
         out_shape=[Shape((tokens, D), bf16), Shape((tokens, D), bf16)]
         + [Shape((8, D), f32)] * 2
@@ -649,7 +636,7 @@
         compiler_params=params(32),
         cost_estimate=cost(22),
         name="backward",
-    )(grad_second, slope, normed, inverse, first_low, att_t, vectors, *blocks, back_table)
+    )(grad_second, slope, normed, inverse, first_low, att_t, vectors, *blocks, *back_blocks)
 
 
 def turn_rows(place, source, turned, columns=slice(None)):
@@ -843,23 +830,28 @@
 
     qkv_blocks = gather_chips(qkv_line)
     mid_line = gather_z(mid)
-    qkv_blocks, mid_line, back = tie(qkv_blocks, mid_line, back)
-
-    back_table = lax.all_gather(back, ALL, axis=0, tiled=False)
+    next_back = send(back, z=1)
+    qkv_blocks, mid_line, back, next_back = tie(qkv_blocks, mid_line, back, next_back)
+
     mid_blocks = gather_chips(jnp.stack(mid_line))
     qkv_blocks = gather_cores(qkv_blocks)
+    back_two = jnp.stack([back, next_back])
     all_vectors = place_vectors(qkv_blocks)
+    back_two, all_vectors = tie(back_two, all_vectors)
+    far_two = send(back_two, z=2)
     attended = attend(position, hidden, all_vectors, key_marks, query_marks, qkv_blocks)
-    attended, mid_blocks = tie(attended, mid_blocks)
+    attended, mid_blocks, far_two = tie(attended, mid_blocks, far_two)
     packed, att, att_t, probs = attended
 
+    back_blocks = gather_chips(jnp.concatenate([back_two, far_two]))
     mid_blocks = gather_cores(mid_blocks)
     inner_outs = inner_forward(position, att, hidden, all_vectors, mid_blocks)
-    inner_outs, back_table = tie(inner_outs, back_table)
+    inner_outs, back_blocks = tie(inner_outs, back_blocks)
+    back_blocks = gather_cores(back_blocks)
     first_low, normed, inverse, activated, slope = inner_outs
 
     output, grad_second, sums_second, *tables_back = outer_forward(
-        position, activated, normed, cotangent, all_vectors, back_table
+        position, activated, normed, cotangent, all_vectors, back_blocks
     )
 
     received_back = [send(block, core=1) for block in tables_back[4:]]
@@ -876,7 +868,7 @@
         att_t,
         all_vectors,
         mid_blocks,
-        back_table,
+        back_blocks,
     )
     back_outs, others_back = tie(back_outs, others_back)
     grad_att, grad_branch, sums_first, sums_inner, *tables_mid = back_outs
@@ -937,8 +929,7 @@
         jnp.concatenate(pair, 2)
         for pair in zip(split_blocks(full_in, 48, 1536), split_blocks(full_out, 48, 384))
     ]
-    back_pieces = full_back.reshape(8, 2, 192, 2, 384).transpose(0, 3, 1, 2, 4)
-    back_pieces = back_pieces.reshape(32, 192, 384)
+    back_pieces = split_blocks(full_back, 192, 384)
     packed, att, att_t, probs = attend(
         origin, hidden, all_vectors, key_marks, query_marks, qkv_blocks
     )

time: 281 us -> 274 us (0.975)
  starting transfers between devices: 45 us -> 59.1 us
  between operations: 14.9 us -> 1.53 us
  waiting for transfers between devices: 61.2 us -> 53.9 us
    ppermute x54 -> x63, starting transfers between devices: 44.9 us -> 59.1 us  [send(): return lax.ppermute(values, ALL, pairs)]
    ppermute x54 -> x63, waiting for transfers between devices: 60 us -> 53.9 us  [send(): return lax.ppermute(values, ALL, pairs)]
    unnamed x81 -> x80, local copies, waits for them, and re-layouts: 10.9 us -> 8.68 us
  transfers between devices with their start and end apart: 55 -> 63, of which waited for: 30 -> 28; matrix products, arithmetic and copies ran while one was open for 5% -> 6% of each run, Pallas kernels for 40% -> 41%
where the time goes in v4:
time: 274 us; the launch traced here: 270 us
  Pallas kernels  132 us (48%)
  starting transfers between devices  59.1 us (22%)
  waiting for transfers between devices  53.9 us (20%)
  local copies, waits for them, and re-layouts  12.3 us (4%)
  other arithmetic  11.8 us (4%)
    ppermute x63, starting transfers between devices, send(): return lax.ppermute(values, ALL, pairs)  59.1 us
    ppermute x63, waiting for transfers between devices, send(): return lax.ppermute(values, ALL, pairs)  53.9 us
    pallas_call x1, Pallas kernels, backward(): pl.pallas_call(functools.partial(backward_kernel, place), grid=(tokens //...  26.4 us
    pallas_call x2, Pallas kernels, attend_back(): pl.pallas_call(kernel, grid=(1,), in_specs=[pl.BlockSpec((length, 3 * D),...  22.1 us
    pallas_call x1, Pallas kernels, attend(): pl.pallas_call(functools.partial(attend_kernel, place), grid=(rows,), in_...  21.2 us
    pallas_call x1, Pallas kernels, outer_forward(): pl.pallas_call(functools.partial(outer_kernel, place), grid=(tokens // TI...  20.8 us
    pallas_call x1, Pallas kernels, inner_forward(): pl.pallas_call(functools.partial(inner_kernel, place), grid=(tokens // TI...  19.6 us
    pallas_call x1, Pallas kernels, grad_of_hidden(): pl.pallas_call(functools.partial(hidden_kernel, place), grid=(tokens // T...  9.71 us
  transfers between devices with their start and end apart: 63, of which 28 were waited for; matrix products, arithmetic and copies ran while one was open for 6% of the time, Pallas kernels for 41%

profile of v4, /device:TPU:0, one launch (start us, length us, event | category | flops | bytes accessed | tf_op | source)
XLA Modules:
  0.0 270.5 jit_solution(10806607343283942280)
XLA Ops:
  6.5 3.1 %collective-permute-start.4 = (bf16[48,1280]{1,0:T(8,128)(2,1)}, bf16[48,1280]{1,0:T(8,128)(2,1)S(1)}, u32[]{:S(2)}, u32[]{:S(2)}) collective-permute-start(bf16[48,1280]{1,0:T(8,128)(2,1)} %pair_up.2), channel_id=1, source_target_pairs={{0,8},{1,9},{2,10},{3,11},{4,12},{5,13},{6,14},{7,15},{8,0},{9,1},... | collective-permute-start | bytes 368648 | tf_op jit(solution)/shard_map/ppermute | solution.py:35
  9.6 2.6 collective-permute-start.5
  14.3 2.1 pair_up.3
  18.6 3.6 %collective-permute-done.5 = bf16[48,1280]{1,0:T(8,128)(2,1)S(1)} collective-permute-done((bf16[48,1280]{1,0:T(8,128)(2,1)}, bf16[48,1280]{1,0:T(8,128)(2,1)S(1)}, u32[]{:S(2)}, u32[]{:S(2)}) %collective-permute-start.5) | collective-permute-done | bytes 122912 | tf_op jit(solution)/shard_map/ppermute | solution.py:35
  27.9 6.1 %collective-permute-done.13 = bf16[192,384]{1,0:T(8,128)(2,1)S(1)} collective-permute-done((bf16[192,384]{1,0:T(8,128)(2,1)S(1)}, bf16[192,384]{1,0:T(8,128)(2,1)S(1)}, u32[]{:S(2)}, u32[]{:S(2)}) %collective-permute-start.13) | collective-permute-done | bytes 147488 | tf_op jit(solution)/shard_map/ppermute | solution.py:35
  34.0 3.0 %collective-permute-start.11 = (bf16[48,1920]{1,0:T(8,128)(2,1)S(1)}, bf16[48,1920]{1,0:T(8,128)(2,1)S(1)}, u32[]{:S(2)}, u32[]{:S(2)}) collective-permute-start(bf16[48,1920]{1,0:T(8,128)(2,1)S(1)} %pad_maximum_fusion.5), channel_id=1, source_target_pairs={{0,16},{1,17},{2,18},{3,19},{4,20},{5,21},{6,22},{7,23},{8,24},{9,... | collective-permute-start | bytes 552968 | tf_op jit(solution)/shard_map/ppermute | solution.py:35
  38.1 10.1 %collective-permute-done.11 = bf16[48,1920]{1,0:T(8,128)(2,1)S(1)} collective-permute-done((bf16[48,1920]{1,0:T(8,128)(2,1)S(1)}, bf16[48,1920]{1,0:T(8,128)(2,1)S(1)}, u32[]{:S(2)}, u32[]{:S(2)}) %collective-permute-start.11) | collective-permute-done | bytes 184352 | tf_op jit(solution)/shard_map/ppermute | solution.py:35
  58.7 4.2 %collective-permute-start.21 = (bf16[2,192,384]{2,1,0:T(8,128)(2,1)}, bf16[2,192,384]{2,1,0:T(8,128)(2,1)}, u32[]{:S(2)}, u32[]{:S(2)}) collective-permute-start(bf16[2,192,384]{2,1,0:T(8,128)(2,1)} %pad_maximum_fusion.2), channel_id=1, source_target_pairs={{0,16},{1,17},{2,18},{3,19},{4,20},{5,21},{6,22},{7,23},{8,24},{9,... | collective-permute-start | bytes 884744 | tf_op jit(solution)/shard_map/ppermute | solution.py:35
  62.9 21.2 %attend.1 = (bf16[1024,2304]{1,0:T(8,128)(2,1)}, bf16[1024,768]{1,0:T(8,128)(2,1)}, bf16[768,1024]{1,0:T(8,128)(2,1)}, bf16[24,512,512]{2,1,0:T(8,128)(2,1)}) custom-call(bf16[1024,768]{1,0:T(8,128)(2,1)} %hidden.1, f32[12,768]{1,0:T(8,128)} %reshape.44.refs_1_.refs_2_.refs_3_.refs_6_, bf16[1024,128]{1,0:T(8,128)(2,1)} %add_convert_fusion.8.refs_2_, ...), custom_call_target="tpu_custom_call" | custom-call | tf_op jit(solution)/shard_map/attend/pallas_call | solution.py:349
  92.3 19.6 %inner_forward.1 = (bf16[1024,768]{1,0:T(8,128)(2,1)}, bf16[1024,768]{1,0:T(8,128)(2,1)}, f32[1024,128]{1,0:T(8,128)}, bf16[1024,3072]{1,0:T(8,128)(2,1)}, bf16[1024,3072]{1,0:T(8,128)(2,1)}) custom-call(bf16[1024,768]{1,0:T(8,128)(2,1)} %get-tuple-element.199.refs_0_, bf16[1024,768]{1,0:T(8,128)(2,1)} %hidden.1, ...), custom_call_target="tpu_custom_call" | custom-call | tf_op jit(solution)/shard_map/inner_forward/pallas_call | solution.py:416
  111.9 3.1 %collective-permute-done.27.refs_6_.refs_17_ = bf16[4,192,384]{2,1,0:T(8,128)(2,1)S(1)} collective-permute-done((bf16[4,192,384]{2,1,0:T(8,128)(2,1)S(1)}, bf16[4,192,384]{2,1,0:T(8,128)(2,1)S(1)}, u32[]{:S(2)}, u32[]{:S(2)}) %collective-permute-start.27) | collective-permute-done | bytes 589856 | tf_op jit(solution)/shard_map/ppermute | solution.py:35
  124.3 20.8 %outer_forward.1 = (bf16[1024,768]{1,0:T(8,128)(2,1)}, bf16[1024,768]{1,0:T(8,128)(2,1)S(1)}, f32[8,768]{1,0:T(8,128)S(1)}, bf16[4,192,384]{2,1,0:T(8,128)(2,1)S...) custom-call(bf16[1024,3072]{1,0:T(8,128)(2,1)} %get-tuple-element.21, ...), custom_call_target="tpu_custom_call" | custom-call | tf_op jit(solution)/shard_map/outer_forward/pallas_call | solution.py:499
  153.4 26.4 %backward.1 = (bf16[1024,768]{1,0:T(8,128)(2,1)S(1)}, bf16[1024,768]{1,0:T(8,128)(2,1)S(1)}, f32[8,768]{1,0:T(8,128)S(1)}, f32[8,768]{1,0:T(8,128)S(1)}, bf16[4,...) custom-call(bf16[1024,768]{1,0:T(8,128)(2,1)S(1)} %get-tuple-element, ...), custom_call_target="tpu_custom_call" | custom-call | tf_op jit(solution)/shard_map/backward/pallas_call | solution.py:616
  187.8 4.2 %collective-permute-start.44 = (bf16[2,192,384]{2,1,0:T(8,128)(2,1)S(1)}, bf16[2,192,384]{2,1,0:T(8,128)(2,1)S(1)}, u32[]{:S(2)}, u32[]{:S(2)}) collective-permute-start(bf16[2,192,384]{2,1,0:T(8,128)(2,1)S(1)} %get-tuple-element.280), channel_id=1, source_target_pairs={{0,16},{1,17},{2,18},{3,19},{4,20},{5,21},{6,22},{7,23},{8,24},{9,... | collective-permute-start | bytes 884744 | tf_op jit(solution)/shard_map/ppermute | solution.py:35
  193.2 10.9 %attend_back.2 = (bf16[1024,2304]{1,0:T(8,128)(2,1)S(1)}, f32[1,8,768]{2,1,0:T(8,128)S(1)}) custom-call(bf16[1024,2304]{1,0:T(8,128)(2,1)S(1)} %bitcast.36, bf16[1024,768]{1,0:T(8,128)(2,1)S(1)} %get-tuple-element.263.grad_att, bf16[24,512,512]{2,1,0:T(8,128)(2,1)} %get-tuple-element.264.probs), custom_call_target="tpu_custom_call" | custom-call | tf_op jit(solution)/shard_map/attend_back/pallas_call | solution.py:699
  204.1 11.2 %attend_back.3 = (bf16[1024,2304]{1,0:T(8,128)(2,1)S(1)}, f32[1,8,768]{2,1,0:T(8,128)S(1)}) custom-call(bf16[1024,2304]{1,0:T(8,128)(2,1)S(1)} %bitcast.36, bf16[1024,768]{1,0:T(8,128)(2,1)S(1)} %get-tuple-element.263.grad_att, bf16[24,512,512]{2,1,0:T(8,128)(2,1)} %get-tuple-element.264.probs, ...), custom_call_target="tpu_custom_call", output_to_operand_aliasing={{0}: (3, {})} | custom-call | tf_op jit(solution)/shard_map/attend_back/pallas_call | solution.py:699
  215.4 4.7 %grad_qkv.1 = (bf16[4,48,1280]{2,1,0:T(8,128)(2,1)S(1)}, bf16[4,48,1280]{2,1,0:T(8,128)(2,1)S(1)}, bf16[4,48,1280]{2,1,0:T(8,128)(2,1)S(1)}, bf16[4,48,1280]{2,1...) custom-call(bf16[1024,768]{1,0:T(8,128)(2,1)S(1)} %copy-done.1, ...), custom_call_target="tpu_custom_call" | custom-call | tf_op jit(solution)/shard_map/grad_qkv/pallas_call | solution.py:751
  225.6 3.4 %collective-permute-start.52 = (bf16[2,48,1920]{2,1,0:T(8,128)(2,1)}, bf16[2,48,1920]{2,1,0:T(8,128)(2,1)}, u32[]{:S(2)}, u32[]{:S(2)}) collective-permute-start(bf16[2,48,1920]{2,1,0:T(8,128)(2,1)} %get-tuple-element.308), channel_id=1, source_target_pairs={{0,16},{1,17},{2,18},{3,19},{4,20},{5,21},{6,22},{7,23},{8,24},{9,... | collective-permute-start | bytes 1105928 | tf_op jit(solution)/shard_map/ppermute | solution.py:35
  230.8 2.4 collective-permute-start.55
  233.7 9.7 %grad_hidden.1 = f32[1024,768]{1,0:T(8,128)} custom-call(bf16[1024,2304]{1,0:T(8,128)(2,1)} %copy-done, bf16[1024,768]{1,0:T(8,128)(2,1)} %copy-done.17, bf16[4,48,1280]{2,1,0:T(8,128)(2,1)} %copy-done.21, bf16[4,48,1280]{2,1,0:T(8,128)(2,1)} %copy-done.22, bf16[4,48,1280]{2,1,0:T(8,128)(2,1)} %copy-done.23, bf16[4,48,1280]{2,1,0:T(8,128)(2,1)} %copy-done.24, ...), custom_call_target="tpu_custom_call" | custom-call | tf_op jit(solution)/shard_map/grad_hidden/pallas_call | solution.py:781
  243.4 2.7 %collective-permute-done.52 = bf16[2,48,1920]{2,1,0:T(8,128)(2,1)} collective-permute-done((bf16[2,48,1920]{2,1,0:T(8,128)(2,1)}, bf16[2,48,1920]{2,1,0:T(8,128)(2,1)}, u32[]{:S(2)}, u32[]{:S(2)}) %collective-permute-start.52) | collective-permute-done | bytes 368672 | tf_op jit(solution)/shard_map/ppermute | solution.py:35
  249.0 5.0 %collective-permute-done.55.refs_2_ = bf16[4,48,1280]{2,1,0:T(8,128)(2,1)S(1)} collective-permute-done((bf16[4,48,1280]{2,1,0:T(8,128)(2,1)S(1)}, bf16[4,48,1280]{2,1,0:T(8,128)(2,1)S(1)}, u32[]{:S(2)}, u32[]{:S(2)}) %collective-permute-start.55) | collective-permute-done | bytes 491552 | tf_op jit(solution)/shard_map/ppermute | solution.py:35
  257.5 2.4 collective-permute-start.61
  262.0 5.9 %collective-permute-done.60 = bf16[48,1280]{1,0:T(8,128)(2,1)S(1)} collective-permute-done((bf16[48,1280]{1,0:T(8,128)(2,1)S(1)}, bf16[48,1280]{1,0:T(8,128)(2,1)S(1)}, u32[]{:S(2)}, u32[]{:S(2)}) %collective-permute-start.60) | collective-permute-done | bytes 122912 | tf_op jit(solution)/shard_map/ppermute | solution.py:35
  (232 shorter events, 80.6 us)
Async XLA Ops:
  22.2 25.9 %collective-permute-start.7 = (bf16[4,48,1280]{2,1,0:T(8,128)(2,1)S(1)}, bf16[4,48,1280]{2,1,0:T(8,128)(2,1)S(1)}, u32[]{:S(2)}, u32[]{:S(2)}) collective-permute-start(bf16[4,48,1280]{2,1,0:T(8,128)(2,1)S(1)} %pad_maximum_fusion.1.refs_0_.refs_4_.refs_2_), channel_id=1, source_target_pairs={{0,2},{1,3},{2,0},{3,1},{4,6},{5,7},{6,4},{7,5},{8,10},{9,11},{10,... | collective-permute-start | bytes 1474568 | tf_op jit(solution)/shard_map/ppermute | solution.py:35
  23.8 24.4 %collective-permute-start.8 = (bf16[4,48,1280]{2,1,0:T(8,128)(2,1)S(1)}, bf16[4,48,1280]{2,1,0:T(8,128)(2,1)S(1)}, u32[]{:S(2)}, u32[]{:S(2)}) collective-permute-start(bf16[4,48,1280]{2,1,0:T(8,128)(2,1)S(1)} %pad_maximum_fusion.1.refs_0_.refs_4_.refs_2_), channel_id=1, source_target_pairs={{0,4},{1,5},{2,6},{3,7},{4,0},{5,1},{6,2},{7,3},{8,12},{9,13},{10,... | collective-permute-start | bytes 1474568 | tf_op jit(solution)/shard_map/ppermute | solution.py:35
  25.3 22.9 %collective-permute-start.9 = (bf16[4,48,1280]{2,1,0:T(8,128)(2,1)S(1)}, bf16[4,48,1280]{2,1,0:T(8,128)(2,1)S(1)}, u32[]{:S(2)}, u32[]{:S(2)}) collective-permute-start(bf16[4,48,1280]{2,1,0:T(8,128)(2,1)S(1)} %pad_maximum_fusion.1.refs_0_.refs_4_.refs_2_), channel_id=1, source_target_pairs={{0,6},{1,7},{2,4},{3,5},{4,2},{5,3},{6,0},{7,1},{8,14},{9,15},{10,... | collective-permute-start | bytes 1474568 | tf_op jit(solution)/shard_map/ppermute | solution.py:35
  34.0 14.2 %collective-permute-start.11 = (bf16[48,1920]{1,0:T(8,128)(2,1)S(1)}, bf16[48,1920]{1,0:T(8,128)(2,1)S(1)}, u32[]{:S(2)}, u32[]{:S(2)}) collective-permute-start(bf16[48,1920]{1,0:T(8,128)(2,1)S(1)} %pad_maximum_fusion.5), channel_id=1, source_target_pairs={{0,16},{1,17},{2,18},{3,19},{4,20},{5,21},{6,22},{7,23},{8,24},{9,... | collective-permute-start | bytes 552968 | tf_op jit(solution)/shard_map/ppermute | solution.py:35
  49.5 34.6 %collective-permute-start.18 = (bf16[4,48,1920]{2,1,0:T(8,128)(2,1)S(1)}, bf16[4,48,1920]{2,1,0:T(8,128)(2,1)S(1)}, u32[]{:S(2)}, u32[]{:S(2)}) collective-permute-start(bf16[4,48,1920]{2,1,0:T(8,128)(2,1)S(1)} %pad_maximum_fusion.refs_3_.refs_7_), channel_id=1, source_target_pairs={{0,2},{1,3},{2,0},{3,1},{4,6},{5,7},{6,4},{7,5},{8,10},{9,11},{10,... | collective-permute-start | bytes 2211848 | tf_op jit(solution)/shard_map/ppermute | solution.py:35
  51.0 34.0 %collective-permute-start.19 = (bf16[4,48,1920]{2,1,0:T(8,128)(2,1)S(1)}, bf16[4,48,1920]{2,1,0:T(8,128)(2,1)S(1)}, u32[]{:S(2)}, u32[]{:S(2)}) collective-permute-start(bf16[4,48,1920]{2,1,0:T(8,128)(2,1)S(1)} %pad_maximum_fusion.refs_3_.refs_7_), channel_id=1, source_target_pairs={{0,4},{1,5},{2,6},{3,7},{4,0},{5,1},{6,2},{7,3},{8,12},{9,13},{10,... | collective-permute-start | bytes 2211848 | tf_op jit(solution)/shard_map/ppermute | solution.py:35
  52.6 32.5 %collective-permute-start.20 = (bf16[4,48,1920]{2,1,0:T(8,128)(2,1)S(1)}, bf16[4,48,1920]{2,1,0:T(8,128)(2,1)S(1)}, u32[]{:S(2)}, u32[]{:S(2)}) collective-permute-start(bf16[4,48,1920]{2,1,0:T(8,128)(2,1)S(1)} %pad_maximum_fusion.refs_3_.refs_7_), channel_id=1, source_target_pairs={{0,6},{1,7},{2,4},{3,5},{4,2},{5,3},{6,0},{7,1},{8,14},{9,15},{10,... | collective-permute-start | bytes 2211848 | tf_op jit(solution)/shard_map/ppermute | solution.py:35
  58.7 26.3 %collective-permute-start.21 = (bf16[2,192,384]{2,1,0:T(8,128)(2,1)}, bf16[2,192,384]{2,1,0:T(8,128)(2,1)}, u32[]{:S(2)}, u32[]{:S(2)}) collective-permute-start(bf16[2,192,384]{2,1,0:T(8,128)(2,1)} %pad_maximum_fusion.2), channel_id=1, source_target_pairs={{0,16},{1,17},{2,18},{3,19},{4,20},{5,21},{6,22},{7,23},{8,24},{9,... | collective-permute-start | bytes 884744 | tf_op jit(solution)/shard_map/ppermute | solution.py:35
  87.2 24.7 %collective-permute-start.26 = (bf16[4,192,384]{2,1,0:T(8,128)(2,1)S(1)}, bf16[4,192,384]{2,1,0:T(8,128)(2,1)}, u32[]{:S(2)}, u32[]{:S(2)}) collective-permute-start(bf16[4,192,384]{2,1,0:T(8,128)(2,1)S(1)} %constant_dynamic-update-slice_fusion.refs_4_.refs_15_), channel_id=1, source_target_pairs={{0,2},{1,3},{2,0},{3,1},{4,6},{5,7},{6,4},{7,5},{8,10},{9,11},{10,... | collective-permute-start | bytes 1769480 | tf_op jit(solution)/shard_map/ppermute | solution.py:35
  88.5 26.5 %collective-permute-start.27 = (bf16[4,192,384]{2,1,0:T(8,128)(2,1)S(1)}, bf16[4,192,384]{2,1,0:T(8,128)(2,1)S(1)}, u32[]{:S(2)}, u32[]{:S(2)}) collective-permute-start(bf16[4,192,384]{2,1,0:T(8,128)(2,1)S(1)} %constant_dynamic-update-slice_fusion.refs_4_.refs_15_), channel_id=1, source_target_pairs={{0,4},{1,5},{2,6},{3,7},{4,0},{5,1},{6,2},{7,3},{8,12},{9,13},{10,... | collective-permute-start | bytes 1769480 | tf_op jit(solution)/shard_map/ppermute | solution.py:35
  89.7 26.4 %collective-permute-start.28 = (bf16[4,192,384]{2,1,0:T(8,128)(2,1)S(1)}, bf16[4,192,384]{2,1,0:T(8,128)(2,1)S(1)}, u32[]{:S(2)}, u32[]{:S(2)}) collective-permute-start(bf16[4,192,384]{2,1,0:T(8,128)(2,1)S(1)} %constant_dynamic-update-slice_fusion.refs_4_.refs_15_), channel_id=1, source_target_pairs={{0,6},{1,7},{2,4},{3,5},{4,2},{5,3},{6,0},{7,1},{8,14},{9,15},{10,... | collective-permute-start | bytes 1769480 | tf_op jit(solution)/shard_map/ppermute | solution.py:35
  149.8 30.0 %collective-permute-start.37 = (bf16[4,192,384]{2,1,0:T(8,128)(2,1)S(1)}, bf16[4,192,384]{2,1,0:T(8,128)(2,1)S(1)}, u32[]{:S(2)}, u32[]{:S(2)}) collective-permute-start(bf16[4,192,384]{2,1,0:T(8,128)(2,1)S(1)} %add_convert_fusion.6), channel_id=1, source_target_pairs={{0,2},{1,3},{2,0},{3,1},{4,6},{5,7},{6,4},{7,5},{8,10},{9,11},{10,... | collective-permute-start | bytes 1769480 | tf_op jit(solution)/shard_map/ppermute | solution.py:35
  150.9 29.0 %collective-permute-start.38 = (bf16[4,192,384]{2,1,0:T(8,128)(2,1)S(1)}, bf16[4,192,384]{2,1,0:T(8,128)(2,1)S(1)}, u32[]{:S(2)}, u32[]{:S(2)}) collective-permute-start(bf16[4,192,384]{2,1,0:T(8,128)(2,1)S(1)} %add_convert_fusion.5), channel_id=1, source_target_pairs={{0,4},{1,5},{2,6},{3,7},{4,0},{5,1},{6,2},{7,3},{8,12},{9,13},{10,... | collective-permute-start | bytes 1769480 | tf_op jit(solution)/shard_map/ppermute | solution.py:35
  152.2 27.6 %collective-permute-start.39 = (bf16[4,192,384]{2,1,0:T(8,128)(2,1)S(1)}, bf16[4,192,384]{2,1,0:T(8,128)(2,1)S(1)}, u32[]{:S(2)}, u32[]{:S(2)}) collective-permute-start(bf16[4,192,384]{2,1,0:T(8,128)(2,1)S(1)} %add_convert_fusion.4), channel_id=1, source_target_pairs={{0,6},{1,7},{2,4},{3,5},{4,2},{5,3},{6,0},{7,1},{8,14},{9,15},{10,... | collective-permute-start | bytes 1769480 | tf_op jit(solution)/shard_map/ppermute | solution.py:35
  185.5 34.6 %collective-permute-start.45 = (bf16[4,48,1920]{2,1,0:T(8,128)(2,1)S(1)}, bf16[4,48,1920]{2,1,0:T(8,128)(2,1)S(1)}, u32[]{:S(2)}, u32[]{:S(2)}) collective-permute-start(bf16[4,48,1920]{2,1,0:T(8,128)(2,1)S(1)} %add_convert_fusion.2), channel_id=1, source_target_pairs={{0,2},{1,3},{2,0},{3,1},{4,6},{5,7},{6,4},{7,5},{8,10},{9,11},{10,... | collective-permute-start | bytes 2211848 | tf_op jit(solution)/shard_map/ppermute | solution.py:35
  186.5 33.6 %collective-permute-start.46 = (bf16[4,48,1920]{2,1,0:T(8,128)(2,1)S(1)}, bf16[4,48,1920]{2,1,0:T(8,128)(2,1)S(1)}, u32[]{:S(2)}, u32[]{:S(2)}) collective-permute-start(bf16[4,48,1920]{2,1,0:T(8,128)(2,1)S(1)} %add_convert_fusion.1), channel_id=1, source_target_pairs={{0,4},{1,5},{2,6},{3,7},{4,0},{5,1},{6,2},{7,3},{8,12},{9,13},{10,... | collective-permute-start | bytes 2211848 | tf_op jit(solution)/shard_map/ppermute | solution.py:35
  187.8 32.3 %collective-permute-start.44 = (bf16[2,192,384]{2,1,0:T(8,128)(2,1)S(1)}, bf16[2,192,384]{2,1,0:T(8,128)(2,1)S(1)}, u32[]{:S(2)}, u32[]{:S(2)}) collective-permute-start(bf16[2,192,384]{2,1,0:T(8,128)(2,1)S(1)} %get-tuple-element.280), channel_id=1, source_target_pairs={{0,16},{1,17},{2,18},{3,19},{4,20},{5,21},{6,22},{7,23},{8,24},{9,... | collective-permute-start | bytes 884744 | tf_op jit(solution)/shard_map/ppermute | solution.py:35
  192.0 32.7 %collective-permute-start.51 = (bf16[4,48,1920]{2,1,0:T(8,128)(2,1)S(1)}, bf16[4,48,1920]{2,1,0:T(8,128)(2,1)S(1)}, u32[]{:S(2)}, u32[]{:S(2)}) collective-permute-start(bf16[4,48,1920]{2,1,0:T(8,128)(2,1)S(1)} %add_convert_fusion), channel_id=1, source_target_pairs={{0,6},{1,7},{2,4},{3,5},{4,2},{5,3},{6,0},{7,1},{8,14},{9,15},{10,... | collective-permute-start | bytes 2211848 | tf_op jit(solution)/shard_map/ppermute | solution.py:35
  225.6 20.5 %collective-permute-start.52 = (bf16[2,48,1920]{2,1,0:T(8,128)(2,1)}, bf16[2,48,1920]{2,1,0:T(8,128)(2,1)}, u32[]{:S(2)}, u32[]{:S(2)}) collective-permute-start(bf16[2,48,1920]{2,1,0:T(8,128)(2,1)} %get-tuple-element.308), channel_id=1, source_target_pairs={{0,16},{1,17},{2,18},{3,19},{4,20},{5,21},{6,22},{7,23},{8,24},{9,... | collective-permute-start | bytes 1105928 | tf_op jit(solution)/shard_map/ppermute | solution.py:35
  229.8 13.6 %collective-permute-start.53 = (bf16[192,384]{1,0:T(8,128)(2,1)}, bf16[192,384]{1,0:T(8,128)(2,1)}, u32[]{:S(2)}, u32[]{:S(2)}) collective-permute-start(bf16[192,384]{1,0:T(8,128)(2,1)} %get-tuple-element.341), channel_id=1, source_target_pairs={{0,8},{1,9},{2,10},{3,11},{4,12},{5,13},{6,14},{7,15},{8,0},{9,1},... | collective-permute-start | bytes 442376 | tf_op jit(solution)/shard_map/ppermute | solution.py:35
  229.8 19.2 %collective-permute-start.54 = (bf16[4,48,1280]{2,1,0:T(8,128)(2,1)S(1)}, bf16[4,48,1280]{2,1,0:T(8,128)(2,1)S(1)}, u32[]{:S(2)}, u32[]{:S(2)}) collective-permute-start(bf16[4,48,1280]{2,1,0:T(8,128)(2,1)S(1)} %get-tuple-element.311), channel_id=1, source_target_pairs={{0,2},{1,3},{2,0},{3,1},{4,6},{5,7},{6,4},{7,5},{8,10},{9,11},{10,... | collective-permute-start | bytes 1474568 | tf_op jit(solution)/shard_map/ppermute | solution.py:35
  230.8 23.2 %collective-permute-start.55 = (bf16[4,48,1280]{2,1,0:T(8,128)(2,1)S(1)}, bf16[4,48,1280]{2,1,0:T(8,128)(2,1)S(1)}, u32[]{:S(2)}, u32[]{:S(2)}) collective-permute-start(bf16[4,48,1280]{2,1,0:T(8,128)(2,1)S(1)} %get-tuple-element.312), channel_id=1, source_target_pairs={{0,4},{1,5},{2,6},{3,7},{4,0},{5,1},{6,2},{7,3},{8,12},{9,13},{10,... | collective-permute-start | bytes 1474568 | tf_op jit(solution)/shard_map/ppermute | solution.py:35
  233.3 21.9 %collective-permute-start.56 = (bf16[4,48,1280]{2,1,0:T(8,128)(2,1)S(1)}, bf16[4,48,1280]{2,1,0:T(8,128)(2,1)S(1)}, u32[]{:S(2)}, u32[]{:S(2)}) collective-permute-start(bf16[4,48,1280]{2,1,0:T(8,128)(2,1)S(1)} %get-tuple-element.313), channel_id=1, source_target_pairs={{0,6},{1,7},{2,4},{3,5},{4,2},{5,3},{6,0},{7,1},{8,14},{9,15},{10,... | collective-permute-start | bytes 1474568 | tf_op jit(solution)/shard_map/ppermute | solution.py:35
  247.3 12.6 %collective-permute-start.57 = (bf16[48,1920]{1,0:T(8,128)(2,1)S(1)}, bf16[48,1920]{1,0:T(8,128)(2,1)S(1)}, u32[]{:S(2)}, u32[]{:S(2)}) collective-permute-start(bf16[48,1920]{1,0:T(8,128)(2,1)S(1)} %get-tuple-element.338), channel_id=1, source_target_pairs={{0,8},{1,9},{2,10},{3,11},{4,12},{5,13},{6,14},{7,15},{8,0},{9,1},... | collective-permute-start | bytes 552968 | tf_op jit(solution)/shard_map/ppermute | solution.py:35
  (77 other events, 558.6 us)

commit v5 on v4

--- a/solution.py
+++ b/solution.py
@@ -830,6 +830,7 @@
 
     qkv_blocks = gather_chips(qkv_line)
     mid_line = gather_z(mid)
+    back, mid_line[2] = tie(back, mid_line[2])
     next_back = send(back, z=1)
     qkv_blocks, mid_line, back, next_back = tie(qkv_blocks, mid_line, back, next_back)
 
@@ -840,14 +841,16 @@
     back_two, all_vectors = tie(back_two, all_vectors)
     far_two = send(back_two, z=2)
     attended = attend(position, hidden, all_vectors, key_marks, query_marks, qkv_blocks)
-    attended, mid_blocks, far_two = tie(attended, mid_blocks, far_two)
+    own_mid = send(mid_blocks[0], core=1)
+    attended, mid_blocks, far_two, own_mid = tie(attended, mid_blocks, far_two, own_mid)
     packed, att, att_t, probs = attended
 
     back_blocks = gather_chips(jnp.concatenate([back_two, far_two]))
-    mid_blocks = gather_cores(mid_blocks)
+    mid_blocks = mid_blocks + [own_mid] + [send(block, core=1) for block in mid_blocks[1:]]
     inner_outs = inner_forward(position, att, hidden, all_vectors, mid_blocks)
-    inner_outs, back_blocks = tie(inner_outs, back_blocks)
-    back_blocks = gather_cores(back_blocks)
+    own_back = send(back_blocks[0], core=1)
+    inner_outs, back_blocks, own_back = tie(inner_outs, back_blocks, own_back)
+    back_blocks = back_blocks + [own_back] + [send(block, core=1) for block in back_blocks[1:]]
     first_low, normed, inverse, activated, slope = inner_outs
 
     output, grad_second, sums_second, *tables_back = outer_forward(

time: 274 us -> 269 us (0.982)
  starting transfers between devices: 59.1 us -> 56.2 us
    ppermute x63, starting transfers between devices: 59.1 us -> 56.2 us  [send(): return lax.ppermute(values, ALL, pairs)]
    unnamed x80 -> x76, local copies, waits for them, and re-layouts: 8.68 us -> 8.45 us
  transfers between devices with their start and end apart: 63 -> 63, of which waited for: 28 -> 29; matrix products, arithmetic and copies ran while one was open for 6% -> 6% of each run, Pallas kernels for 41% -> 42%
where the time goes in v5:
time: 269 us; the launch traced here: 266 us
  Pallas kernels  132 us (49%)
  starting transfers between devices  56.2 us (21%)
  waiting for transfers between devices  52.6 us (20%)
  other arithmetic  11.9 us (4%)
  local copies, waits for them, and re-layouts  11.2 us (4%)
    ppermute x63, starting transfers between devices, send(): return lax.ppermute(values, ALL, pairs)  56.2 us
    ppermute x63, waiting for transfers between devices, send(): return lax.ppermute(values, ALL, pairs)  52.6 us
    pallas_call x1, Pallas kernels, backward(): pl.pallas_call(functools.partial(backward_kernel, place), grid=(tokens //...  26.1 us
    pallas_call x2, Pallas kernels, attend_back(): pl.pallas_call(kernel, grid=(1,), in_specs=[pl.BlockSpec((length, 3 * D),...  22.1 us
    pallas_call x1, Pallas kernels, attend(): pl.pallas_call(functools.partial(attend_kernel, place), grid=(rows,), in_...  21.2 us
    pallas_call x1, Pallas kernels, outer_forward(): pl.pallas_call(functools.partial(outer_kernel, place), grid=(tokens // TI...  21 us
    pallas_call x1, Pallas kernels, inner_forward(): pl.pallas_call(functools.partial(inner_kernel, place), grid=(tokens // TI...  19.6 us
    pallas_call x1, Pallas kernels, grad_of_hidden(): pl.pallas_call(functools.partial(hidden_kernel, place), grid=(tokens // T...  9.71 us
  transfers between devices with their start and end apart: 63, of which 29 were waited for; matrix products, arithmetic and copies ran while one was open for 6% of the time, Pallas kernels for 42%

profile of v5, /device:TPU:0, one launch (start us, length us, event | category | flops | bytes accessed | tf_op | source)
XLA Modules:
  0.0 265.5 jit_solution(15765594456079392986)
XLA Ops:
  6.5 3.1 %collective-permute-start.4 = (bf16[48,1280]{1,0:T(8,128)(2,1)}, bf16[48,1280]{1,0:T(8,128)(2,1)S(1)}, u32[]{:S(2)}, u32[]{:S(2)}) collective-permute-start(bf16[48,1280]{1,0:T(8,128)(2,1)} %pair_up.2), channel_id=1, source_target_pairs={{0,8},{1,9},{2,10},{3,11},{4,12},{5,13},{6,14},{7,15},{8,0},{9,1},... | collective-permute-start | bytes 368648 | tf_op jit(solution)/shard_map/ppermute | solution.py:35
  9.6 2.6 collective-permute-start.5
  14.3 2.1 pair_up.3
  18.5 3.6 %collective-permute-done.5 = bf16[48,1280]{1,0:T(8,128)(2,1)S(1)} collective-permute-done((bf16[48,1280]{1,0:T(8,128)(2,1)}, bf16[48,1280]{1,0:T(8,128)(2,1)S(1)}, u32[]{:S(2)}, u32[]{:S(2)}) %collective-permute-start.5) | collective-permute-done | bytes 122912 | tf_op jit(solution)/shard_map/ppermute | solution.py:35
  25.8 3.1 %collective-permute-start.11 = (bf16[48,1920]{1,0:T(8,128)(2,1)S(1)}, bf16[48,1920]{1,0:T(8,128)(2,1)S(1)}, u32[]{:S(2)}, u32[]{:S(2)}) collective-permute-start(bf16[48,1920]{1,0:T(8,128)(2,1)S(1)} %pad_maximum_fusion.5), channel_id=1, source_target_pairs={{0,16},{1,17},{2,18},{3,19},{4,20},{5,21},{6,22},{7,23},{8,24},{9,... | collective-permute-start | bytes 552968 | tf_op jit(solution)/shard_map/ppermute | solution.py:35
  28.8 8.0 %collective-permute-done.11 = bf16[48,1920]{1,0:T(8,128)(2,1)S(1)} collective-permute-done((bf16[48,1920]{1,0:T(8,128)(2,1)S(1)}, bf16[48,1920]{1,0:T(8,128)(2,1)S(1)}, u32[]{:S(2)}, u32[]{:S(2)}) %collective-permute-start.11) | collective-permute-done | bytes 184352 | tf_op jit(solution)/shard_map/ppermute | solution.py:35
  38.6 5.7 %collective-permute-done.12 = bf16[48,1920]{1,0:T(8,128)(2,1)S(1)} collective-permute-done((bf16[48,1920]{1,0:T(8,128)(2,1)S(1)}, bf16[48,1920]{1,0:T(8,128)(2,1)S(1)}, u32[]{:S(2)}, u32[]{:S(2)}) %collective-permute-start.12) | collective-permute-done | bytes 184352 | tf_op jit(solution)/shard_map/ppermute | solution.py:35
  55.2 4.2 %collective-permute-start.21 = (bf16[2,192,384]{2,1,0:T(8,128)(2,1)}, bf16[2,192,384]{2,1,0:T(8,128)(2,1)S(1)}, u32[]{:S(2)}, u32[]{:S(2)}) collective-permute-start(bf16[2,192,384]{2,1,0:T(8,128)(2,1)} %pad_maximum_fusion.2), channel_id=1, source_target_pairs={{0,16},{1,17},{2,18},{3,19},{4,20},{5,21},{6,22},{7,23},{8,24},{9,... | collective-permute-start | bytes 884744 | tf_op jit(solution)/shard_map/ppermute | solution.py:35
  59.3 21.2 %attend.1 = (bf16[1024,2304]{1,0:T(8,128)(2,1)}, bf16[1024,768]{1,0:T(8,128)(2,1)}, bf16[768,1024]{1,0:T(8,128)(2,1)}, bf16[24,512,512]{2,1,0:T(8,128)(2,1)}) custom-call(bf16[1024,768]{1,0:T(8,128)(2,1)} %hidden.1, f32[12,768]{1,0:T(8,128)} %reshape.44.refs_1_.refs_2_.refs_3_.refs_6_, bf16[1024,128]{1,0:T(8,128)(2,1)} %add_convert_fusion.8.refs_2_, ...), custom_call_target="tpu_custom_call" | custom-call | tf_op jit(solution)/shard_map/attend/pallas_call | solution.py:349
  86.9 19.6 %inner_forward.1 = (bf16[1024,768]{1,0:T(8,128)(2,1)}, bf16[1024,768]{1,0:T(8,128)(2,1)}, f32[1024,128]{1,0:T(8,128)}, bf16[1024,3072]{1,0:T(8,128)(2,1)}, bf16[1024,3072]{1,0:T(8,128)(2,1)}) custom-call(bf16[1024,768]{1,0:T(8,128)(2,1)} %get-tuple-element.205.refs_0_, bf16[1024,768]{1,0:T(8,128)(2,1)} %hidden.1, ...), custom_call_target="tpu_custom_call" | custom-call | tf_op jit(solution)/shard_map/inner_forward/pallas_call | solution.py:416
  106.5 5.7 %collective-permute-done.27.refs_6_.refs_17_ = bf16[4,192,384]{2,1,0:T(8,128)(2,1)S(1)} collective-permute-done((bf16[4,192,384]{2,1,0:T(8,128)(2,1)S(1)}, bf16[4,192,384]{2,1,0:T(8,128)(2,1)S(1)}, u32[]{:S(2)}, u32[]{:S(2)}) %collective-permute-start.27) | collective-permute-done | bytes 589856 | tf_op jit(solution)/shard_map/ppermute | solution.py:35
  119.7 21.0 %outer_forward.1 = (bf16[1024,768]{1,0:T(8,128)(2,1)}, bf16[1024,768]{1,0:T(8,128)(2,1)S(1)}, f32[8,768]{1,0:T(8,128)S(1)}, bf16[4,192,384]{2,1,0:T(8,128)(2,1)S...) custom-call(bf16[1024,3072]{1,0:T(8,128)(2,1)} %get-tuple-element.21, ...), custom_call_target="tpu_custom_call" | custom-call | tf_op jit(solution)/shard_map/outer_forward/pallas_call | solution.py:499
  149.1 26.1 %backward.1 = (bf16[1024,768]{1,0:T(8,128)(2,1)S(1)}, bf16[1024,768]{1,0:T(8,128)(2,1)S(1)}, f32[8,768]{1,0:T(8,128)S(1)}, f32[8,768]{1,0:T(8,128)S(1)}, bf16[4,...) custom-call(bf16[1024,768]{1,0:T(8,128)(2,1)S(1)} %get-tuple-element, ...), custom_call_target="tpu_custom_call" | custom-call | tf_op jit(solution)/shard_map/backward/pallas_call | solution.py:616
  182.8 4.1 %collective-permute-start.44 = (bf16[2,192,384]{2,1,0:T(8,128)(2,1)S(1)}, bf16[2,192,384]{2,1,0:T(8,128)(2,1)S(1)}, u32[]{:S(2)}, u32[]{:S(2)}) collective-permute-start(bf16[2,192,384]{2,1,0:T(8,128)(2,1)S(1)} %get-tuple-element.288), channel_id=1, source_target_pairs={{0,16},{1,17},{2,18},{3,19},{4,20},{5,21},{6,22},{7,23},{8,24},{9,... | collective-permute-start | bytes 884744 | tf_op jit(solution)/shard_map/ppermute | solution.py:35
  188.6 10.9 %attend_back.2 = (bf16[1024,2304]{1,0:T(8,128)(2,1)S(1)}, f32[1,8,768]{2,1,0:T(8,128)S(1)}) custom-call(bf16[1024,2304]{1,0:T(8,128)(2,1)S(1)} %bitcast.36, bf16[1024,768]{1,0:T(8,128)(2,1)S(1)} %get-tuple-element.271.grad_att, bf16[24,512,512]{2,1,0:T(8,128)(2,1)} %get-tuple-element.272.probs), custom_call_target="tpu_custom_call" | custom-call | tf_op jit(solution)/shard_map/attend_back/pallas_call | solution.py:699
  199.6 11.2 %attend_back.3 = (bf16[1024,2304]{1,0:T(8,128)(2,1)S(1)}, f32[1,8,768]{2,1,0:T(8,128)S(1)}) custom-call(bf16[1024,2304]{1,0:T(8,128)(2,1)S(1)} %bitcast.36, bf16[1024,768]{1,0:T(8,128)(2,1)S(1)} %get-tuple-element.271.grad_att, bf16[24,512,512]{2,1,0:T(8,128)(2,1)} %get-tuple-element.272.probs, ...), custom_call_target="tpu_custom_call", output_to_operand_aliasing={{0}: (3, {})} | custom-call | tf_op jit(solution)/shard_map/attend_back/pallas_call | solution.py:699
  210.8 4.7 %grad_qkv.1 = (bf16[4,48,1280]{2,1,0:T(8,128)(2,1)S(1)}, bf16[4,48,1280]{2,1,0:T(8,128)(2,1)S(1)}, bf16[4,48,1280]{2,1,0:T(8,128)(2,1)S(1)}, bf16[4,48,1280]{2,1...) custom-call(bf16[1024,768]{1,0:T(8,128)(2,1)S(1)} %copy-done.1, ...), custom_call_target="tpu_custom_call" | custom-call | tf_op jit(solution)/shard_map/grad_qkv/pallas_call | solution.py:751
  221.5 4.1 %collective-permute-start.52 = (bf16[2,48,1920]{2,1,0:T(8,128)(2,1)S(1)}, bf16[2,48,1920]{2,1,0:T(8,128)(2,1)}, u32[]{:S(2)}, u32[]{:S(2)}) collective-permute-start(bf16[2,48,1920]{2,1,0:T(8,128)(2,1)S(1)} %get-tuple-element.316), channel_id=1, source_target_pairs={{0,16},{1,17},{2,18},{3,19},{4,20},{5,21},{6,22},{7,23},{8,24},{9,... | collective-permute-start | bytes 1105928 | tf_op jit(solution)/shard_map/ppermute | solution.py:35
  229.8 9.7 %grad_hidden.1 = f32[1024,768]{1,0:T(8,128)} custom-call(bf16[1024,2304]{1,0:T(8,128)(2,1)} %copy-done, bf16[1024,768]{1,0:T(8,128)(2,1)} %copy-done.15, bf16[4,48,1280]{2,1,0:T(8,128)(2,1)} %copy-done.20, bf16[4,48,1280]{2,1,0:T(8,128)(2,1)} %copy-done.21, bf16[4,48,1280]{2,1,0:T(8,128)(2,1)} %copy-done.22, bf16[4,48,1280]{2,1,0:T(8,128)(2,1)} %copy-done.23, ...), custom_call_target="tpu_custom_call" | custom-call | tf_op jit(solution)/shard_map/grad_hidden/pallas_call | solution.py:781
  239.5 2.9 %collective-permute-done.52 = bf16[2,48,1920]{2,1,0:T(8,128)(2,1)} collective-permute-done((bf16[2,48,1920]{2,1,0:T(8,128)(2,1)S(1)}, bf16[2,48,1920]{2,1,0:T(8,128)(2,1)}, u32[]{:S(2)}, u32[]{:S(2)}) %collective-permute-start.52) | collective-permute-done | bytes 368672 | tf_op jit(solution)/shard_map/ppermute | solution.py:35
  245.4 5.8 %collective-permute-done.55.refs_2_ = bf16[4,48,1280]{2,1,0:T(8,128)(2,1)S(1)} collective-permute-done((bf16[4,48,1280]{2,1,0:T(8,128)(2,1)S(1)}, bf16[4,48,1280]{2,1,0:T(8,128)(2,1)S(1)}, u32[]{:S(2)}, u32[]{:S(2)}) %collective-permute-start.55) | collective-permute-done | bytes 491552 | tf_op jit(solution)/shard_map/ppermute | solution.py:35
  251.4 1.8 collective-permute-start.59
  253.5 2.3 collective-permute-start.61
  259.0 4.0 %collective-permute-done.60 = bf16[48,1280]{1,0:T(8,128)(2,1)S(1)} collective-permute-done((bf16[48,1280]{1,0:T(8,128)(2,1)S(1)}, bf16[48,1280]{1,0:T(8,128)(2,1)S(1)}, u32[]{:S(2)}, u32[]{:S(2)}) %collective-permute-start.60) | collective-permute-done | bytes 122912 | tf_op jit(solution)/shard_map/ppermute | solution.py:35
  (228 shorter events, 76.5 us)
Async XLA Ops:
  22.2 22.4 %collective-permute-start.7 = (bf16[4,48,1280]{2,1,0:T(8,128)(2,1)S(1)}, bf16[4,48,1280]{2,1,0:T(8,128)(2,1)S(1)}, u32[]{:S(2)}, u32[]{:S(2)}) collective-permute-start(bf16[4,48,1280]{2,1,0:T(8,128)(2,1)S(1)} %pad_maximum_fusion.1.refs_0_.refs_4_.refs_2_), channel_id=1, source_target_pairs={{0,2},{1,3},{2,0},{3,1},{4,6},{5,7},{6,4},{7,5},{8,10},{9,11},{10,... | collective-permute-start | bytes 1474568 | tf_op jit(solution)/shard_map/ppermute | solution.py:35
  23.8 21.3 %collective-permute-start.8 = (bf16[4,48,1280]{2,1,0:T(8,128)(2,1)S(1)}, bf16[4,48,1280]{2,1,0:T(8,128)(2,1)S(1)}, u32[]{:S(2)}, u32[]{:S(2)}) collective-permute-start(bf16[4,48,1280]{2,1,0:T(8,128)(2,1)S(1)} %pad_maximum_fusion.1.refs_0_.refs_4_.refs_2_), channel_id=1, source_target_pairs={{0,4},{1,5},{2,6},{3,7},{4,0},{5,1},{6,2},{7,3},{8,12},{9,13},{10,... | collective-permute-start | bytes 1474568 | tf_op jit(solution)/shard_map/ppermute | solution.py:35
  25.3 19.8 %collective-permute-start.9 = (bf16[4,48,1280]{2,1,0:T(8,128)(2,1)S(1)}, bf16[4,48,1280]{2,1,0:T(8,128)(2,1)S(1)}, u32[]{:S(2)}, u32[]{:S(2)}) collective-permute-start(bf16[4,48,1280]{2,1,0:T(8,128)(2,1)S(1)} %pad_maximum_fusion.1.refs_0_.refs_4_.refs_2_), channel_id=1, source_target_pairs={{0,6},{1,7},{2,4},{3,5},{4,2},{5,3},{6,0},{7,1},{8,14},{9,15},{10,... | collective-permute-start | bytes 1474568 | tf_op jit(solution)/shard_map/ppermute | solution.py:35
  46.3 34.2 %collective-permute-start.18 = (bf16[4,48,1920]{2,1,0:T(8,128)(2,1)S(1)}, bf16[4,48,1920]{2,1,0:T(8,128)(2,1)S(1)}, u32[]{:S(2)}, u32[]{:S(2)}) collective-permute-start(bf16[4,48,1920]{2,1,0:T(8,128)(2,1)S(1)} %pad_maximum_fusion.refs_3_.refs_7_), channel_id=1, source_target_pairs={{0,2},{1,3},{2,0},{3,1},{4,6},{5,7},{6,4},{7,5},{8,10},{9,11},{10,... | collective-permute-start | bytes 2211848 | tf_op jit(solution)/shard_map/ppermute | solution.py:35
  47.5 33.0 %collective-permute-start.19 = (bf16[4,48,1920]{2,1,0:T(8,128)(2,1)S(1)}, bf16[4,48,1920]{2,1,0:T(8,128)(2,1)S(1)}, u32[]{:S(2)}, u32[]{:S(2)}) collective-permute-start(bf16[4,48,1920]{2,1,0:T(8,128)(2,1)S(1)} %pad_maximum_fusion.refs_3_.refs_7_), channel_id=1, source_target_pairs={{0,4},{1,5},{2,6},{3,7},{4,0},{5,1},{6,2},{7,3},{8,12},{9,13},{10,... | collective-permute-start | bytes 2211848 | tf_op jit(solution)/shard_map/ppermute | solution.py:35
  49.0 32.6 %collective-permute-start.20 = (bf16[4,48,1920]{2,1,0:T(8,128)(2,1)S(1)}, bf16[4,48,1920]{2,1,0:T(8,128)(2,1)S(1)}, u32[]{:S(2)}, u32[]{:S(2)}) collective-permute-start(bf16[4,48,1920]{2,1,0:T(8,128)(2,1)S(1)} %pad_maximum_fusion.refs_3_.refs_7_), channel_id=1, source_target_pairs={{0,6},{1,7},{2,4},{3,5},{4,2},{5,3},{6,0},{7,1},{8,14},{9,15},{10,... | collective-permute-start | bytes 2211848 | tf_op jit(solution)/shard_map/ppermute | solution.py:35
  50.5 31.1 %collective-permute-start.22 = (bf16[4,48,1920]{2,1,0:T(8,128)(2,1)S(1)}, bf16[4,48,1920]{2,1,0:T(8,128)(2,1)}, u32[]{:S(2)}, u32[]{:S(2)}) collective-permute-start(bf16[4,48,1920]{2,1,0:T(8,128)(2,1)S(1)} %pad_maximum_fusion.refs_3_.refs_7_), channel_id=1, source_target_pairs={{0,1},{1,0},{2,3},{3,2},{4,5},{5,4},{6,7},{7,6},{8,9},{9,8},{10,11... | collective-permute-start | bytes 2211848 | tf_op jit(solution)/shard_map/ppermute | solution.py:35
  55.2 26.4 %collective-permute-start.21 = (bf16[2,192,384]{2,1,0:T(8,128)(2,1)}, bf16[2,192,384]{2,1,0:T(8,128)(2,1)S(1)}, u32[]{:S(2)}, u32[]{:S(2)}) collective-permute-start(bf16[2,192,384]{2,1,0:T(8,128)(2,1)} %pad_maximum_fusion.2), channel_id=1, source_target_pairs={{0,16},{1,17},{2,18},{3,19},{4,20},{5,21},{6,22},{7,23},{8,24},{9,... | collective-permute-start | bytes 884744 | tf_op jit(solution)/shard_map/ppermute | solution.py:35
  82.4 24.1 %collective-permute-start.26 = (bf16[4,192,384]{2,1,0:T(8,128)(2,1)S(1)}, bf16[4,192,384]{2,1,0:T(8,128)(2,1)S(1)}, u32[]{:S(2)}, u32[]{:S(2)}) collective-permute-start(bf16[4,192,384]{2,1,0:T(8,128)(2,1)S(1)} %constant_dynamic-update-slice_fusion.refs_4_.refs_15_), channel_id=1, source_target_pairs={{0,2},{1,3},{2,0},{3,1},{4,6},{5,7},{6,4},{7,5},{8,10},{9,11},{10,... | collective-permute-start | bytes 1769480 | tf_op jit(solution)/shard_map/ppermute | solution.py:35
  84.2 28.0 %collective-permute-start.27 = (bf16[4,192,384]{2,1,0:T(8,128)(2,1)S(1)}, bf16[4,192,384]{2,1,0:T(8,128)(2,1)S(1)}, u32[]{:S(2)}, u32[]{:S(2)}) collective-permute-start(bf16[4,192,384]{2,1,0:T(8,128)(2,1)S(1)} %constant_dynamic-update-slice_fusion.refs_4_.refs_15_), channel_id=1, source_target_pairs={{0,4},{1,5},{2,6},{3,7},{4,0},{5,1},{6,2},{7,3},{8,12},{9,13},{10,... | collective-permute-start | bytes 1769480 | tf_op jit(solution)/shard_map/ppermute | solution.py:35
  84.9 27.3 %collective-permute-start.28 = (bf16[4,192,384]{2,1,0:T(8,128)(2,1)S(1)}, bf16[4,192,384]{2,1,0:T(8,128)(2,1)}, u32[]{:S(2)}, u32[]{:S(2)}) collective-permute-start(bf16[4,192,384]{2,1,0:T(8,128)(2,1)S(1)} %constant_dynamic-update-slice_fusion.refs_4_.refs_15_), channel_id=1, source_target_pairs={{0,6},{1,7},{2,4},{3,5},{4,2},{5,3},{6,0},{7,1},{8,14},{9,15},{10,... | collective-permute-start | bytes 1769480 | tf_op jit(solution)/shard_map/ppermute | solution.py:35
  86.0 26.2 %collective-permute-start.29 = (bf16[4,192,384]{2,1,0:T(8,128)(2,1)S(1)}, bf16[4,192,384]{2,1,0:T(8,128)(2,1)}, u32[]{:S(2)}, u32[]{:S(2)}) collective-permute-start(bf16[4,192,384]{2,1,0:T(8,128)(2,1)S(1)} %constant_dynamic-update-slice_fusion.refs_4_.refs_15_), channel_id=1, source_target_pairs={{0,1},{1,0},{2,3},{3,2},{4,5},{5,4},{6,7},{7,6},{8,9},{9,8},{10,11... | collective-permute-start | bytes 1769480 | tf_op jit(solution)/shard_map/ppermute | solution.py:35
  145.5 29.8 %collective-permute-start.37 = (bf16[4,192,384]{2,1,0:T(8,128)(2,1)S(1)}, bf16[4,192,384]{2,1,0:T(8,128)(2,1)S(1)}, u32[]{:S(2)}, u32[]{:S(2)}) collective-permute-start(bf16[4,192,384]{2,1,0:T(8,128)(2,1)S(1)} %add_convert_fusion.6), channel_id=1, source_target_pairs={{0,2},{1,3},{2,0},{3,1},{4,6},{5,7},{6,4},{7,5},{8,10},{9,11},{10,... | collective-permute-start | bytes 1769480 | tf_op jit(solution)/shard_map/ppermute | solution.py:35
  146.2 29.1 %collective-permute-start.38 = (bf16[4,192,384]{2,1,0:T(8,128)(2,1)S(1)}, bf16[4,192,384]{2,1,0:T(8,128)(2,1)S(1)}, u32[]{:S(2)}, u32[]{:S(2)}) collective-permute-start(bf16[4,192,384]{2,1,0:T(8,128)(2,1)S(1)} %add_convert_fusion.5), channel_id=1, source_target_pairs={{0,4},{1,5},{2,6},{3,7},{4,0},{5,1},{6,2},{7,3},{8,12},{9,13},{10,... | collective-permute-start | bytes 1769480 | tf_op jit(solution)/shard_map/ppermute | solution.py:35
  147.4 27.9 %collective-permute-start.39 = (bf16[4,192,384]{2,1,0:T(8,128)(2,1)S(1)}, bf16[4,192,384]{2,1,0:T(8,128)(2,1)S(1)}, u32[]{:S(2)}, u32[]{:S(2)}) collective-permute-start(bf16[4,192,384]{2,1,0:T(8,128)(2,1)S(1)} %add_convert_fusion.4), channel_id=1, source_target_pairs={{0,6},{1,7},{2,4},{3,5},{4,2},{5,3},{6,0},{7,1},{8,14},{9,15},{10,... | collective-permute-start | bytes 1769480 | tf_op jit(solution)/shard_map/ppermute | solution.py:35
  180.9 34.6 %collective-permute-start.45 = (bf16[4,48,1920]{2,1,0:T(8,128)(2,1)S(1)}, bf16[4,48,1920]{2,1,0:T(8,128)(2,1)S(1)}, u32[]{:S(2)}, u32[]{:S(2)}) collective-permute-start(bf16[4,48,1920]{2,1,0:T(8,128)(2,1)S(1)} %add_convert_fusion.2), channel_id=1, source_target_pairs={{0,2},{1,3},{2,0},{3,1},{4,6},{5,7},{6,4},{7,5},{8,10},{9,11},{10,... | collective-permute-start | bytes 2211848 | tf_op jit(solution)/shard_map/ppermute | solution.py:35
  181.6 34.0 %collective-permute-start.46 = (bf16[4,48,1920]{2,1,0:T(8,128)(2,1)S(1)}, bf16[4,48,1920]{2,1,0:T(8,128)(2,1)S(1)}, u32[]{:S(2)}, u32[]{:S(2)}) collective-permute-start(bf16[4,48,1920]{2,1,0:T(8,128)(2,1)S(1)} %add_convert_fusion.1), channel_id=1, source_target_pairs={{0,4},{1,5},{2,6},{3,7},{4,0},{5,1},{6,2},{7,3},{8,12},{9,13},{10,... | collective-permute-start | bytes 2211848 | tf_op jit(solution)/shard_map/ppermute | solution.py:35
  182.8 32.7 %collective-permute-start.44 = (bf16[2,192,384]{2,1,0:T(8,128)(2,1)S(1)}, bf16[2,192,384]{2,1,0:T(8,128)(2,1)S(1)}, u32[]{:S(2)}, u32[]{:S(2)}) collective-permute-start(bf16[2,192,384]{2,1,0:T(8,128)(2,1)S(1)} %get-tuple-element.288), channel_id=1, source_target_pairs={{0,16},{1,17},{2,18},{3,19},{4,20},{5,21},{6,22},{7,23},{8,24},{9,... | collective-permute-start | bytes 884744 | tf_op jit(solution)/shard_map/ppermute | solution.py:35
  187.0 34.1 %collective-permute-start.51 = (bf16[4,48,1920]{2,1,0:T(8,128)(2,1)S(1)}, bf16[4,48,1920]{2,1,0:T(8,128)(2,1)S(1)}, u32[]{:S(2)}, u32[]{:S(2)}) collective-permute-start(bf16[4,48,1920]{2,1,0:T(8,128)(2,1)S(1)} %add_convert_fusion), channel_id=1, source_target_pairs={{0,6},{1,7},{2,4},{3,5},{4,2},{5,3},{6,0},{7,1},{8,14},{9,15},{10,... | collective-permute-start | bytes 2211848 | tf_op jit(solution)/shard_map/ppermute | solution.py:35
  221.5 21.0 %collective-permute-start.52 = (bf16[2,48,1920]{2,1,0:T(8,128)(2,1)S(1)}, bf16[2,48,1920]{2,1,0:T(8,128)(2,1)}, u32[]{:S(2)}, u32[]{:S(2)}) collective-permute-start(bf16[2,48,1920]{2,1,0:T(8,128)(2,1)S(1)} %get-tuple-element.316), channel_id=1, source_target_pairs={{0,16},{1,17},{2,18},{3,19},{4,20},{5,21},{6,22},{7,23},{8,24},{9,... | collective-permute-start | bytes 1105928 | tf_op jit(solution)/shard_map/ppermute | solution.py:35
  226.3 13.2 %collective-permute-start.53 = (bf16[192,384]{1,0:T(8,128)(2,1)}, bf16[192,384]{1,0:T(8,128)(2,1)}, u32[]{:S(2)}, u32[]{:S(2)}) collective-permute-start(bf16[192,384]{1,0:T(8,128)(2,1)} %get-tuple-element.349), channel_id=1, source_target_pairs={{0,8},{1,9},{2,10},{3,11},{4,12},{5,13},{6,14},{7,15},{8,0},{9,1},... | collective-permute-start | bytes 442376 | tf_op jit(solution)/shard_map/ppermute | solution.py:35
  226.3 19.0 %collective-permute-start.54 = (bf16[4,48,1280]{2,1,0:T(8,128)(2,1)}, bf16[4,48,1280]{2,1,0:T(8,128)(2,1)S(1)}, u32[]{:S(2)}, u32[]{:S(2)}) collective-permute-start(bf16[4,48,1280]{2,1,0:T(8,128)(2,1)} %get-tuple-element.319), channel_id=1, source_target_pairs={{0,2},{1,3},{2,0},{3,1},{4,6},{5,7},{6,4},{7,5},{8,10},{9,11},{10,... | collective-permute-start | bytes 1474568 | tf_op jit(solution)/shard_map/ppermute | solution.py:35
  227.9 23.2 %collective-permute-start.55 = (bf16[4,48,1280]{2,1,0:T(8,128)(2,1)S(1)}, bf16[4,48,1280]{2,1,0:T(8,128)(2,1)S(1)}, u32[]{:S(2)}, u32[]{:S(2)}) collective-permute-start(bf16[4,48,1280]{2,1,0:T(8,128)(2,1)S(1)} %get-tuple-element.320), channel_id=1, source_target_pairs={{0,4},{1,5},{2,6},{3,7},{4,0},{5,1},{6,2},{7,3},{8,12},{9,13},{10,... | collective-permute-start | bytes 1474568 | tf_op jit(solution)/shard_map/ppermute | solution.py:35
  228.5 22.7 %collective-permute-start.56 = (bf16[4,48,1280]{2,1,0:T(8,128)(2,1)S(1)}, bf16[4,48,1280]{2,1,0:T(8,128)(2,1)S(1)}, u32[]{:S(2)}, u32[]{:S(2)}) collective-permute-start(bf16[4,48,1280]{2,1,0:T(8,128)(2,1)S(1)} %get-tuple-element.321), channel_id=1, source_target_pairs={{0,6},{1,7},{2,4},{3,5},{4,2},{5,3},{6,0},{7,1},{8,14},{9,15},{10,... | collective-permute-start | bytes 1474568 | tf_op jit(solution)/shard_map/ppermute | solution.py:35
  (75 other events, 523.0 us)

commit v6 on v5

--- a/solution.py
+++ b/solution.py
@@ -431,7 +431,7 @@
             pltpu.SemaphoreType.DMA((32,)),
             pltpu.SemaphoreType.DMA((32,)),
         ],
-        compiler_params=params(60),
+        compiler_params=params(57),
         cost_estimate=cost(16),
         name="inner_forward",
     )(att, hidden, vectors, *blocks)
@@ -883,8 +883,9 @@
 
     plane_mid = [send(parts_mid[1], x=1), send(parts_mid[2], y=1)]
     corner_mid = send(parts_mid[3], x=1, y=1)
+    packed_low, sums_zero = attend_back(0, packed, grad_att, probs)
+    packed_low, far_back = tie(packed_low, far_back)
     far_back = send(far_back, z=2)
-    packed_low, sums_zero = attend_back(0, packed, grad_att, probs)
     packed_low, sums_one = attend_back(1, packed, grad_att, probs, packed_low)
     tables_qkv = grad_qkv(
         position, hidden, packed_low, sums_zero, sums_one, sums_first, sums_inner, sums_second
@@ -904,7 +905,9 @@
     next_back = send(near_back[1], z=1)
     near_back, grad_branch = tie(near_back, grad_branch)
     grad_hidden = grad_of_hidden(position, packed_low, grad_branch, qkv_blocks)
-    grad_hidden, far_mid, next_back = tie(grad_hidden, far_mid, next_back)
+    grad_hidden, far_mid, next_back, others_qkv = tie(
+        grad_hidden, far_mid, next_back, others_qkv
+    )
 
     own_back = wide_sum(near_back[0], next_back).T
     near_mid = near_parts(near_mid, far_mid)

time: 269 us -> 270 us (level)
  waiting for transfers between devices: 52.6 us -> 48.9 us
  starting transfers between devices: 56.2 us -> 59.3 us
    ppermute x63, waiting for transfers between devices: 52.6 us -> 48.9 us  [send(): return lax.ppermute(values, ALL, pairs)]
    ppermute x63, starting transfers between devices: 56.2 us -> 59.3 us  [send(): return lax.ppermute(values, ALL, pairs)]
    unnamed x76 -> x86, local copies, waits for them, and re-layouts: 8.45 us -> 9.36 us
  transfers between devices with their start and end apart: 63 -> 63, of which waited for: 29 -> 29; matrix products, arithmetic and copies ran while one was open for 6% -> 5% of each run, Pallas kernels for 42% -> 42%
where the time goes in v6:
time: 270 us; the launch traced here: 266 us
  Pallas kernels  133 us (49%)
  starting transfers between devices  59.3 us (22%)
  waiting for transfers between devices  48.9 us (18%)
  local copies, waits for them, and re-layouts  12.1 us (4%)
  other arithmetic  11.8 us (4%)
    ppermute x63, starting transfers between devices, send(): return lax.ppermute(values, ALL, pairs)  59.3 us
    ppermute x63, waiting for transfers between devices, send(): return lax.ppermute(values, ALL, pairs)  48.9 us
    pallas_call x1, Pallas kernels, backward(): pl.pallas_call(functools.partial(backward_kernel, place), grid=(tokens //...  26.3 us
    pallas_call x2, Pallas kernels, attend_back(): pl.pallas_call(kernel, grid=(1,), in_specs=[pl.BlockSpec((length, 3 * D),...  22 us
    pallas_call x1, Pallas kernels, attend(): pl.pallas_call(functools.partial(attend_kernel, place), grid=(rows,), in_...  21.2 us
    pallas_call x1, Pallas kernels, outer_forward(): pl.pallas_call(functools.partial(outer_kernel, place), grid=(tokens // TI...  20.9 us
    pallas_call x1, Pallas kernels, inner_forward(): pl.pallas_call(functools.partial(inner_kernel, place), grid=(tokens // TI...  19.5 us
    pallas_call x1, Pallas kernels, grad_of_hidden(): pl.pallas_call(functools.partial(hidden_kernel, place), grid=(tokens // T...  9.71 us
  transfers between devices with their start and end apart: 63, of which 29 were waited for; matrix products, arithmetic and copies ran while one was open for 5% of the time, Pallas kernels for 42%

profile of v6, /device:TPU:0, one launch (start us, length us, event | category | flops | bytes accessed | tf_op | source)
XLA Modules:
  0.0 266.2 jit_solution(14477706100846249037)
XLA Ops:
  6.5 3.1 %collective-permute-start.4 = (bf16[48,1280]{1,0:T(8,128)(2,1)}, bf16[48,1280]{1,0:T(8,128)(2,1)S(1)}, u32[]{:S(2)}, u32[]{:S(2)}) collective-permute-start(bf16[48,1280]{1,0:T(8,128)(2,1)} %pair_up.2), channel_id=1, source_target_pairs={{0,8},{1,9},{2,10},{3,11},{4,12},{5,13},{6,14},{7,15},{8,0},{9,1},... | collective-permute-start | bytes 368648 | tf_op jit(solution)/shard_map/ppermute | solution.py:35
  9.6 2.6 collective-permute-start.5
  14.3 2.1 pair_up.3
  18.5 3.6 %collective-permute-done.5 = bf16[48,1280]{1,0:T(8,128)(2,1)S(1)} collective-permute-done((bf16[48,1280]{1,0:T(8,128)(2,1)}, bf16[48,1280]{1,0:T(8,128)(2,1)S(1)}, u32[]{:S(2)}, u32[]{:S(2)}) %collective-permute-start.5) | collective-permute-done | bytes 122912 | tf_op jit(solution)/shard_map/ppermute | solution.py:35
  25.8 3.1 %collective-permute-start.11 = (bf16[48,1920]{1,0:T(8,128)(2,1)S(1)}, bf16[48,1920]{1,0:T(8,128)(2,1)S(1)}, u32[]{:S(2)}, u32[]{:S(2)}) collective-permute-start(bf16[48,1920]{1,0:T(8,128)(2,1)S(1)} %pad_maximum_fusion.5), channel_id=1, source_target_pairs={{0,16},{1,17},{2,18},{3,19},{4,20},{5,21},{6,22},{7,23},{8,24},{9,... | collective-permute-start | bytes 552968 | tf_op jit(solution)/shard_map/ppermute | solution.py:35
  28.8 8.0 %collective-permute-done.11 = bf16[48,1920]{1,0:T(8,128)(2,1)S(1)} collective-permute-done((bf16[48,1920]{1,0:T(8,128)(2,1)S(1)}, bf16[48,1920]{1,0:T(8,128)(2,1)S(1)}, u32[]{:S(2)}, u32[]{:S(2)}) %collective-permute-start.11) | collective-permute-done | bytes 184352 | tf_op jit(solution)/shard_map/ppermute | solution.py:35
  38.6 5.7 %collective-permute-done.12 = bf16[48,1920]{1,0:T(8,128)(2,1)S(1)} collective-permute-done((bf16[48,1920]{1,0:T(8,128)(2,1)S(1)}, bf16[48,1920]{1,0:T(8,128)(2,1)S(1)}, u32[]{:S(2)}, u32[]{:S(2)}) %collective-permute-start.12) | collective-permute-done | bytes 184352 | tf_op jit(solution)/shard_map/ppermute | solution.py:35
  55.2 4.2 %collective-permute-start.21 = (bf16[2,192,384]{2,1,0:T(8,128)(2,1)}, bf16[2,192,384]{2,1,0:T(8,128)(2,1)S(1)}, u32[]{:S(2)}, u32[]{:S(2)}) collective-permute-start(bf16[2,192,384]{2,1,0:T(8,128)(2,1)} %pad_maximum_fusion.2), channel_id=1, source_target_pairs={{0,16},{1,17},{2,18},{3,19},{4,20},{5,21},{6,22},{7,23},{8,24},{9,... | collective-permute-start | bytes 884744 | tf_op jit(solution)/shard_map/ppermute | solution.py:35
  59.3 21.2 %attend.1 = (bf16[1024,2304]{1,0:T(8,128)(2,1)}, bf16[1024,768]{1,0:T(8,128)(2,1)}, bf16[768,1024]{1,0:T(8,128)(2,1)}, bf16[24,512,512]{2,1,0:T(8,128)(2,1)}) custom-call(bf16[1024,768]{1,0:T(8,128)(2,1)} %hidden.1, f32[12,768]{1,0:T(8,128)} %reshape.44.refs_1_.refs_2_.refs_3_.refs_6_, bf16[1024,128]{1,0:T(8,128)(2,1)} %add_convert_fusion.8.refs_2_, ...), custom_call_target="tpu_custom_call" | custom-call | tf_op jit(solution)/shard_map/attend/pallas_call | solution.py:349
  87.7 19.5 %inner_forward.1 = (bf16[1024,768]{1,0:T(8,128)(2,1)}, bf16[1024,768]{1,0:T(8,128)(2,1)}, f32[1024,128]{1,0:T(8,128)}, bf16[1024,3072]{1,0:T(8,128)(2,1)}, bf16[1024,3072]{1,0:T(8,128)(2,1)}) custom-call(bf16[1024,768]{1,0:T(8,128)(2,1)} %get-tuple-element.210.refs_0_, bf16[1024,768]{1,0:T(8,128)(2,1)} %hidden.1, ...), custom_call_target="tpu_custom_call" | custom-call | tf_op jit(solution)/shard_map/inner_forward/pallas_call | solution.py:416
  107.2 5.0 %collective-permute-done.27.refs_6_.refs_17_ = bf16[4,192,384]{2,1,0:T(8,128)(2,1)S(1)} collective-permute-done((bf16[4,192,384]{2,1,0:T(8,128)(2,1)S(1)}, bf16[4,192,384]{2,1,0:T(8,128)(2,1)S(1)}, u32[]{:S(2)}, u32[]{:S(2)}) %collective-permute-start.27) | collective-permute-done | bytes 589856 | tf_op jit(solution)/shard_map/ppermute | solution.py:35
  119.6 20.9 %outer_forward.1 = (bf16[1024,768]{1,0:T(8,128)(2,1)}, bf16[1024,768]{1,0:T(8,128)(2,1)S(1)}, f32[8,768]{1,0:T(8,128)S(1)}, bf16[4,192,384]{2,1,0:T(8,128)(2,1)S...) custom-call(bf16[1024,3072]{1,0:T(8,128)(2,1)} %get-tuple-element.22, ...), custom_call_target="tpu_custom_call" | custom-call | tf_op jit(solution)/shard_map/outer_forward/pallas_call | solution.py:499
  148.9 26.3 %backward.1 = (bf16[1024,768]{1,0:T(8,128)(2,1)S(1)}, bf16[1024,768]{1,0:T(8,128)(2,1)S(1)}, f32[8,768]{1,0:T(8,128)S(1)}, f32[8,768]{1,0:T(8,128)S(1)}, bf16[4,...) custom-call(bf16[1024,768]{1,0:T(8,128)(2,1)S(1)} %get-tuple-element, ...), custom_call_target="tpu_custom_call" | custom-call | tf_op jit(solution)/shard_map/backward/pallas_call | solution.py:616
  182.6 10.9 %attend_back.2 = (bf16[1024,2304]{1,0:T(8,128)(2,1)S(1)}, f32[1,8,768]{2,1,0:T(8,128)S(1)}) custom-call(bf16[1024,2304]{1,0:T(8,128)(2,1)S(1)} %bitcast.36, bf16[1024,768]{1,0:T(8,128)(2,1)S(1)} %get-tuple-element.276.grad_att, bf16[24,512,512]{2,1,0:T(8,128)(2,1)} %get-tuple-element.277.probs), custom_call_target="tpu_custom_call" | custom-call | tf_op jit(solution)/shard_map/attend_back/pallas_call | solution.py:699
  193.5 4.2 %collective-permute-start.44 = (bf16[2,192,384]{2,1,0:T(8,128)(2,1)S(1)}, bf16[2,192,384]{2,1,0:T(8,128)(2,1)S(1)}, u32[]{:S(2)}, u32[]{:S(2)}) collective-permute-start(bf16[2,192,384]{2,1,0:T(8,128)(2,1)S(1)} %get-tuple-element.295), channel_id=1, source_target_pairs={{0,16},{1,17},{2,18},{3,19},{4,20},{5,21},{6,22},{7,23},{8,24},{9,... | collective-permute-start | bytes 884744 | tf_op jit(solution)/shard_map/ppermute | solution.py:35
  199.6 11.1 %attend_back.3 = (bf16[1024,2304]{1,0:T(8,128)(2,1)S(1)}, f32[1,8,768]{2,1,0:T(8,128)S(1)}) custom-call(bf16[1024,2304]{1,0:T(8,128)(2,1)S(1)} %bitcast.36, bf16[1024,768]{1,0:T(8,128)(2,1)S(1)} %get-tuple-element.276.grad_att, bf16[24,512,512]{2,1,0:T(8,128)(2,1)} %get-tuple-element.277.probs, ...), custom_call_target="tpu_custom_call", output_to_operand_aliasing={{0}: (3, {})} | custom-call | tf_op jit(solution)/shard_map/attend_back/pallas_call | solution.py:699
  210.7 4.7 %grad_qkv.1 = (bf16[4,48,1280]{2,1,0:T(8,128)(2,1)S(1)}, bf16[4,48,1280]{2,1,0:T(8,128)(2,1)S(1)}, bf16[4,48,1280]{2,1,0:T(8,128)(2,1)S(1)}, bf16[4,48,1280]{2,1...) custom-call(bf16[1024,768]{1,0:T(8,128)(2,1)S(1)} %copy-done.1, ...), custom_call_target="tpu_custom_call" | custom-call | tf_op jit(solution)/shard_map/grad_qkv/pallas_call | solution.py:751
  222.7 1.9 collective-permute-start.56
  225.4 3.6 %collective-permute-start.52 = (bf16[2,48,1920]{2,1,0:T(8,128)(2,1)}, bf16[2,48,1920]{2,1,0:T(8,128)(2,1)}, u32[]{:S(2)}, u32[]{:S(2)}) collective-permute-start(bf16[2,48,1920]{2,1,0:T(8,128)(2,1)} %get-tuple-element.323), channel_id=1, source_target_pairs={{0,16},{1,17},{2,18},{3,19},{4,20},{5,21},{6,22},{7,23},{8,24},{9,... | collective-permute-start | bytes 1105928 | tf_op jit(solution)/shard_map/ppermute | solution.py:35
  229.8 9.7 %grad_hidden.1 = f32[1024,768]{1,0:T(8,128)} custom-call(bf16[1024,2304]{1,0:T(8,128)(2,1)} %copy-done, bf16[1024,768]{1,0:T(8,128)(2,1)} %copy-done.21, bf16[4,48,1280]{2,1,0:T(8,128)(2,1)} %copy-done.25, bf16[4,48,1280]{2,1,0:T(8,128)(2,1)} %copy-done.26, bf16[4,48,1280]{2,1,0:T(8,128)(2,1)} %copy-done.27, bf16[4,48,1280]{2,1,0:T(8,128)(2,1)} %copy-done.28, ...), custom_call_target="tpu_custom_call" | custom-call | tf_op jit(solution)/shard_map/grad_hidden/pallas_call | solution.py:781
  240.2 5.4 %collective-permute-done.52 = bf16[2,48,1920]{2,1,0:T(8,128)(2,1)} collective-permute-done((bf16[2,48,1920]{2,1,0:T(8,128)(2,1)}, bf16[2,48,1920]{2,1,0:T(8,128)(2,1)}, u32[]{:S(2)}, u32[]{:S(2)}) %collective-permute-start.52) | collective-permute-done | bytes 368672 | tf_op jit(solution)/shard_map/ppermute | solution.py:35
  246.7 3.6 %collective-permute-start.57 = (bf16[48,1920]{1,0:T(8,128)(2,1)S(1)}, bf16[48,1920]{1,0:T(8,128)(2,1)S(1)}, u32[]{:S(2)}, u32[]{:S(2)}) collective-permute-start(bf16[48,1920]{1,0:T(8,128)(2,1)S(1)} %get-tuple-element.356), channel_id=1, source_target_pairs={{0,8},{1,9},{2,10},{3,11},{4,12},{5,13},{6,14},{7,15},{8,0},{9,1},... | collective-permute-start | bytes 552968 | tf_op jit(solution)/shard_map/ppermute | solution.py:35
  250.7 3.0 %collective-permute-start.60 = (bf16[48,1280]{1,0:T(8,128)(2,1)S(1)}, bf16[48,1280]{1,0:T(8,128)(2,1)S(1)}, u32[]{:S(2)}, u32[]{:S(2)}) collective-permute-start(bf16[48,1280]{1,0:T(8,128)(2,1)S(1)} %get-tuple-element.343), channel_id=1, source_target_pairs={{0,16},{1,17},{2,18},{3,19},{4,20},{5,21},{6,22},{7,23},{8,24},{9,... | collective-permute-start | bytes 368648 | tf_op jit(solution)/shard_map/ppermute | solution.py:35
  259.7 4.1 %collective-permute-done.61 = bf16[48,1280]{1,0:T(8,128)(2,1)S(1)} collective-permute-done((bf16[48,1280]{1,0:T(8,128)(2,1)S(1)}, bf16[48,1280]{1,0:T(8,128)(2,1)S(1)}, u32[]{:S(2)}, u32[]{:S(2)}) %collective-permute-start.61) | collective-permute-done | bytes 122912 | tf_op jit(solution)/shard_map/ppermute | solution.py:35
  (238 shorter events, 77.2 us)
Async XLA Ops:
  9.6 12.6 %collective-permute-start.5 = (bf16[48,1280]{1,0:T(8,128)(2,1)}, bf16[48,1280]{1,0:T(8,128)(2,1)S(1)}, u32[]{:S(2)}, u32[]{:S(2)}) collective-permute-start(bf16[48,1280]{1,0:T(8,128)(2,1)} %pair_up.2), channel_id=1, source_target_pairs={{0,16},{1,17},{2,18},{3,19},{4,20},{5,21},{6,22},{7,23},{8,24},{9,... | collective-permute-start | bytes 368648 | tf_op jit(solution)/shard_map/ppermute | solution.py:35
  22.2 22.4 %collective-permute-start.7 = (bf16[4,48,1280]{2,1,0:T(8,128)(2,1)S(1)}, bf16[4,48,1280]{2,1,0:T(8,128)(2,1)S(1)}, u32[]{:S(2)}, u32[]{:S(2)}) collective-permute-start(bf16[4,48,1280]{2,1,0:T(8,128)(2,1)S(1)} %pad_maximum_fusion.1.refs_0_.refs_4_.refs_2_), channel_id=1, source_target_pairs={{0,2},{1,3},{2,0},{3,1},{4,6},{5,7},{6,4},{7,5},{8,10},{9,11},{10,... | collective-permute-start | bytes 1474568 | tf_op jit(solution)/shard_map/ppermute | solution.py:35
  23.8 21.3 %collective-permute-start.8 = (bf16[4,48,1280]{2,1,0:T(8,128)(2,1)S(1)}, bf16[4,48,1280]{2,1,0:T(8,128)(2,1)S(1)}, u32[]{:S(2)}, u32[]{:S(2)}) collective-permute-start(bf16[4,48,1280]{2,1,0:T(8,128)(2,1)S(1)} %pad_maximum_fusion.1.refs_0_.refs_4_.refs_2_), channel_id=1, source_target_pairs={{0,4},{1,5},{2,6},{3,7},{4,0},{5,1},{6,2},{7,3},{8,12},{9,13},{10,... | collective-permute-start | bytes 1474568 | tf_op jit(solution)/shard_map/ppermute | solution.py:35
  25.3 19.8 %collective-permute-start.9 = (bf16[4,48,1280]{2,1,0:T(8,128)(2,1)S(1)}, bf16[4,48,1280]{2,1,0:T(8,128)(2,1)S(1)}, u32[]{:S(2)}, u32[]{:S(2)}) collective-permute-start(bf16[4,48,1280]{2,1,0:T(8,128)(2,1)S(1)} %pad_maximum_fusion.1.refs_0_.refs_4_.refs_2_), channel_id=1, source_target_pairs={{0,6},{1,7},{2,4},{3,5},{4,2},{5,3},{6,0},{7,1},{8,14},{9,15},{10,... | collective-permute-start | bytes 1474568 | tf_op jit(solution)/shard_map/ppermute | solution.py:35
  46.3 34.2 %collective-permute-start.18 = (bf16[4,48,1920]{2,1,0:T(8,128)(2,1)S(1)}, bf16[4,48,1920]{2,1,0:T(8,128)(2,1)S(1)}, u32[]{:S(2)}, u32[]{:S(2)}) collective-permute-start(bf16[4,48,1920]{2,1,0:T(8,128)(2,1)S(1)} %pad_maximum_fusion.refs_3_.refs_7_), channel_id=1, source_target_pairs={{0,2},{1,3},{2,0},{3,1},{4,6},{5,7},{6,4},{7,5},{8,10},{9,11},{10,... | collective-permute-start | bytes 2211848 | tf_op jit(solution)/shard_map/ppermute | solution.py:35
  47.5 33.0 %collective-permute-start.19 = (bf16[4,48,1920]{2,1,0:T(8,128)(2,1)S(1)}, bf16[4,48,1920]{2,1,0:T(8,128)(2,1)S(1)}, u32[]{:S(2)}, u32[]{:S(2)}) collective-permute-start(bf16[4,48,1920]{2,1,0:T(8,128)(2,1)S(1)} %pad_maximum_fusion.refs_3_.refs_7_), channel_id=1, source_target_pairs={{0,4},{1,5},{2,6},{3,7},{4,0},{5,1},{6,2},{7,3},{8,12},{9,13},{10,... | collective-permute-start | bytes 2211848 | tf_op jit(solution)/shard_map/ppermute | solution.py:35
  49.0 32.6 %collective-permute-start.20 = (bf16[4,48,1920]{2,1,0:T(8,128)(2,1)S(1)}, bf16[4,48,1920]{2,1,0:T(8,128)(2,1)S(1)}, u32[]{:S(2)}, u32[]{:S(2)}) collective-permute-start(bf16[4,48,1920]{2,1,0:T(8,128)(2,1)S(1)} %pad_maximum_fusion.refs_3_.refs_7_), channel_id=1, source_target_pairs={{0,6},{1,7},{2,4},{3,5},{4,2},{5,3},{6,0},{7,1},{8,14},{9,15},{10,... | collective-permute-start | bytes 2211848 | tf_op jit(solution)/shard_map/ppermute | solution.py:35
  50.5 31.1 %collective-permute-start.22 = (bf16[4,48,1920]{2,1,0:T(8,128)(2,1)S(1)}, bf16[4,48,1920]{2,1,0:T(8,128)(2,1)}, u32[]{:S(2)}, u32[]{:S(2)}) collective-permute-start(bf16[4,48,1920]{2,1,0:T(8,128)(2,1)S(1)} %pad_maximum_fusion.refs_3_.refs_7_), channel_id=1, source_target_pairs={{0,1},{1,0},{2,3},{3,2},{4,5},{5,4},{6,7},{7,6},{8,9},{9,8},{10,11... | collective-permute-start | bytes 2211848 | tf_op jit(solution)/shard_map/ppermute | solution.py:35
  55.2 26.4 %collective-permute-start.21 = (bf16[2,192,384]{2,1,0:T(8,128)(2,1)}, bf16[2,192,384]{2,1,0:T(8,128)(2,1)S(1)}, u32[]{:S(2)}, u32[]{:S(2)}) collective-permute-start(bf16[2,192,384]{2,1,0:T(8,128)(2,1)} %pad_maximum_fusion.2), channel_id=1, source_target_pairs={{0,16},{1,17},{2,18},{3,19},{4,20},{5,21},{6,22},{7,23},{8,24},{9,... | collective-permute-start | bytes 884744 | tf_op jit(solution)/shard_map/ppermute | solution.py:35
  82.4 24.8 %collective-permute-start.26 = (bf16[4,192,384]{2,1,0:T(8,128)(2,1)S(1)}, bf16[4,192,384]{2,1,0:T(8,128)(2,1)S(1)}, u32[]{:S(2)}, u32[]{:S(2)}) collective-permute-start(bf16[4,192,384]{2,1,0:T(8,128)(2,1)S(1)} %constant_dynamic-update-slice_fusion.refs_4_.refs_15_), channel_id=1, source_target_pairs={{0,2},{1,3},{2,0},{3,1},{4,6},{5,7},{6,4},{7,5},{8,10},{9,11},{10,... | collective-permute-start | bytes 1769480 | tf_op jit(solution)/shard_map/ppermute | solution.py:35
  84.2 28.0 %collective-permute-start.27 = (bf16[4,192,384]{2,1,0:T(8,128)(2,1)S(1)}, bf16[4,192,384]{2,1,0:T(8,128)(2,1)S(1)}, u32[]{:S(2)}, u32[]{:S(2)}) collective-permute-start(bf16[4,192,384]{2,1,0:T(8,128)(2,1)S(1)} %constant_dynamic-update-slice_fusion.refs_4_.refs_15_), channel_id=1, source_target_pairs={{0,4},{1,5},{2,6},{3,7},{4,0},{5,1},{6,2},{7,3},{8,12},{9,13},{10,... | collective-permute-start | bytes 1769480 | tf_op jit(solution)/shard_map/ppermute | solution.py:35
  84.9 27.3 %collective-permute-start.28 = (bf16[4,192,384]{2,1,0:T(8,128)(2,1)S(1)}, bf16[4,192,384]{2,1,0:T(8,128)(2,1)S(1)}, u32[]{:S(2)}, u32[]{:S(2)}) collective-permute-start(bf16[4,192,384]{2,1,0:T(8,128)(2,1)S(1)} %constant_dynamic-update-slice_fusion.refs_4_.refs_15_), channel_id=1, source_target_pairs={{0,6},{1,7},{2,4},{3,5},{4,2},{5,3},{6,0},{7,1},{8,14},{9,15},{10,... | collective-permute-start | bytes 1769480 | tf_op jit(solution)/shard_map/ppermute | solution.py:35
  85.9 26.3 %collective-permute-start.29 = (bf16[4,192,384]{2,1,0:T(8,128)(2,1)S(1)}, bf16[4,192,384]{2,1,0:T(8,128)(2,1)}, u32[]{:S(2)}, u32[]{:S(2)}) collective-permute-start(bf16[4,192,384]{2,1,0:T(8,128)(2,1)S(1)} %constant_dynamic-update-slice_fusion.refs_4_.refs_15_), channel_id=1, source_target_pairs={{0,1},{1,0},{2,3},{3,2},{4,5},{5,4},{6,7},{7,6},{8,9},{9,8},{10,11... | collective-permute-start | bytes 1769480 | tf_op jit(solution)/shard_map/ppermute | solution.py:35
  145.3 30.0 %collective-permute-start.37 = (bf16[4,192,384]{2,1,0:T(8,128)(2,1)S(1)}, bf16[4,192,384]{2,1,0:T(8,128)(2,1)S(1)}, u32[]{:S(2)}, u32[]{:S(2)}) collective-permute-start(bf16[4,192,384]{2,1,0:T(8,128)(2,1)S(1)} %add_convert_fusion.6), channel_id=1, source_target_pairs={{0,2},{1,3},{2,0},{3,1},{4,6},{5,7},{6,4},{7,5},{8,10},{9,11},{10,... | collective-permute-start | bytes 1769480 | tf_op jit(solution)/shard_map/ppermute | solution.py:35
  145.7 29.5 %collective-permute-start.38 = (bf16[4,192,384]{2,1,0:T(8,128)(2,1)S(1)}, bf16[4,192,384]{2,1,0:T(8,128)(2,1)S(1)}, u32[]{:S(2)}, u32[]{:S(2)}) collective-permute-start(bf16[4,192,384]{2,1,0:T(8,128)(2,1)S(1)} %add_convert_fusion.5), channel_id=1, source_target_pairs={{0,4},{1,5},{2,6},{3,7},{4,0},{5,1},{6,2},{7,3},{8,12},{9,13},{10,... | collective-permute-start | bytes 1769480 | tf_op jit(solution)/shard_map/ppermute | solution.py:35
  147.0 28.2 %collective-permute-start.39 = (bf16[4,192,384]{2,1,0:T(8,128)(2,1)S(1)}, bf16[4,192,384]{2,1,0:T(8,128)(2,1)S(1)}, u32[]{:S(2)}, u32[]{:S(2)}) collective-permute-start(bf16[4,192,384]{2,1,0:T(8,128)(2,1)S(1)} %add_convert_fusion.4), channel_id=1, source_target_pairs={{0,6},{1,7},{2,4},{3,5},{4,2},{5,3},{6,0},{7,1},{8,14},{9,15},{10,... | collective-permute-start | bytes 1769480 | tf_op jit(solution)/shard_map/ppermute | solution.py:35
  180.9 34.6 %collective-permute-start.45 = (bf16[4,48,1920]{2,1,0:T(8,128)(2,1)S(1)}, bf16[4,48,1920]{2,1,0:T(8,128)(2,1)S(1)}, u32[]{:S(2)}, u32[]{:S(2)}) collective-permute-start(bf16[4,48,1920]{2,1,0:T(8,128)(2,1)S(1)} %add_convert_fusion.2), channel_id=1, source_target_pairs={{0,2},{1,3},{2,0},{3,1},{4,6},{5,7},{6,4},{7,5},{8,10},{9,11},{10,... | collective-permute-start | bytes 2211848 | tf_op jit(solution)/shard_map/ppermute | solution.py:35
  181.3 34.1 %collective-permute-start.46 = (bf16[4,48,1920]{2,1,0:T(8,128)(2,1)S(1)}, bf16[4,48,1920]{2,1,0:T(8,128)(2,1)S(1)}, u32[]{:S(2)}, u32[]{:S(2)}) collective-permute-start(bf16[4,48,1920]{2,1,0:T(8,128)(2,1)S(1)} %add_convert_fusion.1), channel_id=1, source_target_pairs={{0,4},{1,5},{2,6},{3,7},{4,0},{5,1},{6,2},{7,3},{8,12},{9,13},{10,... | collective-permute-start | bytes 2211848 | tf_op jit(solution)/shard_map/ppermute | solution.py:35
  193.5 21.9 %collective-permute-start.44 = (bf16[2,192,384]{2,1,0:T(8,128)(2,1)S(1)}, bf16[2,192,384]{2,1,0:T(8,128)(2,1)S(1)}, u32[]{:S(2)}, u32[]{:S(2)}) collective-permute-start(bf16[2,192,384]{2,1,0:T(8,128)(2,1)S(1)} %get-tuple-element.295), channel_id=1, source_target_pairs={{0,16},{1,17},{2,18},{3,19},{4,20},{5,21},{6,22},{7,23},{8,24},{9,... | collective-permute-start | bytes 884744 | tf_op jit(solution)/shard_map/ppermute | solution.py:35
  197.7 23.3 %collective-permute-start.51 = (bf16[4,48,1920]{2,1,0:T(8,128)(2,1)S(1)}, bf16[4,48,1920]{2,1,0:T(8,128)(2,1)S(1)}, u32[]{:S(2)}, u32[]{:S(2)}) collective-permute-start(bf16[4,48,1920]{2,1,0:T(8,128)(2,1)S(1)} %add_convert_fusion), channel_id=1, source_target_pairs={{0,6},{1,7},{2,4},{3,5},{4,2},{5,3},{6,0},{7,1},{8,14},{9,15},{10,... | collective-permute-start | bytes 2211848 | tf_op jit(solution)/shard_map/ppermute | solution.py:35
  221.0 24.6 %collective-permute-start.54 = (bf16[4,48,1280]{2,1,0:T(8,128)(2,1)}, bf16[4,48,1280]{2,1,0:T(8,128)(2,1)S(1)}, u32[]{:S(2)}, u32[]{:S(2)}) collective-permute-start(bf16[4,48,1280]{2,1,0:T(8,128)(2,1)} %get-tuple-element.324), channel_id=1, source_target_pairs={{0,2},{1,3},{2,0},{3,1},{4,6},{5,7},{6,4},{7,5},{8,10},{9,11},{10,... | collective-permute-start | bytes 1474568 | tf_op jit(solution)/shard_map/ppermute | solution.py:35
  221.3 24.3 %collective-permute-start.55 = (bf16[4,48,1280]{2,1,0:T(8,128)(2,1)S(1)}, bf16[4,48,1280]{2,1,0:T(8,128)(2,1)S(1)}, u32[]{:S(2)}, u32[]{:S(2)}) collective-permute-start(bf16[4,48,1280]{2,1,0:T(8,128)(2,1)S(1)} %get-tuple-element.325), channel_id=1, source_target_pairs={{0,4},{1,5},{2,6},{3,7},{4,0},{5,1},{6,2},{7,3},{8,12},{9,13},{10,... | collective-permute-start | bytes 1474568 | tf_op jit(solution)/shard_map/ppermute | solution.py:35
  222.7 22.9 %collective-permute-start.56 = (bf16[4,48,1280]{2,1,0:T(8,128)(2,1)S(1)}, bf16[4,48,1280]{2,1,0:T(8,128)(2,1)S(1)}, u32[]{:S(2)}, u32[]{:S(2)}) collective-permute-start(bf16[4,48,1280]{2,1,0:T(8,128)(2,1)S(1)} %get-tuple-element.326), channel_id=1, source_target_pairs={{0,6},{1,7},{2,4},{3,5},{4,2},{5,3},{6,0},{7,1},{8,14},{9,15},{10,... | collective-permute-start | bytes 1474568 | tf_op jit(solution)/shard_map/ppermute | solution.py:35
  225.4 20.2 %collective-permute-start.52 = (bf16[2,48,1920]{2,1,0:T(8,128)(2,1)}, bf16[2,48,1920]{2,1,0:T(8,128)(2,1)}, u32[]{:S(2)}, u32[]{:S(2)}) collective-permute-start(bf16[2,48,1920]{2,1,0:T(8,128)(2,1)} %get-tuple-element.323), channel_id=1, source_target_pairs={{0,16},{1,17},{2,18},{3,19},{4,20},{5,21},{6,22},{7,23},{8,24},{9,... | collective-permute-start | bytes 1105928 | tf_op jit(solution)/shard_map/ppermute | solution.py:35
  (80 other events, 582.7 us)
